TPU v7x, 128 devices: a whole 4x4x4 slice. The times are simulated.
128 devices in a mesh: grp: 8 (over z_hi, x), sub: 16 (over z_lo, y, core).
Axes of the slice: x: 4, y: 4, z: 4 (z_hi: 2, z_lo: 2; z = z_hi * 2 + z_lo), core: 2. Of those that a mesh axis runs over, the one named last changes fastest.
Arguments:
- residual_field: float32 [16, 32, 128, 384], P('grp', 'sub'), may hold values from -6 to 6
- line_inverse: bfloat16 [32, 64, 5, 384, 384], P('grp', 'sub'), may hold values from -5 to 5
- deflation: bfloat16 [16, 32, 48, 384], P('grp', 'sub'), may hold values from -0.21875 to 0.21875
- counts: int32 [8, 16], P('grp', 'sub'), may hold values from 12 to 48
- coarse_factor: float32 [6144, 6144], P(('grp', 'sub')), may hold values from -2 to 2, as said below
Outputs:
- preconditioned: float32 [16, 32, 128, 384], P('grp', 'sub')
Inputs may be any that keep to these rules, and one draw needn't show every extreme that they name: `coarse_factor`: lower triangular with a positive diagonal.
All inputs are finite; a program needn't handle non-finite values.
Results may differ from a plain program's by a relative error of at most 0.0029.
Values may be sent and summed in bfloat16 or wider, within the bound.
No kernel may reach another device: no remote copies, remote signals or barrier semaphores. Data moves between devices by JAX's collectives and lax.ppermute only.
A program may use at most 128 MiB of HBM per device.

v0:
```python
import jax
import jax.numpy as jnp
from jax import lax
from jax.sharding import PartitionSpec as P

NEIGHBOUR_STEPS = ((-1, 0), (0, -1), (0, 0), (0, 1), (1, 0))


def with_halo(cells, sides, width):
    for axis, dim in sides:
        count = lax.axis_size(axis)
        ends = count - 1
        head = lax.slice_in_dim(cells, 0, width, axis=dim)
        tail = lax.slice_in_dim(cells, cells.shape[dim] - width, cells.shape[dim], axis=dim)
        cells = jnp.concatenate(
            [
                lax.ppermute(tail, axis, [(i, (i + 1) % count) for i in range(ends)]),
                cells,
                lax.ppermute(head, axis, [((i + 1) % count, i) for i in range(ends)]),
            ],
            axis=dim,
        )
    return cells


def fold_edges(source, fold_dim, own_cells):
    middle = lax.slice_in_dim(source, 2, own_cells + 2, axis=fold_dim)
    lower = lax.slice_in_dim(source, 0, 1, axis=fold_dim)
    upper = lax.slice_in_dim(source, own_cells + 3, own_cells + 4, axis=fold_dim)
    widths_low = [(0, 0)] * source.ndim
    widths_low[fold_dim] = (0, own_cells - 1)
    widths_high = [(0, 0)] * source.ndim
    widths_high[fold_dim] = (own_cells - 1, 0)
    return middle + jnp.pad(lower, widths_low) + jnp.pad(upper, widths_high)


def coupled_solve(extended, line_inverse):
    wide_x = extended.shape[0]
    wide_y = extended.shape[1]
    framed = jnp.pad(extended, ((1, 1), (1, 1), (0, 0), (0, 0)))
    local_sol = jnp.zeros(extended.shape, jnp.float32)
    for index, (step_p, step_q) in enumerate(NEIGHBOUR_STEPS):
        shifted = framed[1 + step_p : 1 + step_p + wide_x, 1 + step_q : 1 + step_q + wide_y]
        local_sol = local_sol + jnp.einsum(
            "abru,abuv->abrv",
            shifted,
            line_inverse[:, :, index],
            preferred_element_type=jnp.float32,
        )
    return local_sol


def schwarz_solve(rounded, line_inverse, own_x, own_y):
    extended = with_halo(rounded, (("grp", 0), ("sub", 1)), 1)
    local_sol = coupled_solve(extended, line_inverse)
    returned = with_halo(local_sol, (("grp", 0), ("sub", 1)), 1)
    return fold_edges(fold_edges(returned, 0, own_x), 1, own_y)


def coarse_solve(rounded, deflation, counts, coarse_factor):
    slot_count = deflation.shape[2]
    coarse_part = jnp.einsum(
        "abku,abru->kr", deflation, rounded, preferred_element_type=jnp.float32
    )
    slot_ids = lax.broadcasted_iota(jnp.int32, (slot_count, 1), 0)
    keeper = (slot_ids < counts).astype(jnp.float32)
    coarse_part = coarse_part * keeper
    columns = coarse_factor
    lowered = jnp.dot(
        columns,
        lax.all_gather(coarse_part, ("grp", "sub"), axis=0, tiled=True),
        precision=lax.Precision.HIGHEST,
        preferred_element_type=jnp.float32,
    )
    columns = coarse_factor
    solved = lax.psum_scatter(
        jnp.dot(
            columns.T, lowered, precision=lax.Precision.HIGHEST, preferred_element_type=jnp.float32
        ),
        ("grp", "sub"),
        scatter_dimension=0,
        tiled=True,
    )
    solved = (solved * keeper).astype(jnp.bfloat16)
    return jnp.einsum("abku,kr->abru", deflation, solved, preferred_element_type=jnp.float32)


def body(residual_field, line_inverse, deflation, counts, coarse_factor):
    own_x = residual_field.shape[0]
    own_y = residual_field.shape[1]
    rounded = residual_field.astype(jnp.bfloat16)
    schwarz = schwarz_solve(rounded, line_inverse, own_x, own_y)
    correction = coarse_solve(rounded, deflation, counts, coarse_factor)
    return schwarz + correction


def solution(mesh):
    return jax.shard_map(
        body,
        mesh=mesh,
        in_specs=(
            P("grp", "sub", None, None),
            P("grp", "sub", None, None, None),
            P("grp", "sub", None, None),
            P("grp", "sub"),
            P(("grp", "sub"), None),
        ),
        out_specs=P("grp", "sub", None, None),
        check_vma=False,
    )
```

profile of v0, /device:TPU:0, one launch (start us, length us, event | category | flops | bytes accessed | tf_op | source)
XLA Modules:
  0.0 875.6 jit_solution(10709818256796610138)
XLA Ops:
  7.3 1.2 convert_element_type.24
  8.5 1.8 fusion.22
  10.4 3.5 collective-permute-start
  13.9 1.3 collective-permute-start.1
  15.2 2.8 collective-permute-done
  18.0 4.1 collective-permute-done.1
  22.3 1.3 collective-permute-start.2
  23.7 1.3 collective-permute-start.3
  25.0 4.1 collective-permute-done.3
  29.1 5.3 fusion.4
  34.4 5.2 fusion.6
  39.6 5.1 fusion.2
  44.7 166.6 %all-gather.2.cloned.1.call-done = f32[6144,128]{1,0:T(8,128)} async-done(((f32[48,128]{1,0:T(8,128)}), f32[6144,128]{1,0:T(8,128)}) %all-gather.2.cloned.1.call-update) | async-done | bytes 3145744 | tf_op jit(solution)/shard_map/all_gather | solution.py:71
  211.3 6.9 fusion.36
  218.2 6.9 convolution_bitcast_fusion
  225.2 3.3 fusion.8
  228.5 0.9 copy-done.4
  229.4 0.9 copy-done.5
  230.3 3.7 add_add_fusion
  234.2 2.7 collective-permute-start.4
  236.8 1.3 collective-permute-start.5
  238.1 15.0 %collective-permute-done.4 = f32[1,4,128,384]{3,2,1,0:T(8,128)S(1)} collective-permute-done((f32[1,4,128,384]{3,2,1,0:T(8,128)S(1)}, f32[1,4,128,384]{3,2,1,0:T(8,128)S(1)}, u32[]{:S(2)}, u32[]{:S(2)}) %collective-permute-start.4) | collective-permute-done | bytes 786464 | tf_op jit(solution)/shard_map/ppermute | solution.py:17
  253.1 4.7 collective-permute-done.5
  258.0 1.4 collective-permute-start.6
  259.4 1.3 collective-permute-start.7
  260.7 1.1 collective-permute-done.6
  261.7 3.3 collective-permute-done.7
  265.1 0.8 pad_maximum_fusion
  265.9 0.5 fusion.15
  266.4 0.8 slice.105
  267.1 599.3 %reduce-scatter.2.cloned.1.call-done = f32[48,128]{1,0:T(8,128)} async-done(((f32[6144,128]{1,0:T(8,128)}), f32[48,128]{1,0:T(8,128)}) %reduce-scatter.2.cloned.1.call-update) | async-done | bytes 24592 | tf_op jit(solution)/shard_map/reduce_scatter | solution.py:76
  866.5 2.3 fusion.25
  (21 shorter events, 0.6 us)
Async XLA Ops:
  6.5 204.8 %copy-start = (f32[48,6144]{1,0:T(8,128)S(1)}, f32[48,6144]{1,0:T(8,128)}, u32[]{:S(2)}) copy-start(f32[48,6144]{1,0:T(8,128)} %param.9) | copy-start | bytes 3538948
  6.5 204.8 %all-gather.2.cloned.1.call-start = ((), (), s32[]{:S(2)}) async-start(), calls=%async_computation.1 | async-start | bytes 3170304 | tf_op jit(solution)/shard_map/all_gather | solution.py:71
  10.3 856.2 %reduce-scatter.2.cloned.1.call-start = ((), (), s32[]{:S(2)}) async-start(), calls=%async_computation.2 | async-start | bytes 3170304 | tf_op jit(solution)/shard_map/reduce_scatter | solution.py:76
  10.4 7.6 collective-permute-start
  13.9 8.3 collective-permute-start.1
  22.3 2.6 collective-permute-start.2
  23.7 5.4 collective-permute-start.3
  225.2 3.4 copy-start.3
  225.2 4.3 copy-start.4
  225.2 5.2 copy-start.5
  234.2 19.0 %collective-permute-start.4 = (f32[1,4,128,384]{3,2,1,0:T(8,128)S(1)}, f32[1,4,128,384]{3,2,1,0:T(8,128)S(1)}, u32[]{:S(2)}, u32[]{:S(2)}) collective-permute-start(f32[1,4,128,384]{3,2,1,0:T(8,128)S(1)} %get-tuple-element.7), channel_id=1, source_target_pairs={{0,16},{16,32},{32,48},{48,64},{64,80},{80,96},{96,112},{1,17},{17... | collective-permute-start | bytes 2359304 | tf_op jit(solution)/shard_map/ppermute | solution.py:17
  236.8 21.0 %collective-permute-start.5 = (f32[1,4,128,384]{3,2,1,0:T(8,128)S(1)}, f32[1,4,128,384]{3,2,1,0:T(8,128)S(1)}, u32[]{:S(2)}, u32[]{:S(2)}) collective-permute-start(f32[1,4,128,384]{3,2,1,0:T(8,128)S(1)} %get-tuple-element.8), channel_id=1, source_target_pairs={{16,0},{32,16},{48,32},{64,48},{80,64},{96,80},{112,96},{17,1},{33... | collective-permute-start | bytes 2359304 | tf_op jit(solution)/shard_map/ppermute | solution.py:19
  258.0 3.8 collective-permute-start.6
  259.4 6.5 copy-start.2
  259.4 5.7 collective-permute-start.7
  265.8 603.0 %copy-start.1 = (f32[48,6144]{1,0:T(8,128)S(1)}, f32[48,6144]{1,0:T(8,128)}, u32[]{:S(2)}) copy-start(f32[48,6144]{1,0:T(8,128)} %param.9) | copy-start | bytes 3538948
Sparse Core Ops, SparseCore 0:
  10.4 200.8 all-gather.1
  225.3 641.1 reduce-scatter.1
where the time goes:
time: 876 us
  waiting for transfers between devices  801 us (91%)
  matrix products  40.6 us (5%)
  between operations  14.4 us (2%)
  starting transfers between devices  14.1 us (2%)
    reduce_scatter x1, waiting for transfers between devices, coarse_solve(): lax.psum_scatter(jnp.dot(columns.T, lowered, precision=lax.Precision.HIGH...  599 us
    all_gather x1, waiting for transfers between devices, coarse_solve(): lax.all_gather(coarse_part, ('grp', 'sub'), axis=0, tiled=True)  167 us
    dot_general x5, matrix products, coupled_solve(): jnp.einsum('abru,abuv->abrv', shifted, line_inverse[:, :, index], preferr...  22.7 us
    ppermute x4, waiting for transfers between devices, with_halo(): lax.ppermute(tail, axis, [(i, (i + 1) % count) for i in range(ends)])  18.9 us
  transfers between devices with their start and end apart: 10, of which 9 were waited for; matrix products, arithmetic and copies ran while one was open for 3% of the time, Pallas kernels for 0%

commit v1 on v0

v1 whole, which is shorter than its diff:
```python
import jax
import jax.numpy as jnp
from jax import lax
from jax.experimental import pallas as pl
from jax.experimental.pallas import tpu as pltpu
from jax.sharding import Mesh, PartitionSpec as P

AXES = ("zh", "x", "zl", "y", "c")
GRP = ("zh", "x")
SUB = ("zl", "y", "c")
RING = ("zh", "zl")
GATHER = ("x", "y", "c")

STEPS = ((-1, 0), (0, -1), (0, 0), (0, 1), (1, 0))
WIDE = 4


def shift(value, axes, size, step):
    pairs = [(i, i + step) for i in range(size) if 0 <= i + step < size]
    return lax.ppermute(value, axes, pairs)


def rotate(value, axes, size, step):
    return lax.ppermute(value, axes, [(i, (i + step) % size) for i in range(size)])


def terms(a, b):
    found = []
    for k, (p, q) in enumerate(STEPS):
        if 0 <= a + p < WIDE and 0 <= b + q < WIDE:
            found.append((k, a + p, b + q))
    return found


def line_kernel(cells, own, low_x, high_x, low_y, high_y, blocks, *rest):
    outs, (held, sems) = rest[:-2], rest[-2:]

    def window(a, b):
        if b == 0:
            return low_y[a, 0]
        if b == WIDE - 1:
            return high_y[a, 0]
        if a == 0:
            return low_x[0, b - 1]
        if a == WIDE - 1:
            return high_x[0, b - 1]
        return own[a - 1, b - 1]

    slot = 0
    plan = []
    for a, b, _, _ in cells:
        mine = []
        for k, sa, sb in terms(a, b):
            copy = pltpu.make_async_copy(blocks.at[a, b, k], held.at[slot], sems.at[slot])
            copy.start()
            mine.append((copy, slot, sa, sb))
            slot += 1
        plan.append(mine)
    for (a, b, out, at), mine in zip(cells, plan):
        total = None
        for copy, place, sa, sb in mine:
            copy.wait()
            part = jnp.dot(window(sa, sb), held[place], preferred_element_type=jnp.float32)
            total = part if total is None else total + part
        outs[out][at] = total.astype(outs[out].dtype)


def line_solve(cells, shapes, windows, line_inverse):
    count = sum(len(terms(a, b)) for a, b, _, _ in cells)
    line = line_inverse.shape[-1]
    rhs = windows[0].shape[2]

    def body(*refs):
        line_kernel(cells, *refs)

    return pl.pallas_call(
        body,
        out_shape=[jax.ShapeDtypeStruct(s, d) for s, d in shapes],
        in_specs=[pl.BlockSpec(memory_space=pltpu.VMEM)] * 5 + [pl.BlockSpec(memory_space=pl.ANY)],
        out_specs=[pl.BlockSpec(memory_space=pltpu.VMEM)] * len(shapes),
        scratch_shapes=[
            pltpu.VMEM((count, line, line), line_inverse.dtype),
            pltpu.SemaphoreType.DMA((count,)),
        ],
        compiler_params=pltpu.CompilerParams(vmem_limit_bytes=40 * 1024 * 1024),
        cost_estimate=pl.CostEstimate(
            flops=2 * count * rhs * line * line, bytes_accessed=count * line * line * 2, transcendentals=0
        ),
    )(*windows, line_inverse)


def schwarz_solve(rounded, line_inverse, n_grp, n_sub):
    rhs, line = rounded.shape[2:]
    low_x = shift(rounded[1:2], GRP, n_grp, 1)
    high_x = shift(rounded[0:1], GRP, n_grp, -1)
    low_y = shift(jnp.concatenate([low_x[:, 1:2], rounded[:, 1:2], high_x[:, 1:2]], 0), SUB, n_sub, 1)
    high_y = shift(jnp.concatenate([low_x[:, 0:1], rounded[:, 0:1], high_x[:, 0:1]], 0), SUB, n_sub, -1)
    windows = (rounded, low_x, high_x, low_y, high_y)

    edge = ((WIDE, 1, rhs, line), jnp.bfloat16)
    cells = [(a, b, i, (a, 0)) for a in range(WIDE) for i, b in enumerate((0, WIDE - 1))]
    to_low, to_high = line_solve(cells, [edge, edge], windows, line_inverse)
    back_low = shift(to_high, SUB, n_sub, 1)
    back_high = shift(to_low, SUB, n_sub, -1)

    whole = ((WIDE, 2, rhs, line), jnp.float32)
    cells = [(a, b, 0, (a, b - 1)) for a in (0, WIDE - 1, 1, 2) for b in (1, 2)]
    (middle,) = line_solve(cells, [whole], windows, line_inverse)
    folded = middle + jnp.concatenate([back_low, back_high], 1).astype(jnp.float32)

    from_low = shift(folded[3:4].astype(jnp.bfloat16), GRP, n_grp, 1)
    from_high = shift(folded[0:1].astype(jnp.bfloat16), GRP, n_grp, -1)
    return folded[1:3] + jnp.concatenate([from_low, from_high], 0).astype(jnp.float32)


def coarse_solve(rounded, deflation, counts, coarse_factor, sizes):
    slots = deflation.shape[2]
    rhs = rounded.shape[2]
    ring = sizes["zh"] * sizes["zl"]
    group = sizes["x"] * sizes["y"] * sizes["c"]
    keeper = (lax.broadcasted_iota(jnp.int32, (slots, 1), 0) < counts).astype(jnp.float32)

    parts = coarse_factor.reshape(slots, sizes["zh"], sizes["x"], sizes["zl"], -1)
    here = lax.axis_index(RING)
    rows = []
    for step in range(ring):
        there = lax.rem(here + step, ring)
        block = lax.dynamic_slice(
            parts,
            (0, there // sizes["zl"], 0, lax.rem(there, sizes["zl"]), 0),
            (slots, 1, sizes["x"], 1, parts.shape[-1]),
        ).reshape(slots, -1)
        rows.append(rotate(block, RING, ring, step) if step else block)
    factor = jnp.concatenate(rows, 0)

    coarse_part = jnp.einsum("abku,abru->kr", deflation, rounded, preferred_element_type=jnp.float32) * keeper
    spread = jnp.broadcast_to(coarse_part[None], (group, slots, rhs))
    gathered = lax.all_to_all(spread, GATHER, 0, 0).reshape(group * slots, rhs)

    partial = jnp.dot(factor, gathered, precision=lax.Precision.HIGHEST, preferred_element_type=jnp.float32)
    lowered = partial.reshape(ring, slots, rhs)
    total = lowered
    for step in range(1, ring):
        total = total + jnp.roll(rotate(lowered, RING, ring, step), step, 0)
    terms_back = jnp.dot(
        factor.T, total.reshape(ring * slots, rhs), precision=lax.Precision.HIGHEST, preferred_element_type=jnp.float32
    )
    solved = lax.all_to_all(terms_back.reshape(group, slots, rhs), GATHER, 0, 0).sum(0)
    solved = (solved * keeper).astype(jnp.bfloat16)
    return jnp.einsum("abku,kr->abru", deflation, solved, preferred_element_type=jnp.float32)


def solution(mesh):
    n_grp, n_sub = mesh.shape["grp"], mesh.shape["sub"]
    sizes = {"zh": 2, "x": n_grp // 2, "zl": 2, "y": n_sub // 4, "c": 2}
    fine = Mesh(mesh.devices.reshape([sizes[a] for a in AXES]), AXES)

    def body(residual_field, line_inverse, deflation, counts, coarse_factor):
        rounded = residual_field.astype(jnp.bfloat16)
        schwarz = schwarz_solve(rounded, line_inverse, n_grp, n_sub)
        return schwarz + coarse_solve(rounded, deflation, counts, coarse_factor, sizes)

    return jax.shard_map(
        body,
        mesh=fine,
        in_specs=(
            P(GRP, SUB, None, None),
            P(GRP, SUB, None, None, None),
            P(GRP, SUB, None, None),
            P(GRP, SUB),
            P(AXES, None),
        ),
        out_specs=P(GRP, SUB, None, None),
        check_vma=False,
    )
```

time: 876 us -> 108 us (0.12)
  the two profiles are of different devices: /device:TPU:0 before, /device:TPU:38 now
where the time goes in v1:
time: 108 us; the launch traced here: 107 us
  starting transfers between devices  50.6 us (47%)
  waiting for transfers between devices  16 us (15%)
  Pallas kernels  14.1 us (13%)
  local copies, waits for them, and re-layouts  13.2 us (12%)
  matrix products  6.33 us (6%)
  other arithmetic  6.03 us (6%)
    ppermute x8, starting transfers between devices, shift(): return lax.ppermute(value, axes, pairs)  26.2 us
    ppermute x8, waiting for transfers between devices, shift(): return lax.ppermute(value, axes, pairs)  16 us
    pallas_call x2, Pallas kernels, line_solve(): pl.pallas_call(body, out_shape=[jax.ShapeDtypeStruct(s, d) for s, d in sh...  14.1 us
    all_to_all x1, starting transfers between devices, coarse_solve(): lax.all_to_all(terms_back.reshape(group, slots, rhs), GATHER, 0, 0).sum(0)  8.79 us
    ppermute x6, starting transfers between devices, rotate(): lax.ppermute(value, axes, [(i, (i + step) % size) for i in range(size)])  8.01 us
    all_to_all x1, starting transfers between devices, coarse_solve(): gathered = lax.all_to_all(spread, GATHER, 0, 0).reshape(group * slots, rhs)  7.65 us
    ppermute x3, local copies, waits for them, and re-layouts, rotate(): lax.ppermute(value, axes, [(i, (i + step) % size) for i in range(size)])  3.49 us
    concatenate x1, other arithmetic, coarse_solve(): factor = jnp.concatenate(rows, 0)  2.92 us
  transfers between devices with their start and end apart: 16, of which 4 were waited for; matrix products, arithmetic and copies ran while one was open for 18% of the time, Pallas kernels for 13%

profile of v1, /device:TPU:38, one launch (start us, length us, event | category | flops | bytes accessed | tf_op | source)
XLA Modules:
  0.0 107.3 jit_solution(171882164135336079)
XLA Ops:
  0.0 2.3 %reshape.35 = f32[48,2,4,2,384]{4,3,2,1,0:T(2,128)S(1)} reshape(f32[48,6144]{1,0:T(8,128)} %param.9) | data formatting | bytes 2359296 | tf_op jit(solution)/shard_map/reshape | solution.py:123
  2.4 2.9 %dynamic-slice_reduce_fusion.2 = (f32[48,4,384]{2,1,0:T(4,128)S(1)}, f32[48,4,384]{2,1,0:T(4,128)S(1)}, f32[48,4,384]{2,1,0:T(4,128)S(1)}, f32[48,1,4,1,384]{4,3,2,1,0:T(1,128)S(1)}) fusion(f32[48,2,4,2,384]{4,3,2,1,0:T(2,128)S(1)} %reshape.35, s32[]{:T(128)S(6)} %select_n.42, s32[]{:T(128)S(6)} %select_n.43, s32[]{:T(128)S(6)} %select_n.48, ...), kind=kLoop, calls=%fused_computation.11 | loop fusion | bytes 2359328 | tf_op jit(solution)/shard_map/dynamic_slice | solution.py:128
  5.3 2.0 %collective-permute-start.8 = (f32[48,1536]{1,0:T(8,128)S(1)}, f32[48,1536]{1,0:T(8,128)S(1)}, u32[]{:S(2)}, u32[]{:S(2)}) collective-permute-start(f32[48,1536]{1,0:T(8,128)S(1)} %bitcast.50), channel_id=1, source_target_pairs={{0,8},{8,64},{64,72},{72,0},{1,9},{9,65},{65,73},{73,1},{2,10},{10... | collective-permute-start | bytes 884744 | tf_op jit(solution)/shard_map/ppermute | solution.py:24
  7.3 1.2 %collective-permute-start.9 = (f32[48,1536]{1,0:T(8,128)S(1)}, f32[48,1536]{1,0:T(8,128)S(1)}, u32[]{:S(2)}, u32[]{:S(2)}) collective-permute-start(f32[48,1536]{1,0:T(8,128)S(1)} %bitcast.51), channel_id=1, source_target_pairs={{0,64},{8,72},{64,0},{72,8},{1,65},{9,73},{65,1},{73,9},{2,66},{10... | collective-permute-start | bytes 884744 | tf_op jit(solution)/shard_map/ppermute | solution.py:24
  8.5 2.7 %collective-permute-start.10 = (f32[48,1536]{1,0:T(8,128)S(1)}, f32[48,1536]{1,0:T(8,128)S(1)}, u32[]{:S(2)}, u32[]{:S(2)}) collective-permute-start(f32[48,1536]{1,0:T(8,128)S(1)} %bitcast.52), channel_id=1, source_target_pairs={{0,72},{8,0},{64,8},{72,64},{1,73},{9,1},{65,9},{73,65},{2,74},{10... | collective-permute-start | bytes 884744 | tf_op jit(solution)/shard_map/ppermute | solution.py:24
  13.0 7.7 %all-to-all-start = ((f32[32,48,128]{2,1,0:T(8,128)}), f32[32,48,128]{2,1,0:T(8,128)}, u32[]{:S(2)}, u32[]{:S(2)}) async-start(f32[32,48,128]{2,1,0:T(8,128)} %broadcast_in_dim.2), calls=%async_computation | async-start | bytes 1572864 | tf_op jit(solution)/shard_map/all_to_all | solution.py:138
  20.7 1.9 %collective-permute-start = (bf16[1,2,128,384]{3,2,1,0:T(8,128)(2,1)S(1)}, bf16[1,2,128,384]{3,2,1,0:T(8,128)(2,1)S(1)}, u32[]{:S(2)}, u32[]{:S(2)}) collective-permute-start(bf16[1,2,128,384]{3,2,1,0:T(8,128)(2,1)S(1)} %get-tuple-element.20), channel_id=1, source_target_pairs={{0,16},{16,32},{32,48},{48,64},{64,80},{80,96},{96,112},{1,17},{17... | collective-permute-start | bytes 589832 | tf_op jit(solution)/shard_map/ppermute | solution.py:20
  22.7 3.9 %collective-permute-start.1 = (bf16[1,2,128,384]{3,2,1,0:T(8,128)(2,1)S(1)}, bf16[1,2,128,384]{3,2,1,0:T(8,128)(2,1)S(1)}, u32[]{:S(2)}, u32[]{:S(2)}) collective-permute-start(bf16[1,2,128,384]{3,2,1,0:T(8,128)(2,1)S(1)} %get-tuple-element.19), channel_id=1, source_target_pairs={{16,0},{32,16},{48,32},{64,48},{80,64},{96,80},{112,96},{17,1},{33... | collective-permute-start | bytes 589832 | tf_op jit(solution)/shard_map/ppermute | solution.py:20
  26.6 1.2 %copy.21 = f32[48,1,4,1,384]{0,4,2,3,1:T(8,128)} copy(f32[48,1,4,1,384]{4,3,2,1,0:T(1,128)S(1)} %get-tuple-element.14) | data formatting | bytes 589824
  27.8 7.4 %collective-permute-done.refs_1_ = bf16[1,2,128,384]{3,2,1,0:T(8,128)(2,1)S(1)} collective-permute-done((bf16[1,2,128,384]{3,2,1,0:T(8,128)(2,1)S(1)}, bf16[1,2,128,384]{3,2,1,0:T(8,128)(2,1)S(1)}, u32[]{:S(2)}, u32[]{:S(2)}) %collective-permute-start) | collective-permute-done | bytes 196640 | tf_op jit(solution)/shard_map/ppermute | solution.py:20
  36.2 4.2 %collective-permute-start.3 = (bf16[4,1,128,384]{3,2,1,0:T(8,128)(2,1)}, bf16[4,1,128,384]{3,2,1,0:T(8,128)(2,1)S(1)}, u32[]{:S(2)}, u32[]{:S(2)}) collective-permute-start(bf16[4,1,128,384]{3,2,1,0:T(8,128)(2,1)} %pad_maximum_fusion.2), channel_id=1, source_target_pairs={{1,0},{2,1},{3,2},{4,3},{5,4},{6,5},{7,6},{8,7},{9,8},{10,9},{11,1... | collective-permute-start | bytes 1179656 | tf_op jit(solution)/shard_map/ppermute | solution.py:20
  41.2 1.9 %collective-permute-start.2 = (bf16[4,1,128,384]{3,2,1,0:T(8,128)(2,1)}, bf16[4,1,128,384]{3,2,1,0:T(8,128)(2,1)S(1)}, u32[]{:S(2)}, u32[]{:S(2)}) collective-permute-start(bf16[4,1,128,384]{3,2,1,0:T(8,128)(2,1)} %pad_maximum_fusion.1), channel_id=1, source_target_pairs={{0,1},{1,2},{2,3},{3,4},{4,5},{5,6},{6,7},{7,8},{8,9},{9,10},{10,1... | collective-permute-start | bytes 1179656 | tf_op jit(solution)/shard_map/ppermute | solution.py:20
  43.1 1.2 %copy.15 = f32[48,1536]{0,1:T(8,128)} copy(f32[48,1536]{1,0:T(8,128)S(1)} %collective-permute-done.8) | data formatting | bytes 589824 | tf_op jit(solution)/shard_map/ppermute | solution.py:24
  44.2 1.2 %copy.16 = f32[48,1536]{0,1:T(8,128)} copy(f32[48,1536]{1,0:T(8,128)S(1)} %collective-permute-done.9) | data formatting | bytes 589824 | tf_op jit(solution)/shard_map/ppermute | solution.py:24
  45.4 1.2 %copy.17 = f32[48,1536]{0,1:T(8,128)} copy(f32[48,1536]{1,0:T(8,128)S(1)} %collective-permute-done.10) | data formatting | bytes 589824 | tf_op jit(solution)/shard_map/ppermute | solution.py:24
  46.6 2.9 %pad_maximum_fusion = f32[192,1536]{0,1:T(8,128)S(1)} fusion(f32[48,1536]{0,1:T(8,128)} %copy.17, f32[48,1536]{0,1:T(8,128)} %copy.16, f32[48,1536]{0,1:T(8,128)} %copy.15, f32[48,1536]{0,1:T(8,128)} %bitcast.45), kind=kLoop, calls=%fused_computation | loop fusion | flops 884736 | bytes 2359296 | tf_op jit(solution)/shard_map/concatenate | solution.py:134
  49.5 1.5 %copy.18 = f32[192,1536]{1,0:T(8,128)} copy(f32[192,1536]{0,1:T(8,128)S(1)} %pad_maximum_fusion) | data formatting | bytes 2359296 | tf_op jit(solution)/shard_map/concatenate | solution.py:134
  51.1 2.6 %fusion.16 = f32[4,48,128]{2,1,0:T(8,128)S(1)} fusion(f32[4,48,1536]{2,1,0:T(8,128)} %bitcast.44, f32[1536,128,1]{1,0,2:T(8,128)} %bitcast.8), kind=kOutput, calls=%fused_computation.27 | convolution fusion | flops 452984832 | bytes 2064384 | tf_op jit(solution)/shard_map/dot_general | solution.py:140
  53.8 1.1 collective-permute-start.11
  54.8 1.0 collective-permute-start.13
  55.9 6.4 %shard_map.56 = (bf16[4,1,128,384]{3,2,1,0:T(8,128)(2,1)S(1)}, bf16[4,1,128,384]{3,2,1,0:T(8,128)(2,1)S(1)}) custom-call(bf16[2,2,128,384]{3,2,1,0:T(8,128)(2,1)S(1)} %convert_element_type.22.refs_0_, bf16[1,2,128,384]{3,2,1,0:T(8,128)(2,1)S(1)} %collective-permute-done.refs_1_, bf16[1,2,128,384]{3,2,1,0:T(8,128)(2,1)S(1)} %collective-permute-done.1.refs_2_, ...), custom_call_target="tpu_custom_call" | custom-call | flops 1056964608 | bytes 8257536 | tf_op jit(solution)/shard_map/pallas_call | solution.py:76
  62.2 1.9 %collective-permute-start.4 = (bf16[4,1,128,384]{3,2,1,0:T(8,128)(2,1)S(1)}, bf16[4,1,128,384]{3,2,1,0:T(8,128)(2,1)}, u32[]{:S(2)}, u32[]{:S(2)}) collective-permute-start(bf16[4,1,128,384]{3,2,1,0:T(8,128)(2,1)S(1)} %get-tuple-element.7), channel_id=1, source_target_pairs={{0,1},{1,2},{2,3},{3,4},{4,5},{5,6},{6,7},{7,8},{8,9},{9,10},{10,1... | collective-permute-start | bytes 1179656 | tf_op jit(solution)/shard_map/ppermute | solution.py:20
  64.2 6.5 %collective-permute-start.5 = (bf16[4,1,128,384]{3,2,1,0:T(8,128)(2,1)S(1)}, bf16[4,1,128,384]{3,2,1,0:T(8,128)(2,1)}, u32[]{:S(2)}, u32[]{:S(2)}) collective-permute-start(bf16[4,1,128,384]{3,2,1,0:T(8,128)(2,1)S(1)} %get-tuple-element.8), channel_id=1, source_target_pairs={{1,0},{2,1},{3,2},{4,3},{5,4},{6,5},{7,6},{8,7},{9,8},{10,9},{11,1... | collective-permute-start | bytes 1179656 | tf_op jit(solution)/shard_map/ppermute | solution.py:20
  70.8 2.3 %fusion.17 = f32[32,48,128]{2,1,0:T(8,128)} fusion(f32[32,48,192]{2,1,0:T(8,128)S(1)} %bitcast.43, f32[192,128,1]{1,0,2:T(8,128)S(1)} %bitcast.49), kind=kOutput, calls=%fused_computation.28 | convolution fusion | flops 452984832 | bytes 2064384 | tf_op jit(solution)/shard_map/dot_general | solution.py:145
  73.1 8.8 %all-to-all-start.1 = ((f32[32,48,128]{2,1,0:T(8,128)}), f32[32,48,128]{2,1,0:T(8,128)S(1)}, u32[]{:S(2)}, u32[]{:S(2)}) async-start(f32[32,48,128]{2,1,0:T(8,128)} %fusion.17), calls=%async_computation.1 | async-start | bytes 1572864 | tf_op jit(solution)/shard_map/all_to_all | solution.py:148
  81.9 7.7 %shard_map.55 = f32[4,2,128,384]{3,2,1,0:T(8,128)S(1)} custom-call(bf16[2,2,128,384]{3,2,1,0:T(8,128)(2,1)S(1)} %convert_element_type.22.refs_0_, bf16[1,2,128,384]{3,2,1,0:T(8,128)(2,1)S(1)} %collective-permute-done.refs_1_, bf16[1,2,128,384]{3,2,1,0:T(8,128)(2,1)S(1)} %collective-permute-done.1.refs_2_, ...), custom_call_target="tpu_custom_call" | custom-call | flops 1358954496 | bytes 10616832 | tf_op jit(solution)/shard_map/pallas_call | solution.py:76
  89.6 1.4 %fusion.9 = (bf16[4,2,128,384]{3,2,1,0:T(8,128)(2,1)S(1)}, f32[4,2,128,384]{3,2,1,0:T(8,128)S(1)}) fusion(f32[4,2,128,384]{3,2,1,0:T(8,128)S(1)} %shard_map.55, bf16[4,1,128,384]{3,2,1,0:T(8,128)(2,1)} %collective-permute-done.5, bf16[4,1,128,384]{3,2,1,0:T(8,128)(2,1)} %collective-permute-done.4), kind=kLoop, calls=%fused_computation.20 | loop fusion | flops 1572864 | bytes 4718592 | tf_op jit(solution)/shard_map/convert.1
  91.7 1.9 %collective-permute-start.6 = (bf16[1,2,128,384]{3,2,1,0:T(8,128)(2,1)}, bf16[1,2,128,384]{3,2,1,0:T(8,128)(2,1)S(1)}, u32[]{:S(2)}, u32[]{:S(2)}) collective-permute-start(bf16[1,2,128,384]{3,2,1,0:T(8,128)(2,1)} %get-tuple-element.15), channel_id=1, source_target_pairs={{0,16},{16,32},{32,48},{48,64},{64,80},{80,96},{96,112},{1,17},{17... | collective-permute-start | bytes 589832 | tf_op jit(solution)/shard_map/ppermute | solution.py:20
  93.6 3.9 %collective-permute-start.7 = (bf16[1,2,128,384]{3,2,1,0:T(8,128)(2,1)S(1)}, bf16[1,2,128,384]{3,2,1,0:T(8,128)(2,1)S(1)}, u32[]{:S(2)}, u32[]{:S(2)}) collective-permute-start(bf16[1,2,128,384]{3,2,1,0:T(8,128)(2,1)S(1)} %get-tuple-element.16), channel_id=1, source_target_pairs={{16,0},{32,16},{48,32},{64,48},{80,64},{96,80},{112,96},{17,1},{33... | collective-permute-start | bytes 589832 | tf_op jit(solution)/shard_map/ppermute | solution.py:20
  97.6 3.1 %collective-permute-done.6 = bf16[1,2,128,384]{3,2,1,0:T(8,128)(2,1)S(1)} collective-permute-done((bf16[1,2,128,384]{3,2,1,0:T(8,128)(2,1)}, bf16[1,2,128,384]{3,2,1,0:T(8,128)(2,1)S(1)}, u32[]{:S(2)}, u32[]{:S(2)}) %collective-permute-start.6) | collective-permute-done | bytes 196640 | tf_op jit(solution)/shard_map/ppermute | solution.py:20
  100.8 5.3 %collective-permute-done.7 = bf16[1,2,128,384]{3,2,1,0:T(8,128)(2,1)S(1)} collective-permute-done((bf16[1,2,128,384]{3,2,1,0:T(8,128)(2,1)S(1)}, bf16[1,2,128,384]{3,2,1,0:T(8,128)(2,1)S(1)}, u32[]{:S(2)}, u32[]{:S(2)}) %collective-permute-start.7) | collective-permute-done | bytes 196640 | tf_op jit(solution)/shard_map/ppermute | solution.py:20
  106.1 1.2 %fusion.1 = f32[2,2,128,384]{3,2,1,0:T(8,128)} fusion(f32[4,2,128,384]{3,2,1,0:T(8,128)S(1)} %get-tuple-element.13, bf16[1,2,128,384]{3,2,1,0:T(8,128)(2,1)S(1)} %collective-permute-done.7, bf16[1,2,128,384]{3,2,1,0:T(8,128)(2,1)S(1)} %collective-permute-done.6, bf16[2,2,48,384]{3,2,1,0:T(8,128)(2,1)S(1)} %copy-done, f32[48,128]{1,0:T(8,128)S(1)} %reduce_sum.9, ...), kind=kOutput, calls=%fused_computation.6 | convolution fusion | flops 19673088 | bytes 2138304 | tf_op jit(solution)/shard_map/abku,kr->abru/dot_general | solution.py:150
  (43 shorter events, 4.1 us)
Async XLA Ops:
  0.0 11.8 %copy-start = (bf16[2,2,48,384]{3,2,1,0:T(8,128)(2,1)S(1)}, bf16[2,2,48,384]{3,2,1,0:T(8,128)(2,1)}, u32[]{:S(2)}) copy-start(bf16[2,2,48,384]{3,2,1,0:T(8,128)(2,1)} %param.7) | copy-start | bytes 442372
  2.4 8.8 %copy-start.3 = (f32[2,2,128,384]{3,2,1,0:T(8,128)S(1)}, f32[2,2,128,384]{3,2,1,0:T(8,128)}, u32[]{:S(2)}) copy-start(f32[2,2,128,384]{3,2,1,0:T(8,128)} %param.5) | copy-start | bytes 2359300
  5.3 37.8 %collective-permute-start.8 = (f32[48,1536]{1,0:T(8,128)S(1)}, f32[48,1536]{1,0:T(8,128)S(1)}, u32[]{:S(2)}, u32[]{:S(2)}) collective-permute-start(f32[48,1536]{1,0:T(8,128)S(1)} %bitcast.50), channel_id=1, source_target_pairs={{0,8},{8,64},{64,72},{72,0},{1,9},{9,65},{65,73},{73,1},{2,10},{10... | collective-permute-start | bytes 884744 | tf_op jit(solution)/shard_map/ppermute | solution.py:24
  7.3 37.0 %collective-permute-start.9 = (f32[48,1536]{1,0:T(8,128)S(1)}, f32[48,1536]{1,0:T(8,128)S(1)}, u32[]{:S(2)}, u32[]{:S(2)}) collective-permute-start(f32[48,1536]{1,0:T(8,128)S(1)} %bitcast.51), channel_id=1, source_target_pairs={{0,64},{8,72},{64,0},{72,8},{1,65},{9,73},{65,1},{73,9},{2,66},{10... | collective-permute-start | bytes 884744 | tf_op jit(solution)/shard_map/ppermute | solution.py:24
  8.5 37.0 %collective-permute-start.10 = (f32[48,1536]{1,0:T(8,128)S(1)}, f32[48,1536]{1,0:T(8,128)S(1)}, u32[]{:S(2)}, u32[]{:S(2)}) collective-permute-start(f32[48,1536]{1,0:T(8,128)S(1)} %bitcast.52), channel_id=1, source_target_pairs={{0,72},{8,0},{64,8},{72,64},{1,73},{9,1},{65,9},{73,65},{2,74},{10... | collective-permute-start | bytes 884744 | tf_op jit(solution)/shard_map/ppermute | solution.py:24
  13.0 38.0 %all-to-all-start = ((f32[32,48,128]{2,1,0:T(8,128)}), f32[32,48,128]{2,1,0:T(8,128)}, u32[]{:S(2)}, u32[]{:S(2)}) async-start(f32[32,48,128]{2,1,0:T(8,128)} %broadcast_in_dim.2), calls=%async_computation | async-start | bytes 1572864 | tf_op jit(solution)/shard_map/all_to_all | solution.py:138
  20.7 14.5 %collective-permute-start = (bf16[1,2,128,384]{3,2,1,0:T(8,128)(2,1)S(1)}, bf16[1,2,128,384]{3,2,1,0:T(8,128)(2,1)S(1)}, u32[]{:S(2)}, u32[]{:S(2)}) collective-permute-start(bf16[1,2,128,384]{3,2,1,0:T(8,128)(2,1)S(1)} %get-tuple-element.20), channel_id=1, source_target_pairs={{0,16},{16,32},{32,48},{48,64},{64,80},{80,96},{96,112},{1,17},{17... | collective-permute-start | bytes 589832 | tf_op jit(solution)/shard_map/ppermute | solution.py:20
  22.7 12.7 %collective-permute-start.1 = (bf16[1,2,128,384]{3,2,1,0:T(8,128)(2,1)S(1)}, bf16[1,2,128,384]{3,2,1,0:T(8,128)(2,1)S(1)}, u32[]{:S(2)}, u32[]{:S(2)}) collective-permute-start(bf16[1,2,128,384]{3,2,1,0:T(8,128)(2,1)S(1)} %get-tuple-element.19), channel_id=1, source_target_pairs={{16,0},{32,16},{48,32},{64,48},{80,64},{96,80},{112,96},{17,1},{33... | collective-permute-start | bytes 589832 | tf_op jit(solution)/shard_map/ppermute | solution.py:20
  36.2 19.7 %collective-permute-start.3 = (bf16[4,1,128,384]{3,2,1,0:T(8,128)(2,1)}, bf16[4,1,128,384]{3,2,1,0:T(8,128)(2,1)S(1)}, u32[]{:S(2)}, u32[]{:S(2)}) collective-permute-start(bf16[4,1,128,384]{3,2,1,0:T(8,128)(2,1)} %pad_maximum_fusion.2), channel_id=1, source_target_pairs={{1,0},{2,1},{3,2},{4,3},{5,4},{6,5},{7,6},{8,7},{9,8},{10,9},{11,1... | collective-permute-start | bytes 1179656 | tf_op jit(solution)/shard_map/ppermute | solution.py:20
  41.2 14.7 %collective-permute-start.2 = (bf16[4,1,128,384]{3,2,1,0:T(8,128)(2,1)}, bf16[4,1,128,384]{3,2,1,0:T(8,128)(2,1)S(1)}, u32[]{:S(2)}, u32[]{:S(2)}) collective-permute-start(bf16[4,1,128,384]{3,2,1,0:T(8,128)(2,1)} %pad_maximum_fusion.1), channel_id=1, source_target_pairs={{0,1},{1,2},{2,3},{3,4},{4,5},{5,6},{6,7},{7,8},{8,9},{9,10},{10,1... | collective-permute-start | bytes 1179656 | tf_op jit(solution)/shard_map/ppermute | solution.py:20
  49.5 4.2 %copy-start.1 = (f32[192,1536]{0,1:T(8,128)}, f32[192,1536]{0,1:T(8,128)S(1)}, u32[]{:S(2)}) copy-start(f32[192,1536]{0,1:T(8,128)S(1)} %pad_maximum_fusion) | copy-start | bytes 3538948
  53.7 17.1 %collective-permute-start.12 = (f32[4,48,128]{2,1,0:T(8,128)S(1)}, f32[4,48,128]{2,1,0:T(8,128)S(1)}, u32[]{:S(2)}, u32[]{:S(2)}) collective-permute-start(f32[4,48,128]{2,1,0:T(8,128)S(1)} %fusion.16), channel_id=1, source_target_pairs={{0,64},{8,72},{64,0},{72,8},{1,65},{9,73},{65,1},{73,9},{2,66},{10... | collective-permute-start | bytes 294920 | tf_op jit(solution)/shard_map/ppermute | solution.py:24
  53.8 16.9 %collective-permute-start.11 = (f32[4,48,128]{2,1,0:T(8,128)S(1)}, f32[4,48,128]{2,1,0:T(8,128)S(1)}, u32[]{:S(2)}, u32[]{:S(2)}) collective-permute-start(f32[4,48,128]{2,1,0:T(8,128)S(1)} %fusion.16), channel_id=1, source_target_pairs={{0,8},{8,64},{64,72},{72,0},{1,9},{9,65},{65,73},{73,1},{2,10},{10... | collective-permute-start | bytes 294920 | tf_op jit(solution)/shard_map/ppermute | solution.py:24
  54.8 15.9 %collective-permute-start.13 = (f32[4,48,128]{2,1,0:T(8,128)S(1)}, f32[4,48,128]{2,1,0:T(8,128)S(1)}, u32[]{:S(2)}, u32[]{:S(2)}) collective-permute-start(f32[4,48,128]{2,1,0:T(8,128)S(1)} %fusion.16), channel_id=1, source_target_pairs={{0,72},{8,0},{64,8},{72,64},{1,73},{9,1},{65,9},{73,65},{2,74},{10... | collective-permute-start | bytes 294920 | tf_op jit(solution)/shard_map/ppermute | solution.py:24
  55.9 15.0 %copy-start.2 = (f32[192,1536]{0,1:T(8,128)S(1)}, f32[192,1536]{0,1:T(8,128)}, u32[]{:S(2)}) copy-start(f32[192,1536]{0,1:T(8,128)} %copy-done.1) | copy-start | bytes 3538948
  62.2 27.4 %collective-permute-start.4 = (bf16[4,1,128,384]{3,2,1,0:T(8,128)(2,1)S(1)}, bf16[4,1,128,384]{3,2,1,0:T(8,128)(2,1)}, u32[]{:S(2)}, u32[]{:S(2)}) collective-permute-start(bf16[4,1,128,384]{3,2,1,0:T(8,128)(2,1)S(1)} %get-tuple-element.7), channel_id=1, source_target_pairs={{0,1},{1,2},{2,3},{3,4},{4,5},{5,6},{6,7},{7,8},{8,9},{9,10},{10,1... | collective-permute-start | bytes 1179656 | tf_op jit(solution)/shard_map/ppermute | solution.py:20
  64.2 25.5 %collective-permute-start.5 = (bf16[4,1,128,384]{3,2,1,0:T(8,128)(2,1)S(1)}, bf16[4,1,128,384]{3,2,1,0:T(8,128)(2,1)}, u32[]{:S(2)}, u32[]{:S(2)}) collective-permute-start(bf16[4,1,128,384]{3,2,1,0:T(8,128)(2,1)S(1)} %get-tuple-element.8), channel_id=1, source_target_pairs={{1,0},{2,1},{3,2},{4,3},{5,4},{6,5},{7,6},{8,7},{9,8},{10,9},{11,1... | collective-permute-start | bytes 1179656 | tf_op jit(solution)/shard_map/ppermute | solution.py:20
  73.1 24.5 %all-to-all-start.1 = ((f32[32,48,128]{2,1,0:T(8,128)}), f32[32,48,128]{2,1,0:T(8,128)S(1)}, u32[]{:S(2)}, u32[]{:S(2)}) async-start(f32[32,48,128]{2,1,0:T(8,128)} %fusion.17), calls=%async_computation.1 | async-start | bytes 1572864 | tf_op jit(solution)/shard_map/all_to_all | solution.py:148
  91.7 9.1 %collective-permute-start.6 = (bf16[1,2,128,384]{3,2,1,0:T(8,128)(2,1)}, bf16[1,2,128,384]{3,2,1,0:T(8,128)(2,1)S(1)}, u32[]{:S(2)}, u32[]{:S(2)}) collective-permute-start(bf16[1,2,128,384]{3,2,1,0:T(8,128)(2,1)} %get-tuple-element.15), channel_id=1, source_target_pairs={{0,16},{16,32},{32,48},{48,64},{64,80},{80,96},{96,112},{1,17},{17... | collective-permute-start | bytes 589832 | tf_op jit(solution)/shard_map/ppermute | solution.py:20
  93.6 12.5 %collective-permute-start.7 = (bf16[1,2,128,384]{3,2,1,0:T(8,128)(2,1)S(1)}, bf16[1,2,128,384]{3,2,1,0:T(8,128)(2,1)S(1)}, u32[]{:S(2)}, u32[]{:S(2)}) collective-permute-start(bf16[1,2,128,384]{3,2,1,0:T(8,128)(2,1)S(1)} %get-tuple-element.16), channel_id=1, source_target_pairs={{16,0},{32,16},{48,32},{64,48},{80,64},{96,80},{112,96},{17,1},{33... | collective-permute-start | bytes 589832 | tf_op jit(solution)/shard_map/ppermute | solution.py:20

commit v2 on v1

v2 whole, which is shorter than its diff:
```python
import jax
import jax.numpy as jnp
from jax import lax
from jax.experimental import pallas as pl
from jax.experimental.pallas import tpu as pltpu
from jax.sharding import Mesh, PartitionSpec as P

AXES = ("zh", "x", "zl", "y", "c")
GRP = ("zh", "x")
SUB = ("zl", "y", "c")
SPREAD = ("zh", "x", "y")

STEPS = ((-1, 0), (0, -1), (0, 0), (0, 1), (1, 0))
WIDE = 4
VMEM = pl.BlockSpec(memory_space=pltpu.VMEM)
SMEM = pl.BlockSpec(memory_space=pltpu.SMEM)
ANY = pl.BlockSpec(memory_space=pl.ANY)
HBM = pl.BlockSpec(memory_space=pltpu.HBM)
MIB = 1024 * 1024
F32 = jnp.float32
BF16 = jnp.bfloat16


def limit(mib):
    return pltpu.CompilerParams(vmem_limit_bytes=mib * MIB)


def struct(shape, dtype):
    return jax.ShapeDtypeStruct(shape, dtype)


def estimate(flops, size):
    return pl.CostEstimate(flops=flops, bytes_accessed=size, transcendentals=0)


def swap(value, axis):
    return lax.ppermute(value, axis, [(0, 1), (1, 0)])


def swap_across(value):
    return lax.ppermute(value, ("zl", "c"), [(i, 3 - i) for i in range(4)])


def swap_pairs(value, axes, size, begin):
    pairs = []
    for i in range(begin, size - 1, 2):
        pairs += [(i, i + 1), (i + 1, i)]
    return lax.ppermute(value, axes, pairs)


def swap_outward(value, size):
    pairs = []
    for i in range(1, size, 2):
        pairs += [(i, (i + 1) % size), ((i + 1) % size, i)]
    return lax.ppermute(value, SUB, pairs)


def present(flag, value):
    return jnp.where(flag, value, jnp.zeros_like(value))


def terms(a, b):
    found = []
    for k, (p, q) in enumerate(STEPS):
        if 0 <= a + p < WIDE and 0 <= b + q < WIDE:
            found.append((k, a + p, b + q))
    return found


def position():
    spot = {axis: lax.axis_index(axis) for axis in AXES}
    size = {axis: lax.axis_size(axis) for axis in AXES}
    core, x = spot["c"], spot["x"]
    before = jnp.logical_or(spot["zh"] > 0, x > 0)
    after = jnp.logical_or(spot["zh"] < size["zh"] - 1, x < size["x"] - 1)
    outward = spot["zl"] * size["y"] + spot["y"]
    past = jnp.where(core == 0, outward > 0, outward < size["zl"] * size["y"] - 1)
    return core, before, after, past, lax.rem(x, 2)


def line_kernel(cells, put, own, ends, pair, outer, blocks, *rest):
    at = position()
    more, (sides, held, sems) = rest[:-3], rest[-3:]
    slot, plan = 0, []
    for a, b in cells:
        found = terms(a, b)
        start, run, copies = slot, 0, []
        for i, (k, _, _) in enumerate(found):
            run += 1
            if i + 1 == len(found) or found[i + 1][0] != k + 1:
                source = blocks.at[a, b, pl.ds(k + 1 - run, run)]
                copies.append(pltpu.make_async_copy(source, held.at[pl.ds(slot, run)], sems.at[slot]))
                copies[-1].start()
                slot, run = slot + run, 0
        plan.append((start, copies, found))

    first = at[0] == 0
    for a in range(WIDE):
        near, far = pair[a, 0], present(at[3], outer[a, 0])
        sides[0, a] = jnp.where(first, far, near)
        sides[1, a] = jnp.where(first, near, far)

    def window(a, b):
        if b == 0:
            return sides[0, a]
        if b == WIDE - 1:
            return sides[1, a]
        if a in (0, WIDE - 1):
            return ends[0 if a == 0 else 1, b - 1]
        return own[a - 1, b - 1]

    line = held.shape[-1]
    for (a, b), (start, copies, found) in zip(cells, plan):
        for copy in copies:
            copy.wait()
        sources = jnp.concatenate([window(sa, sb) for _, sa, sb in found], axis=1)
        weights = held[start : start + len(found)].reshape(len(found) * line, line)
        put(a, b, jnp.dot(sources, weights, preferred_element_type=F32), at, more)


def line_solve(cells, put, shapes, windows, line_inverse, extra=()):
    count = sum(len(terms(a, b)) for a, b in cells)
    line = line_inverse.shape[-1]
    rhs = windows[0].shape[2]

    def body(*refs):
        line_kernel(cells, put, *refs)

    return pl.pallas_call(
        body,
        out_shape=shapes,
        in_specs=[VMEM] * 4 + [HBM] + [VMEM] * len(extra),
        out_specs=[VMEM] * len(shapes),
        scratch_shapes=[
            pltpu.VMEM((2, WIDE, rhs, line), BF16),
            pltpu.VMEM((count, line, line), line_inverse.dtype),
            pltpu.SemaphoreType.DMA((count,)),
        ],
        compiler_params=limit(42),
        cost_estimate=estimate(2 * count * rhs * line * line, count * line * line * 2),
    )(*windows, line_inverse, *extra)


def put_rim(a, b, value, at, refs):
    value = value.astype(BF16)
    first = at[0] == 0
    to_pair = first if b else jnp.logical_not(first)

    @pl.when(to_pair)
    def _():
        refs[0][a, 0] = value

    @pl.when(jnp.logical_not(to_pair))
    def _():
        refs[1][a, 0] = value


def returned(at, from_pair, from_outer, a, b):
    near, far = from_pair[a, 0], present(at[3], from_outer[a, 0])
    return jnp.where((at[0] == 0) == (b == 1), far, near).astype(F32)


def put_rows(a, b, value, at, refs):
    from_pair, from_outer, near, far = refs
    value = (value + returned(at, from_pair, from_outer, a, b)).astype(BF16)
    to_near = (at[4] == 0) == (a != 0)

    @pl.when(to_near)
    def _():
        near[0, b - 1] = value

    @pl.when(jnp.logical_not(to_near))
    def _():
        far[0, b - 1] = value


def put_inner(a, b, value, at, refs):
    refs[-1][a - 1, b - 1] = value


def columns(near, far, rounded):
    rhs, line = rounded.shape[2:]

    def body(near, far, rounded, pair, outer, own, ends):
        at = position()
        first, even = at[0] == 0, at[4] == 0
        for a in range(WIDE):
            if a in (0, WIDE - 1):
                for b in range(2):
                    low, high = (far, near) if a == 0 else (near, far)
                    ends[a // 2, b] = present(at[1 + a // 2], jnp.where(even, low[0, b], high[0, b]))
                left, right = ends[a // 2, 0], ends[a // 2, 1]
            else:
                left, right = rounded[a - 1, 0], rounded[a - 1, 1]
                own[a - 1, 0], own[a - 1, 1] = left, right
            pair[a, 0] = jnp.where(first, right, left)
            outer[a, 0] = jnp.where(first, left, right)

    out, square = struct((WIDE, 1, rhs, line), BF16), struct(rounded.shape, BF16)
    return pl.pallas_call(
        body,
        out_shape=[out, out, square, square],
        in_specs=[VMEM] * 3,
        out_specs=[VMEM] * 4,
        compiler_params=limit(4),
    )(near, far, rounded)


def rim_lines(windows, line_inverse):
    _, _, rhs, line = windows[0].shape
    column = struct((WIDE, 1, rhs, line), BF16)
    cells = [(a, b) for a in range(WIDE) for b in (0, WIDE - 1)]
    return line_solve(cells, put_rim, [column, column], windows, line_inverse)


def row_lines(windows, line_inverse, from_pair, from_outer):
    _, _, rhs, line = windows[0].shape
    row = struct((1, 2, rhs, line), BF16)
    cells = [(a, b) for a in (0, WIDE - 1) for b in (1, 2)]
    return line_solve(cells, put_rows, [row, row], windows, line_inverse, (from_pair, from_outer))


def inner_lines(windows, line_inverse):
    cells = [(a, b) for a in (1, 2) for b in (1, 2)]
    return line_solve(cells, put_inner, [struct(windows[0].shape, F32)], windows, line_inverse)[0]


def collect(inner, from_pair, from_outer, from_near, from_far):
    cx, cy, _, _ = inner.shape

    def body(inner, from_pair, from_outer, from_near, from_far, out):
        at = position()
        for a in range(cx):
            for b in range(cy):
                side = returned(at, from_pair, from_outer, a + 1, b + 1)
                low, high = (from_far, from_near) if a == 0 else (from_near, from_far)
                across = present(at[1 + a], jnp.where(at[4] == 0, low[0, b], high[0, b])).astype(F32)
                out[a, b] = inner[a, b] + side + across

    return pl.pallas_call(
        body,
        out_shape=struct(inner.shape, F32),
        in_specs=[VMEM] * 5,
        out_specs=VMEM,
        compiler_params=limit(8),
        cost_estimate=estimate(10**9, 4 * 10**6),
    )(inner, from_pair, from_outer, from_near, from_far)


def keep_mask(count, slots, rhs):
    return lax.broadcasted_iota(jnp.int32, (slots, rhs), 0) < count[0, 0]


def enter(residual_field, deflation, counts, copies):
    slots, line = deflation.shape[2:]
    cx, cy, rhs, _ = residual_field.shape

    def body(count, residual, vectors, rounded, near, far, spread, held, basis, cells, sums, sems):
        copies_in = []
        for a in range(cx):
            for b in range(cy):
                for n, (source, place) in enumerate(((residual, held), (vectors, basis))):
                    copy = pltpu.make_async_copy(source.at[a, b], place.at[a, b], sems.at[n, a, b])
                    copy.start()
                    copies_in.append(copy)
        total, copies_out = None, []
        for a in range(cx):
            for b in range(cy):
                for n in range(2):
                    copies_in[2 * (a * cy + b) + n].wait()
                value = held[a, b].astype(BF16)
                cells[a, b] = value
                part = lax.dot_general(
                    basis[a, b], value, (((1,), (1,)), ((), ())), preferred_element_type=F32
                )
                total = part if total is None else total + part
                copy = pltpu.make_async_copy(cells.at[a, b], rounded.at[a, b], sems.at[2, a, b])
                copy.start()
                copies_out.append(copy)
        even = position()[4] == 0
        for n, out in enumerate((near, far)):
            row = jnp.where(even, 1 - n, n)
            copy = pltpu.make_async_copy(cells.at[pl.ds(row, 1)], out, sems.at[3, n, 0])
            copy.start()
            copies_out.append(copy)
        total = jnp.where(keep_mask(count, slots, rhs), total, 0.0).astype(BF16)
        for i in range(copies):
            sums[i] = total
        copy = pltpu.make_async_copy(sums, spread, sems.at[0, 0, 0])
        copy.start()
        copy.wait()
        for copy in copies_out:
            copy.wait()

    row = struct((1, cy, rhs, line), BF16)
    return pl.pallas_call(
        body,
        out_shape=[struct(residual_field.shape, BF16), row, row, struct((copies, slots, rhs), BF16)],
        in_specs=[SMEM, HBM, HBM],
        out_specs=[HBM] * 4,
        scratch_shapes=[
            pltpu.VMEM(residual_field.shape, F32),
            pltpu.VMEM(deflation.shape, deflation.dtype),
            pltpu.VMEM(residual_field.shape, BF16),
            pltpu.VMEM((copies, slots, rhs), BF16),
            pltpu.SemaphoreType.DMA((4, cx, cy)),
        ],
        compiler_params=limit(60),
    )(counts, residual_field, deflation)


def halves(value):
    high = value.astype(BF16)
    return high, (value - high.astype(F32)).astype(BF16)


def cut_factor(factor, blocks, width):
    slots = factor.shape[0]

    def body(factor, *refs):
        outs, (held, sems, out_sems) = refs[:2], refs[2:]
        half = lax.axis_index("zl")
        copies = []
        for n, side in ((1, 1 - half), (0, half)):
            for j in range(blocks):
                start = pl.multiple_of((2 * j + side) * width, width)
                copy = pltpu.make_async_copy(factor.at[:, pl.ds(start, width)], held.at[n, j], sems.at[n, j])
                copy.start()
                copies.append(copy)
        saves = []
        for n in (1, 0):
            for j in range(blocks):
                copies[(1 - n) * blocks + j].wait()
            saves.append(pltpu.make_async_copy(held.at[n], outs[n], out_sems.at[n]))
            saves[-1].start()
        for save in saves:
            save.wait()

    return pl.pallas_call(
        body,
        out_shape=[struct((blocks, slots, width), F32)] * 2,
        in_specs=[HBM],
        out_specs=[HBM] * 2,
        scratch_shapes=[
            pltpu.VMEM((2, blocks, slots, width), F32),
            pltpu.SemaphoreType.DMA((2, blocks)),
            pltpu.SemaphoreType.DMA((2,)),
        ],
        compiler_params=limit(60),
    )(factor)


def lower(rows, gathered):
    blocks, slots, width = rows[0].shape
    count, _, rhs = gathered.shape
    per = count // blocks
    sets = len(rows)

    def body(*refs):
        rows, (gathered, out) = refs[:sets], refs[sets:]
        first = lax.axis_index("c") == 0
        zero = jnp.zeros((slots, rhs), BF16)
        total = None
        for j in range(blocks):
            pieces = []
            for y in range(per):
                mine = gathered[j * per + y]
                pieces += [jnp.where(first, mine, zero), jnp.where(first, zero, mine)]
            high, low = halves(jnp.concatenate([r[j] for r in rows], 0))
            part = jnp.dot(
                jnp.concatenate([high, low], 0), jnp.concatenate(pieces, 0), preferred_element_type=F32
            )
            total = part if total is None else total + part
        for n in range(sets):
            out[n] = total[n * slots : (n + 1) * slots] + total[(sets + n) * slots : (sets + n + 1) * slots]

    return pl.pallas_call(
        body,
        out_shape=struct((sets, slots, rhs), F32),
        in_specs=[VMEM] * (sets + 1),
        out_specs=VMEM,
        compiler_params=limit(8),
    )(*rows, gathered)


def raise_back(rows, partials):
    blocks, slots, width = rows[0].shape
    rhs = partials[0].shape[2]
    per = width // (2 * slots)
    sets = len(rows)

    def body(*refs):
        rows, partials, (out, made, sems) = refs[:sets], refs[sets : 2 * sets], refs[2 * sets :]
        first = lax.axis_index("c") == 0
        sums = []
        for n in range(sets):
            total = partials[0][n]
            for m in range(1, sets):
                total = total + partials[m][n ^ m]
            sums.append(total)
        lowered_high, lowered_low = halves(jnp.concatenate(sums, 0))
        over = (((0,), (0,)), ((), ()))
        copies = []
        for j in range(blocks):
            high, low = halves(jnp.concatenate([r[j] for r in rows], 0))
            part = lax.dot_general(high, lowered_high, over, preferred_element_type=F32)
            part = part + lax.dot_general(high, lowered_low, over, preferred_element_type=F32)
            part = part + lax.dot_general(low, lowered_high, over, preferred_element_type=F32)
            for y in range(per):
                a = part[2 * y * slots : (2 * y + 1) * slots]
                b = part[(2 * y + 1) * slots : (2 * y + 2) * slots]
                made[j * per + y] = jnp.where(first, a, b).astype(BF16)
            piece = pl.ds(j * per, per)
            copies.append(pltpu.make_async_copy(made.at[piece], out.at[piece], sems.at[j]))
            copies[j].start()
        for copy in copies:
            copy.wait()

    shape = (blocks * per, slots, rhs)
    return pl.pallas_call(
        body,
        out_shape=struct(shape, BF16),
        in_specs=[VMEM] * (2 * sets),
        out_specs=HBM,
        scratch_shapes=[pltpu.VMEM(shape, BF16), pltpu.SemaphoreType.DMA((blocks,))],
        compiler_params=limit(8),
    )(*rows, *partials)


def leave(counts, first_level, terms_in, deflation):
    cx, cy, rhs, line = first_level.shape
    slots = deflation.shape[2]

    def body(count, first_level, terms_in, vectors, out, held, basis, made, sems):
        loads = []
        for a in range(cx):
            for b in range(cy):
                for n, (source, place) in enumerate(((vectors, basis), (first_level, held))):
                    copy = pltpu.make_async_copy(source.at[a, b], place.at[a, b], sems.at[n, a, b])
                    copy.start()
                    loads.append(copy)
        total = terms_in[0].astype(F32)
        for i in range(1, terms_in.shape[0]):
            total = total + terms_in[i].astype(F32)
        solved = jnp.where(keep_mask(count, slots, rhs), total, 0.0).astype(BF16)
        saves = []
        for a in range(cx):
            for b in range(cy):
                for n in range(2):
                    loads[2 * (a * cy + b) + n].wait()
                value = lax.dot_general(
                    solved, basis[a, b], (((0,), (0,)), ((), ())), preferred_element_type=F32
                )
                made[a, b] = value + held[a, b]
                copy = pltpu.make_async_copy(made.at[a, b], out.at[a, b], sems.at[2, a, b])
                copy.start()
                saves.append(copy)
        for copy in saves:
            copy.wait()

    return pl.pallas_call(
        body,
        out_shape=struct(first_level.shape, F32),
        in_specs=[SMEM, HBM, VMEM, HBM],
        out_specs=HBM,
        scratch_shapes=[
            pltpu.VMEM(first_level.shape, F32),
            pltpu.VMEM(deflation.shape, deflation.dtype),
            pltpu.VMEM(first_level.shape, F32),
            pltpu.SemaphoreType.DMA((3, cx, cy)),
        ],
        compiler_params=limit(40),
    )(counts, first_level, terms_in, deflation)


def solution(mesh):
    n_grp, n_sub = mesh.shape["grp"], mesh.shape["sub"]
    sizes = {"zh": 2, "x": n_grp // 2, "zl": 2, "y": n_sub // 4, "c": 2}
    fine = Mesh(mesh.devices.reshape([sizes[a] for a in AXES]), AXES)

    def body(residual_field, line_inverse, deflation, counts, coarse_factor):
        tie = lax.optimization_barrier
        width = deflation.shape[2] * sizes["y"] * sizes["c"]

        rounded, to_near, to_far, spread = enter(residual_field, deflation, counts, n_grp * sizes["y"])
        near, far = swap_pairs(to_near, GRP, n_grp, 0), swap_pairs(to_far, GRP, n_grp, 1)
        coarse_factor, _ = tie((coarse_factor, to_near))
        kept, away = cut_factor(coarse_factor, n_grp, width)
        given = swap(away, "zl")
        far, _ = tie((far, kept))
        to_pair, to_outer, own, ends = columns(near, far, rounded)
        outer, pair = swap_outward(to_outer, n_sub), swap(to_pair, "c")
        spread, _ = tie((spread, to_outer))
        gathered = lax.all_to_all(spread, SPREAD, 0, 0)

        windows = (own, ends, pair, outer)
        to_pair, to_outer = rim_lines(windows, line_inverse)
        from_outer, from_pair = swap_outward(to_outer, n_sub), swap(to_pair, "c")
        gathered, kept, given, _ = tie((gathered, kept, given, to_outer))
        rows = (kept, given, swap(kept, "c"), swap(given, "c"))
        partial = lower(rows, gathered)
        partials = (partial, swap(partial, "zl"), swap(partial, "c"), swap_across(partial))
        own, _ = tie((own, partial))
        inner = inner_lines((own, ends, pair, outer), line_inverse)
        partial, own, inner = tie((partial, own, inner))
        terms_out = raise_back(rows, (partial, *partials[1:]))
        terms_in = lax.all_to_all(terms_out, SPREAD, 0, 0)
        own, _ = tie((own, terms_out))
        to_near, to_far = row_lines((own, ends, pair, outer), line_inverse, from_pair, from_outer)
        from_near, from_far = swap_pairs(to_near, GRP, n_grp, 0), swap_pairs(to_far, GRP, n_grp, 1)
        first_level = collect(inner, from_pair, from_outer, from_near, from_far)
        return leave(counts, first_level, terms_in, deflation)

    return jax.shard_map(
        body,
        mesh=fine,
        in_specs=(
            P(GRP, SUB, None, None),
            P(GRP, SUB, None, None, None),
            P(GRP, SUB, None, None),
            P(GRP, SUB),
            P(AXES, None),
        ),
        out_specs=P(GRP, SUB, None, None),
        check_vma=False,
    )
```

time: 108 us -> 84.5 us (0.78)
  the two profiles are of different devices: /device:TPU:38 before, /device:TPU:6 now
where the time goes in v2:
time: 84.5 us; the launch traced here: 84 us
  starting transfers between devices  37.2 us (44%)
  Pallas kernels  25.2 us (30%)
  waiting for transfers between devices  18.9 us (22%)
  local copies, waits for them, and re-layouts  1.91 us (2%)
    pallas_call x3, Pallas kernels, line_solve(): pl.pallas_call(body, out_shape=shapes, in_specs=[VMEM] * 4 + [HBM] + [VME...  12.5 us
    ppermute x4, starting transfers between devices, swap_pairs(): return lax.ppermute(value, axes, pairs)  12.2 us
    ppermute x4, waiting for transfers between devices, swap_pairs(): return lax.ppermute(value, axes, pairs)  9.31 us
    all_to_all x1, starting transfers between devices, body(): terms_in = lax.all_to_all(terms_out, SPREAD, 0, 0)  8.12 us
    ppermute x2, starting transfers between devices, swap_outward(): return lax.ppermute(value, SUB, pairs)  7.46 us
    all_to_all x1, starting transfers between devices, body(): gathered = lax.all_to_all(spread, SPREAD, 0, 0)  5.5 us
    all_to_all x1, waiting for transfers between devices, body(): gathered = lax.all_to_all(spread, SPREAD, 0, 0)  5.22 us
    pallas_call x1, Pallas kernels, leave(): pl.pallas_call(body, out_shape=struct(first_level.shape, F32), in_specs=[...  2.71 us
  transfers between devices with their start and end apart: 16, of which 5 were waited for; matrix products, arithmetic and copies ran while one was open for 0% of the time, Pallas kernels for 24%

profile of v2, /device:TPU:6, one launch (start us, length us, event | category | flops | bytes accessed | tf_op | source)
XLA Modules:
  0.0 84.0 jit_solution(17024261089260587714)
XLA Ops:
  0.7 2.5 %shard_map.55 = (bf16[2,2,128,384]{3,2,1,0:T(8,128)(2,1)}, bf16[1,2,128,384]{3,2,1,0:T(8,128)(2,1)}, bf16[1,2,128,384]{3,2,1,0:T(8,128)(2,1)}, bf16[32,48,128]{2,1,0:T(8,128)(2,1)}) custom-call(s32[1,1]{1,0:T(1,128)S(6)} %copy.6.count, f32[2,2,128,384]{3,2,1,0:T(8,128)} %residual.1, bf16[2,2,48,384]{3,2,1,0:T(8,128)(2,1)} %vectors.3), custom_call_target="tpu_custom_call" | custom-call | tf_op jit(solution)/shard_map/pallas_call | solution.py:296
  3.2 5.7 %collective-permute-start.1 = (bf16[1,2,128,384]{3,2,1,0:T(8,128)(2,1)}, bf16[1,2,128,384]{3,2,1,0:T(8,128)(2,1)S(1)}, u32[]{:S(2)}, u32[]{:S(2)}) collective-permute-start(bf16[1,2,128,384]{3,2,1,0:T(8,128)(2,1)} %get-tuple-element.32), channel_id=1, source_target_pairs={{16,32},{32,16},{48,64},{64,48},{80,96},{96,80},{17,33},{33,17},{4... | collective-permute-start | bytes 589832 | tf_op jit(solution)/shard_map/ppermute | solution.py:48
  8.9 0.1 collective-permute-start
  9.0 2.3 %shard_map.56 = (f32[8,48,384]{2,1,0:T(8,128)}, f32[8,48,384]{2,1,0:T(8,128)}) custom-call(f32[48,6144]{1,0:T(8,128)} %factor), custom_call_target="tpu_custom_call" | custom-call | tf_op jit(solution)/shard_map/pallas_call | solution.py:339
  11.3 1.1 %collective-permute-start.2 = (f32[8,48,384]{2,1,0:T(8,128)}, f32[8,48,384]{2,1,0:T(8,128)S(1)}, u32[]{:S(2)}, u32[]{:S(2)}) collective-permute-start(f32[8,48,384]{2,1,0:T(8,128)} %get-tuple-element.39), channel_id=1, source_target_pairs={{0,8},{8,0},{1,9},{9,1},{2,10},{10,2},{3,11},{11,3},{4,12},{12,4},... | collective-permute-start | bytes 1769480 | tf_op jit(solution)/shard_map/ppermute | solution.py:37
  12.4 3.2 %collective-permute-done.1.far = bf16[1,2,128,384]{3,2,1,0:T(8,128)(2,1)S(1)} collective-permute-done((bf16[1,2,128,384]{3,2,1,0:T(8,128)(2,1)}, bf16[1,2,128,384]{3,2,1,0:T(8,128)(2,1)S(1)}, u32[]{:S(2)}, u32[]{:S(2)}) %collective-permute-start.1) | collective-permute-done | bytes 196640 | tf_op jit(solution)/shard_map/ppermute | solution.py:48
  15.6 1.0 %copy-done.2 = bf16[2,2,128,384]{3,2,1,0:T(8,128)(2,1)S(1)} copy-done((bf16[2,2,128,384]{3,2,1,0:T(8,128)(2,1)S(1)}, bf16[2,2,128,384]{3,2,1,0:T(8,128)(2,1)}, u32[]{:S(2)}) %copy-start.2) | copy-done | bytes 393240
  16.6 0.9 %shard_map.57 = (bf16[4,1,128,384]{3,2,1,0:T(8,128)(2,1)}, bf16[4,1,128,384]{3,2,1,0:T(8,128)(2,1)S(1)}, bf16[2,2,128,384]{3,2,1,0:T(8,128)(2,1)S(1)}, bf16[2,2,128,384]{3,2,1,0:T(8,128)(2,1)S(1)}) custom-call(bf16[1,2,128,384]{3,2,1,0:T(8,128)(2,1)S(1)} %collective-permute-done.near, bf16[1,2,128,384]{3,2,1,0:T(8,128)(2,1)S(1)} %collective-permute-done.1.far, ...), custom_call_target="tpu_custom_call" | custom-call | tf_op jit(solution)/shard_map/pallas_call | solution.py:200
  17.6 4.5 %collective-permute-start.4 = (bf16[4,1,128,384]{3,2,1,0:T(8,128)(2,1)S(1)}, bf16[4,1,128,384]{3,2,1,0:T(8,128)(2,1)S(1)}, u32[]{:S(2)}, u32[]{:S(2)}) collective-permute-start(bf16[4,1,128,384]{3,2,1,0:T(8,128)(2,1)S(1)} %get-tuple-element.37), channel_id=1, source_target_pairs={{1,2},{2,1},{3,4},{4,3},{5,6},{6,5},{7,8},{8,7},{9,10},{10,9},{11,... | collective-permute-start | bytes 1179656 | tf_op jit(solution)/shard_map/ppermute | solution.py:55
  22.0 5.5 %all-to-all-start = ((bf16[32,48,128]{2,1,0:T(8,128)(2,1)}), bf16[32,48,128]{2,1,0:T(8,128)(2,1)S(1)}, u32[]{:S(2)}, u32[]{:S(2)}) async-start(bf16[32,48,128]{2,1,0:T(8,128)(2,1)} %get-tuple-element.38), calls=%async_computation | async-start | bytes 786432 | tf_op jit(solution)/shard_map/all_to_all | solution.py:494
  27.6 0.0 collective-permute-done.4.refs_3_
  27.6 5.2 %shard_map.58 = (bf16[4,1,128,384]{3,2,1,0:T(8,128)(2,1)}, bf16[4,1,128,384]{3,2,1,0:T(8,128)(2,1)}) custom-call(bf16[2,2,128,384]{3,2,1,0:T(8,128)(2,1)S(1)} %get-tuple-element.52.refs_0_, bf16[2,2,128,384]{3,2,1,0:T(8,128)(2,1)S(1)} %get-tuple-element.41.refs_1_, bf16[4,1,128,384]{3,2,1,0:T(8,128)(2,1)S(1)} %collective-permute-done.3.refs_2_, ...), custom_call_target="tpu_custom_call" | custom-call | flops 1056964608 | bytes 8257536 | tf_op jit(solution)/shard_map/pallas_call | solution.py:129
  32.8 5.2 %all-to-all-done.refs_4_ = bf16[32,48,128]{2,1,0:T(8,128)(2,1)S(1)} async-done(((bf16[32,48,128]{2,1,0:T(8,128)(2,1)}), bf16[32,48,128]{2,1,0:T(8,128)(2,1)S(1)}, u32[]{:S(2)}, u32[]{:S(2)}) %all-to-all-start) | async-done | bytes 393248 | tf_op jit(solution)/shard_map/all_to_all | solution.py:494
  38.0 0.5 collective-permute-start.6
  38.5 0.1 collective-permute-start.7
  38.6 3.0 %collective-permute-start.8 = (bf16[4,1,128,384]{3,2,1,0:T(8,128)(2,1)}, bf16[4,1,128,384]{3,2,1,0:T(8,128)(2,1)}, u32[]{:S(2)}, u32[]{:S(2)}) collective-permute-start(bf16[4,1,128,384]{3,2,1,0:T(8,128)(2,1)} %get-tuple-element.43), channel_id=1, source_target_pairs={{1,2},{2,1},{3,4},{4,3},{5,6},{6,5},{7,8},{8,7},{9,10},{10,9},{11,... | collective-permute-start | bytes 1179656 | tf_op jit(solution)/shard_map/ppermute | solution.py:55
  41.6 0.8 shard_map.59.refs_4_
  42.4 0.9 %collective-permute-start.9 = (f32[4,48,128]{2,1,0:T(8,128)S(1)}, f32[4,48,128]{2,1,0:T(8,128)S(1)}, u32[]{:S(2)}, u32[]{:S(2)}) collective-permute-start(f32[4,48,128]{2,1,0:T(8,128)S(1)} %shard_map.59.refs_4_), channel_id=1, source_target_pairs={{0,8},{8,0},{1,9},{9,1},{2,10},{10,2},{3,11},{11,3},{4,12},{12,4},... | collective-permute-start | bytes 294920 | tf_op jit(solution)/shard_map/ppermute | solution.py:37
  43.3 1.3 %collective-permute-start.11 = (f32[4,48,128]{2,1,0:T(8,128)S(1)}, f32[4,48,128]{2,1,0:T(8,128)S(1)}, u32[]{:S(2)}, u32[]{:S(2)}) collective-permute-start(f32[4,48,128]{2,1,0:T(8,128)S(1)} %shard_map.59.refs_4_), channel_id=1, source_target_pairs={{0,9},{1,8},{8,1},{9,0},{2,11},{3,10},{10,3},{11,2},{4,13},{5,12},... | collective-permute-start | bytes 294920 | tf_op jit(solution)/shard_map/ppermute | solution.py:41
  44.6 3.3 %shard_map.60.inner = f32[2,2,128,384]{3,2,1,0:T(8,128)S(1)} custom-call(bf16[2,2,128,384]{3,2,1,0:T(8,128)(2,1)S(1)} %get-tuple-element.52.refs_0_, bf16[2,2,128,384]{3,2,1,0:T(8,128)(2,1)S(1)} %get-tuple-element.41.refs_1_, bf16[4,1,128,384]{3,2,1,0:T(8,128)(2,1)S(1)} %collective-permute-done.3.refs_2_, ...), custom_call_target="tpu_custom_call" | custom-call | flops 754974720 | bytes 5898240 | tf_op jit(solution)/shard_map/pallas_call | solution.py:129
  47.9 2.4 %collective-permute-done.9.refs_5_ = f32[4,48,128]{2,1,0:T(8,128)S(1)} collective-permute-done((f32[4,48,128]{2,1,0:T(8,128)S(1)}, f32[4,48,128]{2,1,0:T(8,128)S(1)}, u32[]{:S(2)}, u32[]{:S(2)}) %collective-permute-start.9) | collective-permute-done | bytes 98336 | tf_op jit(solution)/shard_map/ppermute | solution.py:37
  50.3 1.9 %collective-permute-done.11.refs_7_ = f32[4,48,128]{2,1,0:T(8,128)S(1)} collective-permute-done((f32[4,48,128]{2,1,0:T(8,128)S(1)}, f32[4,48,128]{2,1,0:T(8,128)S(1)}, u32[]{:S(2)}, u32[]{:S(2)}) %collective-permute-start.11) | collective-permute-done | bytes 98336 | tf_op jit(solution)/shard_map/ppermute | solution.py:41
  52.2 2.1 %shard_map.61 = bf16[32,48,128]{2,1,0:T(8,128)(2,1)} custom-call(f32[8,48,384]{2,1,0:T(8,128)S(1)} %copy-done, f32[8,48,384]{2,1,0:T(8,128)S(1)} %collective-permute-done.2.refs_1_, f32[8,48,384]{2,1,0:T(8,128)S(1)} %collective-permute-done.5.refs_2_, f32[8,48,384]{2,1,0:T(8,128)S(1)} %collective-permute-done.6.refs_3_, ...), custom_call_target="tpu_custom_call" | custom-call | tf_op jit(solution)/shard_map/pallas_call | solution.py:420
  54.4 8.1 %all-to-all-start.1 = ((bf16[32,48,128]{2,1,0:T(8,128)(2,1)}), bf16[32,48,128]{2,1,0:T(8,128)(2,1)S(1)}, u32[]{:S(2)}, u32[]{:S(2)}) async-start(bf16[32,48,128]{2,1,0:T(8,128)(2,1)} %shard_map.61), calls=%async_computation.1 | async-start | bytes 786432 | tf_op jit(solution)/shard_map/all_to_all | solution.py:507
  62.5 4.1 %shard_map.62 = (bf16[1,2,128,384]{3,2,1,0:T(8,128)(2,1)S(1)}, bf16[1,2,128,384]{3,2,1,0:T(8,128)(2,1)S(1)}) custom-call(bf16[2,2,128,384]{3,2,1,0:T(8,128)(2,1)S(1)} %get-tuple-element.52.refs_0_, bf16[2,2,128,384]{3,2,1,0:T(8,128)(2,1)S(1)} %get-tuple-element.41.refs_1_, bf16[4,1,128,384]{3,2,1,0:T(8,128)(2,1)S(1)} %collective-permute-done.3.refs_2_, ...), custom_call_target="tpu_custom_call" | custom-call | flops 603979776 | bytes 4718592 | tf_op jit(solution)/shard_map/pallas_call | solution.py:129
  66.6 0.9 %collective-permute-start.12 = (bf16[1,2,128,384]{3,2,1,0:T(8,128)(2,1)S(1)}, bf16[1,2,128,384]{3,2,1,0:T(8,128)(2,1)S(1)}, u32[]{:S(2)}, u32[]{:S(2)}) collective-permute-start(bf16[1,2,128,384]{3,2,1,0:T(8,128)(2,1)S(1)} %get-tuple-element.53), channel_id=1, source_target_pairs={{0,16},{16,0},{32,48},{48,32},{64,80},{80,64},{96,112},{112,96},{1... | collective-permute-start | bytes 589832 | tf_op jit(solution)/shard_map/ppermute | solution.py:48
  67.5 5.5 %collective-permute-start.13 = (bf16[1,2,128,384]{3,2,1,0:T(8,128)(2,1)S(1)}, bf16[1,2,128,384]{3,2,1,0:T(8,128)(2,1)S(1)}, u32[]{:S(2)}, u32[]{:S(2)}) collective-permute-start(bf16[1,2,128,384]{3,2,1,0:T(8,128)(2,1)S(1)} %get-tuple-element.54), channel_id=1, source_target_pairs={{16,32},{32,16},{48,64},{64,48},{80,96},{96,80},{17,33},{33,17},{4... | collective-permute-start | bytes 589832 | tf_op jit(solution)/shard_map/ppermute | solution.py:48
  73.0 0.0 collective-permute-done.12.from_near
  73.0 6.1 %collective-permute-done.13.from_far = bf16[1,2,128,384]{3,2,1,0:T(8,128)(2,1)S(1)} collective-permute-done((bf16[1,2,128,384]{3,2,1,0:T(8,128)(2,1)S(1)}, bf16[1,2,128,384]{3,2,1,0:T(8,128)(2,1)S(1)}, u32[]{:S(2)}, u32[]{:S(2)}) %collective-permute-start.13) | collective-permute-done | bytes 196640 | tf_op jit(solution)/shard_map/ppermute | solution.py:48
  79.1 1.3 %shard_map.63.first_level = f32[2,2,128,384]{3,2,1,0:T(8,128)S(1)} custom-call(f32[2,2,128,384]{3,2,1,0:T(8,128)S(1)} %shard_map.60.inner, bf16[4,1,128,384]{3,2,1,0:T(8,128)(2,1)} %collective-permute-done.7.refs_5_.from_pair, bf16[4,1,128,384]{3,2,1,0:T(8,128)(2,1)} %collective-permute-done.8.refs_6_.from_outer, ...), custom_call_target="tpu_custom_call" | custom-call | flops 1000000000 | bytes 4000000 | tf_op jit(solution)/shard_map/pallas_call | solution.py:240
  80.4 0.9 %copy-done.1 = bf16[2,2,48,384]{3,2,1,0:T(8,128)(2,1)S(1)} copy-done((bf16[2,2,48,384]{3,2,1,0:T(8,128)(2,1)S(1)}, bf16[2,2,48,384]{3,2,1,0:T(8,128)(2,1)}, u32[]{:S(2)}) %copy-start.1) | copy-done | bytes 147480
  81.3 2.7 %shard_map.64 = f32[2,2,128,384]{3,2,1,0:T(8,128)} custom-call(s32[1,1]{1,0:T(1,128)S(6)} %copy.6.count, f32[2,2,128,384]{3,2,1,0:T(8,128)S(1)} %shard_map.63.first_level, bf16[32,48,128]{2,1,0:T(8,128)(2,1)S(1)} %all-to-all-done.1.terms_in, bf16[2,2,48,384]{3,2,1,0:T(8,128)(2,1)S(1)} %copy-done.1), custom_call_target="tpu_custom_call" | custom-call | tf_op jit(solution)/shard_map/pallas_call | solution.py:461
  (16 shorter events, 0.0 us)
Async XLA Ops:
  3.2 12.5 %collective-permute-start.1 = (bf16[1,2,128,384]{3,2,1,0:T(8,128)(2,1)}, bf16[1,2,128,384]{3,2,1,0:T(8,128)(2,1)S(1)}, u32[]{:S(2)}, u32[]{:S(2)}) collective-permute-start(bf16[1,2,128,384]{3,2,1,0:T(8,128)(2,1)} %get-tuple-element.32), channel_id=1, source_target_pairs={{16,32},{32,16},{48,64},{64,48},{80,96},{96,80},{17,33},{33,17},{4... | collective-permute-start | bytes 589832 | tf_op jit(solution)/shard_map/ppermute | solution.py:48
  8.9 6.8 %collective-permute-start = (bf16[1,2,128,384]{3,2,1,0:T(8,128)(2,1)}, bf16[1,2,128,384]{3,2,1,0:T(8,128)(2,1)S(1)}, u32[]{:S(2)}, u32[]{:S(2)}) collective-permute-start(bf16[1,2,128,384]{3,2,1,0:T(8,128)(2,1)} %get-tuple-element.31), channel_id=1, source_target_pairs={{0,16},{16,0},{32,48},{48,32},{64,80},{80,64},{96,112},{112,96},{1... | collective-permute-start | bytes 589832 | tf_op jit(solution)/shard_map/ppermute | solution.py:48
  11.3 26.7 %copy-start = (f32[8,48,384]{2,1,0:T(8,128)S(1)}, f32[8,48,384]{2,1,0:T(8,128)}, u32[]{:S(2)}) copy-start(f32[8,48,384]{2,1,0:T(8,128)} %get-tuple-element.44.refs_0_) | copy-start | bytes 1769476
  11.3 26.7 %collective-permute-start.2 = (f32[8,48,384]{2,1,0:T(8,128)}, f32[8,48,384]{2,1,0:T(8,128)S(1)}, u32[]{:S(2)}, u32[]{:S(2)}) collective-permute-start(f32[8,48,384]{2,1,0:T(8,128)} %get-tuple-element.39), channel_id=1, source_target_pairs={{0,8},{8,0},{1,9},{9,1},{2,10},{10,2},{3,11},{11,3},{4,12},{12,4},... | collective-permute-start | bytes 1769480 | tf_op jit(solution)/shard_map/ppermute | solution.py:37
  15.6 1.0 %copy-start.2 = (bf16[2,2,128,384]{3,2,1,0:T(8,128)(2,1)S(1)}, bf16[2,2,128,384]{3,2,1,0:T(8,128)(2,1)}, u32[]{:S(2)}) copy-start(bf16[2,2,128,384]{3,2,1,0:T(8,128)(2,1)} %get-tuple-element.36.rounded) | copy-start | bytes 1179652
  17.6 10.0 %collective-permute-start.3 = (bf16[4,1,128,384]{3,2,1,0:T(8,128)(2,1)}, bf16[4,1,128,384]{3,2,1,0:T(8,128)(2,1)S(1)}, u32[]{:S(2)}, u32[]{:S(2)}) collective-permute-start(bf16[4,1,128,384]{3,2,1,0:T(8,128)(2,1)} %get-tuple-element.42), channel_id=1, source_target_pairs={{0,1},{1,0},{2,3},{3,2},{4,5},{5,4},{6,7},{7,6},{8,9},{9,8},{10,11... | collective-permute-start | bytes 1179656 | tf_op jit(solution)/shard_map/ppermute | solution.py:37
  17.6 10.0 %collective-permute-start.4 = (bf16[4,1,128,384]{3,2,1,0:T(8,128)(2,1)S(1)}, bf16[4,1,128,384]{3,2,1,0:T(8,128)(2,1)S(1)}, u32[]{:S(2)}, u32[]{:S(2)}) collective-permute-start(bf16[4,1,128,384]{3,2,1,0:T(8,128)(2,1)S(1)} %get-tuple-element.37), channel_id=1, source_target_pairs={{1,2},{2,1},{3,4},{4,3},{5,6},{6,5},{7,8},{8,7},{9,10},{10,9},{11,... | collective-permute-start | bytes 1179656 | tf_op jit(solution)/shard_map/ppermute | solution.py:55
  22.0 16.0 %all-to-all-start = ((bf16[32,48,128]{2,1,0:T(8,128)(2,1)}), bf16[32,48,128]{2,1,0:T(8,128)(2,1)S(1)}, u32[]{:S(2)}, u32[]{:S(2)}) async-start(bf16[32,48,128]{2,1,0:T(8,128)(2,1)} %get-tuple-element.38), calls=%async_computation | async-start | bytes 786432 | tf_op jit(solution)/shard_map/all_to_all | solution.py:494
  38.0 3.6 %collective-permute-start.5 = (f32[8,48,384]{2,1,0:T(8,128)S(1)}, f32[8,48,384]{2,1,0:T(8,128)S(1)}, u32[]{:S(2)}, u32[]{:S(2)}) collective-permute-start(f32[8,48,384]{2,1,0:T(8,128)S(1)} %copy-done), channel_id=1, source_target_pairs={{0,1},{1,0},{2,3},{3,2},{4,5},{5,4},{6,7},{7,6},{8,9},{9,8},{10,11... | collective-permute-start | bytes 1769480 | tf_op jit(solution)/shard_map/ppermute | solution.py:37
  38.0 3.6 %collective-permute-start.6 = (f32[8,48,384]{2,1,0:T(8,128)S(1)}, f32[8,48,384]{2,1,0:T(8,128)S(1)}, u32[]{:S(2)}, u32[]{:S(2)}) collective-permute-start(f32[8,48,384]{2,1,0:T(8,128)S(1)} %collective-permute-done.2.refs_1_), channel_id=1, source_target_pairs={{0,1},{1,0},{2,3},{3,2},{4,5},{5,4},{6,7},{7,6},{8,9},{9,8},{10,11... | collective-permute-start | bytes 1769480 | tf_op jit(solution)/shard_map/ppermute | solution.py:37
  38.5 24.0 %collective-permute-start.7 = (bf16[4,1,128,384]{3,2,1,0:T(8,128)(2,1)}, bf16[4,1,128,384]{3,2,1,0:T(8,128)(2,1)}, u32[]{:S(2)}, u32[]{:S(2)}) collective-permute-start(bf16[4,1,128,384]{3,2,1,0:T(8,128)(2,1)} %get-tuple-element.49), channel_id=1, source_target_pairs={{0,1},{1,0},{2,3},{3,2},{4,5},{5,4},{6,7},{7,6},{8,9},{9,8},{10,11... | collective-permute-start | bytes 1179656 | tf_op jit(solution)/shard_map/ppermute | solution.py:37
  38.6 23.9 %collective-permute-start.8 = (bf16[4,1,128,384]{3,2,1,0:T(8,128)(2,1)}, bf16[4,1,128,384]{3,2,1,0:T(8,128)(2,1)}, u32[]{:S(2)}, u32[]{:S(2)}) collective-permute-start(bf16[4,1,128,384]{3,2,1,0:T(8,128)(2,1)} %get-tuple-element.43), channel_id=1, source_target_pairs={{1,2},{2,1},{3,4},{4,3},{5,6},{6,5},{7,8},{8,7},{9,10},{10,9},{11,... | collective-permute-start | bytes 1179656 | tf_op jit(solution)/shard_map/ppermute | solution.py:55
  42.4 8.0 %collective-permute-start.9 = (f32[4,48,128]{2,1,0:T(8,128)S(1)}, f32[4,48,128]{2,1,0:T(8,128)S(1)}, u32[]{:S(2)}, u32[]{:S(2)}) collective-permute-start(f32[4,48,128]{2,1,0:T(8,128)S(1)} %shard_map.59.refs_4_), channel_id=1, source_target_pairs={{0,8},{8,0},{1,9},{9,1},{2,10},{10,2},{3,11},{11,3},{4,12},{12,4},... | collective-permute-start | bytes 294920 | tf_op jit(solution)/shard_map/ppermute | solution.py:37
  43.3 7.0 %collective-permute-start.10 = (f32[4,48,128]{2,1,0:T(8,128)S(1)}, f32[4,48,128]{2,1,0:T(8,128)S(1)}, u32[]{:S(2)}, u32[]{:S(2)}) collective-permute-start(f32[4,48,128]{2,1,0:T(8,128)S(1)} %shard_map.59.refs_4_), channel_id=1, source_target_pairs={{0,1},{1,0},{2,3},{3,2},{4,5},{5,4},{6,7},{7,6},{8,9},{9,8},{10,11... | collective-permute-start | bytes 294920 | tf_op jit(solution)/shard_map/ppermute | solution.py:37
  43.3 8.9 %collective-permute-start.11 = (f32[4,48,128]{2,1,0:T(8,128)S(1)}, f32[4,48,128]{2,1,0:T(8,128)S(1)}, u32[]{:S(2)}, u32[]{:S(2)}) collective-permute-start(f32[4,48,128]{2,1,0:T(8,128)S(1)} %shard_map.59.refs_4_), channel_id=1, source_target_pairs={{0,9},{1,8},{8,1},{9,0},{2,11},{3,10},{10,3},{11,2},{4,13},{5,12},... | collective-permute-start | bytes 294920 | tf_op jit(solution)/shard_map/ppermute | solution.py:41
  54.4 26.0 %all-to-all-start.1 = ((bf16[32,48,128]{2,1,0:T(8,128)(2,1)}), bf16[32,48,128]{2,1,0:T(8,128)(2,1)S(1)}, u32[]{:S(2)}, u32[]{:S(2)}) async-start(bf16[32,48,128]{2,1,0:T(8,128)(2,1)} %shard_map.61), calls=%async_computation.1 | async-start | bytes 786432 | tf_op jit(solution)/shard_map/all_to_all | solution.py:507
  66.6 6.4 %collective-permute-start.12 = (bf16[1,2,128,384]{3,2,1,0:T(8,128)(2,1)S(1)}, bf16[1,2,128,384]{3,2,1,0:T(8,128)(2,1)S(1)}, u32[]{:S(2)}, u32[]{:S(2)}) collective-permute-start(bf16[1,2,128,384]{3,2,1,0:T(8,128)(2,1)S(1)} %get-tuple-element.53), channel_id=1, source_target_pairs={{0,16},{16,0},{32,48},{48,32},{64,80},{80,64},{96,112},{112,96},{1... | collective-permute-start | bytes 589832 | tf_op jit(solution)/shard_map/ppermute | solution.py:48
  67.5 11.6 %collective-permute-start.13 = (bf16[1,2,128,384]{3,2,1,0:T(8,128)(2,1)S(1)}, bf16[1,2,128,384]{3,2,1,0:T(8,128)(2,1)S(1)}, u32[]{:S(2)}, u32[]{:S(2)}) collective-permute-start(bf16[1,2,128,384]{3,2,1,0:T(8,128)(2,1)S(1)} %get-tuple-element.54), channel_id=1, source_target_pairs={{16,32},{32,16},{48,64},{64,48},{80,96},{96,80},{17,33},{33,17},{4... | collective-permute-start | bytes 589832 | tf_op jit(solution)/shard_map/ppermute | solution.py:48
  80.4 0.9 %copy-start.1 = (bf16[2,2,48,384]{3,2,1,0:T(8,128)(2,1)S(1)}, bf16[2,2,48,384]{3,2,1,0:T(8,128)(2,1)}, u32[]{:S(2)}) copy-start(bf16[2,2,48,384]{3,2,1,0:T(8,128)(2,1)} %vectors.3) | copy-start | bytes 442372

commit v3 on v2

--- a/solution.py
+++ b/solution.py
@@ -8,7 +8,8 @@
 AXES = ("zh", "x", "zl", "y", "c")
 GRP = ("zh", "x")
 SUB = ("zl", "y", "c")
-SPREAD = ("zh", "x", "y")
+SPREAD = ("zh", "zl", "y")
+RING = "x"
 
 STEPS = ((-1, 0), (0, -1), (0, 0), (0, 1), (1, 0))
 WIDE = 4
@@ -33,12 +34,12 @@
     return pl.CostEstimate(flops=flops, bytes_accessed=size, transcendentals=0)
 
 
+def rotate(value, axes, size, step):
+    return lax.ppermute(value, axes, [(i, (i + step) % size) for i in range(size)])
+
+
 def swap(value, axis):
     return lax.ppermute(value, axis, [(0, 1), (1, 0)])
-
-
-def swap_across(value):
-    return lax.ppermute(value, ("zl", "c"), [(i, 3 - i) for i in range(4)])
 
 
 def swap_pairs(value, axes, size, begin):
@@ -78,9 +79,17 @@
     return core, before, after, past, lax.rem(x, 2)
 
 
-def line_kernel(cells, put, own, ends, pair, outer, blocks, *rest):
+def line_kernel(cells, put, fetch, own, ends, pair, outer, blocks, *rest):
     at = position()
     more, (sides, held, sems) = rest[:-3], rest[-3:]
+    if fetch:
+        window_sems, more = more[-1], more[:-1]
+        targets, more = more[-2:], more[:-2]
+        loads = []
+        for i, (source, target) in enumerate(zip((own, ends), targets)):
+            loads.append(pltpu.make_async_copy(source, target, window_sems.at[i]))
+            loads[i].start()
+        own, ends = targets
     slot, plan = 0, []
     for a, b in cells:
         found = terms(a, b)
@@ -94,6 +103,9 @@
                 slot, run = slot + run, 0
         plan.append((start, copies, found))
 
+    if fetch:
+        for load in loads:
+            load.wait()
     first = at[0] == 0
     for a in range(WIDE):
         near, far = pair[a, 0], present(at[3], outer[a, 0])
@@ -118,20 +130,23 @@
         put(a, b, jnp.dot(sources, weights, preferred_element_type=F32), at, more)
 
 
-def line_solve(cells, put, shapes, windows, line_inverse, extra=()):
+def line_solve(cells, put, shapes, windows, line_inverse, extra=(), fetch=False):
     count = sum(len(terms(a, b)) for a, b in cells)
     line = line_inverse.shape[-1]
     rhs = windows[0].shape[2]
 
     def body(*refs):
-        line_kernel(cells, put, *refs)
-
+        line_kernel(cells, put, fetch, *refs)
+
+    if fetch:
+        shapes = shapes + [struct(w.shape, w.dtype) for w in windows[:2]]
     return pl.pallas_call(
         body,
         out_shape=shapes,
-        in_specs=[VMEM] * 4 + [HBM] + [VMEM] * len(extra),
+        in_specs=[ANY if fetch else VMEM] * 2 + [VMEM] * 2 + [HBM] + [VMEM] * len(extra),
         out_specs=[VMEM] * len(shapes),
-        scratch_shapes=[
+        scratch_shapes=[pltpu.SemaphoreType.DMA((2,))] * fetch
+        + [
             pltpu.VMEM((2, WIDE, rhs, line), BF16),
             pltpu.VMEM((count, line, line), line_inverse.dtype),
             pltpu.SemaphoreType.DMA((count,)),
@@ -210,7 +225,7 @@
     _, _, rhs, line = windows[0].shape
     column = struct((WIDE, 1, rhs, line), BF16)
     cells = [(a, b) for a in range(WIDE) for b in (0, WIDE - 1)]
-    return line_solve(cells, put_rim, [column, column], windows, line_inverse)
+    return line_solve(cells, put_rim, [column, column], windows, line_inverse, fetch=True)
 
 
 def row_lines(windows, line_inverse, from_pair, from_outer):
@@ -251,62 +266,72 @@
     return lax.broadcasted_iota(jnp.int32, (slots, rhs), 0) < count[0, 0]
 
 
-def enter(residual_field, deflation, counts, copies):
+def round_cells(residual_field):
+    cx, cy, rhs, line = residual_field.shape
+
+    def body(residual, rounded, near, far):
+        even = position()[4] == 0
+        for b in range(cy):
+            first, second = residual[0, b].astype(BF16), residual[1, b].astype(BF16)
+            rounded[0, b], rounded[1, b] = first, second
+            near[0, b] = jnp.where(even, second, first)
+            far[0, b] = jnp.where(even, first, second)
+
+    row = struct((1, cy, rhs, line), BF16)
+    return pl.pallas_call(
+        body,
+        out_shape=[struct(residual_field.shape, BF16), row, row],
+        in_specs=[VMEM],
+        out_specs=[VMEM] * 3,
+        compiler_params=limit(4),
+    )(residual_field)
+
+
+def prepare(rounded, deflation, counts, factor, copies, ring, blocks):
     slots, line = deflation.shape[2:]
-    cx, cy, rhs, _ = residual_field.shape
-
-    def body(count, residual, vectors, rounded, near, far, spread, held, basis, cells, sums, sems):
-        copies_in = []
+    cx, cy, rhs, _ = rounded.shape
+    width = factor.shape[1] // (ring * blocks)
+
+    def body(count, rounded, vectors, factor, *refs):
+        spread, parts = refs[0], refs[1 : 1 + ring]
+        made, cut, sems = refs[1 + ring :]
+        here = lax.axis_index("x")
+        saves = []
+        for step in range(ring):
+            n = (step + 1) % ring
+            there = lax.rem(here + n, ring)
+            for j in range(blocks):
+                start = pl.multiple_of((j * ring + there) * width, width)
+                cut[n, j] = factor[:, pl.ds(start, width)].astype(BF16)
+            saves.append(pltpu.make_async_copy(cut.at[n], parts[n], sems.at[n]))
+            saves[-1].start()
+        total = None
         for a in range(cx):
             for b in range(cy):
-                for n, (source, place) in enumerate(((residual, held), (vectors, basis))):
-                    copy = pltpu.make_async_copy(source.at[a, b], place.at[a, b], sems.at[n, a, b])
-                    copy.start()
-                    copies_in.append(copy)
-        total, copies_out = None, []
-        for a in range(cx):
-            for b in range(cy):
-                for n in range(2):
-                    copies_in[2 * (a * cy + b) + n].wait()
-                value = held[a, b].astype(BF16)
-                cells[a, b] = value
                 part = lax.dot_general(
-                    basis[a, b], value, (((1,), (1,)), ((), ())), preferred_element_type=F32
+                    vectors[a, b], rounded[a, b], (((1,), (1,)), ((), ())), preferred_element_type=F32
                 )
                 total = part if total is None else total + part
-                copy = pltpu.make_async_copy(cells.at[a, b], rounded.at[a, b], sems.at[2, a, b])
-                copy.start()
-                copies_out.append(copy)
-        even = position()[4] == 0
-        for n, out in enumerate((near, far)):
-            row = jnp.where(even, 1 - n, n)
-            copy = pltpu.make_async_copy(cells.at[pl.ds(row, 1)], out, sems.at[3, n, 0])
-            copy.start()
-            copies_out.append(copy)
         total = jnp.where(keep_mask(count, slots, rhs), total, 0.0).astype(BF16)
         for i in range(copies):
-            sums[i] = total
-        copy = pltpu.make_async_copy(sums, spread, sems.at[0, 0, 0])
-        copy.start()
-        copy.wait()
-        for copy in copies_out:
-            copy.wait()
-
-    row = struct((1, cy, rhs, line), BF16)
-    return pl.pallas_call(
-        body,
-        out_shape=[struct(residual_field.shape, BF16), row, row, struct((copies, slots, rhs), BF16)],
-        in_specs=[SMEM, HBM, HBM],
-        out_specs=[HBM] * 4,
+            made[i] = total
+        saves.append(pltpu.make_async_copy(made, spread, sems.at[ring]))
+        saves[-1].start()
+        for save in saves:
+            save.wait()
+
+    return pl.pallas_call(
+        body,
+        out_shape=[struct((copies, slots, rhs), BF16)] + [struct((blocks, slots, width), BF16)] * ring,
+        in_specs=[SMEM, VMEM, VMEM, VMEM],
+        out_specs=[HBM] * (1 + ring),
         scratch_shapes=[
-            pltpu.VMEM(residual_field.shape, F32),
-            pltpu.VMEM(deflation.shape, deflation.dtype),
-            pltpu.VMEM(residual_field.shape, BF16),
             pltpu.VMEM((copies, slots, rhs), BF16),
-            pltpu.SemaphoreType.DMA((4, cx, cy)),
+            pltpu.VMEM((ring, blocks, slots, width), BF16),
+            pltpu.SemaphoreType.DMA((1 + ring,)),
         ],
-        compiler_params=limit(60),
-    )(counts, residual_field, deflation)
+        compiler_params=limit(6),
+    )(counts, rounded, deflation, factor)
 
 
 def halves(value):
@@ -314,117 +339,72 @@
     return high, (value - high.astype(F32)).astype(BF16)
 
 
-def cut_factor(factor, blocks, width):
-    slots = factor.shape[0]
-
-    def body(factor, *refs):
-        outs, (held, sems, out_sems) = refs[:2], refs[2:]
-        half = lax.axis_index("zl")
-        copies = []
-        for n, side in ((1, 1 - half), (0, half)):
-            for j in range(blocks):
-                start = pl.multiple_of((2 * j + side) * width, width)
-                copy = pltpu.make_async_copy(factor.at[:, pl.ds(start, width)], held.at[n, j], sems.at[n, j])
-                copy.start()
-                copies.append(copy)
-        saves = []
-        for n in (1, 0):
-            for j in range(blocks):
-                copies[(1 - n) * blocks + j].wait()
-            saves.append(pltpu.make_async_copy(held.at[n], outs[n], out_sems.at[n]))
-            saves[-1].start()
-        for save in saves:
-            save.wait()
-
-    return pl.pallas_call(
-        body,
-        out_shape=[struct((blocks, slots, width), F32)] * 2,
-        in_specs=[HBM],
-        out_specs=[HBM] * 2,
-        scratch_shapes=[
-            pltpu.VMEM((2, blocks, slots, width), F32),
-            pltpu.SemaphoreType.DMA((2, blocks)),
-            pltpu.SemaphoreType.DMA((2,)),
-        ],
-        compiler_params=limit(60),
-    )(factor)
-
-
-def lower(rows, gathered):
-    blocks, slots, width = rows[0].shape
-    count, _, rhs = gathered.shape
+def lower(rows, mine, other):
+    sets = len(rows)
+    blocks, slots, _ = rows[0].shape
+    count, _, rhs = mine.shape
     per = count // blocks
-    sets = len(rows)
 
     def body(*refs):
-        rows, (gathered, out) = refs[:sets], refs[sets:]
+        rows, (mine, other, out) = refs[:sets], refs[sets:]
         first = lax.axis_index("c") == 0
-        zero = jnp.zeros((slots, rhs), BF16)
         total = None
         for j in range(blocks):
             pieces = []
             for y in range(per):
-                mine = gathered[j * per + y]
-                pieces += [jnp.where(first, mine, zero), jnp.where(first, zero, mine)]
-            high, low = halves(jnp.concatenate([r[j] for r in rows], 0))
-            part = jnp.dot(
-                jnp.concatenate([high, low], 0), jnp.concatenate(pieces, 0), preferred_element_type=F32
-            )
+                a, b = mine[j * per + y], other[j * per + y]
+                pieces += [jnp.where(first, a, b), jnp.where(first, b, a)]
+            factor = jnp.concatenate([r[j] for r in rows], 0)
+            part = jnp.dot(factor, jnp.concatenate(pieces, 0), preferred_element_type=F32)
             total = part if total is None else total + part
         for n in range(sets):
-            out[n] = total[n * slots : (n + 1) * slots] + total[(sets + n) * slots : (sets + n + 1) * slots]
+            out[n] = total[n * slots : (n + 1) * slots]
 
     return pl.pallas_call(
         body,
         out_shape=struct((sets, slots, rhs), F32),
-        in_specs=[VMEM] * (sets + 1),
+        in_specs=[VMEM] * (sets + 2),
         out_specs=VMEM,
         compiler_params=limit(8),
-    )(*rows, gathered)
-
-
-def raise_back(rows, partials):
+    )(*rows, mine, other)
+
+
+def raise_back(rows, partial, received):
+    sets = len(rows)
     blocks, slots, width = rows[0].shape
-    rhs = partials[0].shape[2]
+    rhs = partial.shape[2]
     per = width // (2 * slots)
-    sets = len(rows)
 
     def body(*refs):
-        rows, partials, (out, made, sems) = refs[:sets], refs[sets : 2 * sets], refs[2 * sets :]
+        rows, partial, received = refs[:sets], refs[sets], refs[sets + 1 : 2 * sets]
+        mine, other = refs[2 * sets :]
         first = lax.axis_index("c") == 0
         sums = []
         for n in range(sets):
-            total = partials[0][n]
-            for m in range(1, sets):
-                total = total + partials[m][n ^ m]
+            total = partial[n]
+            for step in range(1, sets):
+                total = total + received[step - 1][(n - step) % sets]
             sums.append(total)
         lowered_high, lowered_low = halves(jnp.concatenate(sums, 0))
         over = (((0,), (0,)), ((), ()))
-        copies = []
         for j in range(blocks):
-            high, low = halves(jnp.concatenate([r[j] for r in rows], 0))
-            part = lax.dot_general(high, lowered_high, over, preferred_element_type=F32)
-            part = part + lax.dot_general(high, lowered_low, over, preferred_element_type=F32)
-            part = part + lax.dot_general(low, lowered_high, over, preferred_element_type=F32)
+            factor = jnp.concatenate([r[j] for r in rows], 0)
+            part = lax.dot_general(factor, lowered_high, over, preferred_element_type=F32)
+            part = part + lax.dot_general(factor, lowered_low, over, preferred_element_type=F32)
             for y in range(per):
                 a = part[2 * y * slots : (2 * y + 1) * slots]
                 b = part[(2 * y + 1) * slots : (2 * y + 2) * slots]
-                made[j * per + y] = jnp.where(first, a, b).astype(BF16)
-            piece = pl.ds(j * per, per)
-            copies.append(pltpu.make_async_copy(made.at[piece], out.at[piece], sems.at[j]))
-            copies[j].start()
-        for copy in copies:
-            copy.wait()
+                mine[j * per + y] = jnp.where(first, a, b)
+                other[j * per + y] = jnp.where(first, b, a).astype(BF16)
 
     shape = (blocks * per, slots, rhs)
     return pl.pallas_call(
         body,
-        out_shape=struct(shape, BF16),
+        out_shape=[struct(shape, F32), struct(shape, BF16)],
         in_specs=[VMEM] * (2 * sets),
-        out_specs=HBM,
-        scratch_shapes=[pltpu.VMEM(shape, BF16), pltpu.SemaphoreType.DMA((blocks,))],
+        out_specs=[VMEM, VMEM],
         compiler_params=limit(8),
-    )(*rows, *partials)
+    )(*rows, partial, *received)
 
 
 def leave(counts, first_level, terms_in, deflation):
@@ -480,34 +460,36 @@
 
     def body(residual_field, line_inverse, deflation, counts, coarse_factor):
         tie = lax.optimization_barrier
-        width = deflation.shape[2] * sizes["y"] * sizes["c"]
-
-        rounded, to_near, to_far, spread = enter(residual_field, deflation, counts, n_grp * sizes["y"])
+        ring = sizes["x"]
+
+        rounded, to_near, to_far = round_cells(residual_field)
         near, far = swap_pairs(to_near, GRP, n_grp, 0), swap_pairs(to_far, GRP, n_grp, 1)
-        coarse_factor, _ = tie((coarse_factor, to_near))
-        kept, away = cut_factor(coarse_factor, n_grp, width)
-        given = swap(away, "zl")
-        far, _ = tie((far, kept))
+        receivers = sizes["zh"] * sizes["zl"] * sizes["y"]
+        spread, *parts = prepare(rounded, deflation, counts, coarse_factor, receivers, ring, sizes["zh"])
+        rows = [parts[0]] + [rotate(parts[n], RING, ring, n) for n in range(1, ring)]
+        far, _ = tie((far, parts[0]))
         to_pair, to_outer, own, ends = columns(near, far, rounded)
         outer, pair = swap_outward(to_outer, n_sub), swap(to_pair, "c")
         spread, _ = tie((spread, to_outer))
         gathered = lax.all_to_all(spread, SPREAD, 0, 0)
-
-        windows = (own, ends, pair, outer)
-        to_pair, to_outer = rim_lines(windows, line_inverse)
+        outer, *rows = tie((outer, *rows))
+
+        to_pair, to_outer, own, ends = rim_lines((own, ends, pair, outer), line_inverse)
         from_outer, from_pair = swap_outward(to_outer, n_sub), swap(to_pair, "c")
-        gathered, kept, given, _ = tie((gathered, kept, given, to_outer))
-        rows = (kept, given, swap(kept, "c"), swap(given, "c"))
-        partial = lower(rows, gathered)
-        partials = (partial, swap(partial, "zl"), swap(partial, "c"), swap_across(partial))
+        gathered, _ = tie((gathered, to_outer))
+        partial = lower(rows, gathered, swap(gathered, "c"))
+        received = [rotate(partial, RING, ring, n) for n in range(1, ring)]
         own, _ = tie((own, partial))
-        inner = inner_lines((own, ends, pair, outer), line_inverse)
-        partial, own, inner = tie((partial, own, inner))
-        terms_out = raise_back(rows, (partial, *partials[1:]))
+        to_near, to_far = row_lines((own, ends, pair, outer), line_inverse, from_pair, from_outer)
+        partial, _ = tie((partial, to_near))
+        own_terms, other_terms = raise_back(rows, partial, received)
+        to_near, to_far, other_terms = tie((to_near, to_far, other_terms))
+        from_near, from_far = swap_pairs(to_near, GRP, n_grp, 0), swap_pairs(to_far, GRP, n_grp, 1)
+        own_terms, from_near = tie((own_terms, from_near))
+        terms_out = (own_terms + swap(other_terms, "c").astype(F32)).astype(BF16)
         terms_in = lax.all_to_all(terms_out, SPREAD, 0, 0)
         own, _ = tie((own, terms_out))
-        to_near, to_far = row_lines((own, ends, pair, outer), line_inverse, from_pair, from_outer)
-        from_near, from_far = swap_pairs(to_near, GRP, n_grp, 0), swap_pairs(to_far, GRP, n_grp, 1)
+        inner = inner_lines((own, ends, pair, outer), line_inverse)
         first_level = collect(inner, from_pair, from_outer, from_near, from_far)
         return leave(counts, first_level, terms_in, deflation)
 

time: 84.5 us -> 72.8 us (0.86)
  the two profiles are of different devices: /device:TPU:6 before, /device:TPU:0 now
where the time goes in v3:
time: 72.8 us; the launch traced here: 72.4 us
  starting transfers between devices  33.8 us (46%)
  Pallas kernels  17.6 us (24%)
  waiting for transfers between devices  16.2 us (22%)
  local copies, waits for them, and re-layouts  3.31 us (5%)
  between operations  0.82 us (1%)
  other arithmetic  0.73 us (1%)
    pallas_call x3, Pallas kernels, line_solve(): pl.pallas_call(body, out_shape=shapes, in_specs=[ANY if fetch else VMEM]...  11.8 us
    ppermute x6, starting transfers between devices, rotate(): lax.ppermute(value, axes, [(i, (i + step) % size) for i in range(size)])  11.2 us
    ppermute x4, starting transfers between devices, swap_pairs(): return lax.ppermute(value, axes, pairs)  6.08 us
    all_to_all x1, starting transfers between devices, body(): terms_in = lax.all_to_all(terms_out, SPREAD, 0, 0)  5.75 us
    ppermute x4, waiting for transfers between devices, swap_pairs(): return lax.ppermute(value, axes, pairs)  5.52 us
    ppermute x2, starting transfers between devices, swap_outward(): return lax.ppermute(value, SUB, pairs)  5.34 us
    all_to_all x1, starting transfers between devices, body(): gathered = lax.all_to_all(spread, SPREAD, 0, 0)  5.33 us
    all_to_all x1, waiting for transfers between devices, body(): terms_in = lax.all_to_all(terms_out, SPREAD, 0, 0)  4.8 us
  transfers between devices with their start and end apart: 18, of which 7 were waited for; matrix products, arithmetic and copies ran while one was open for 1% of the time, Pallas kernels for 19%

profile of v3, /device:TPU:0, one launch (start us, length us, event | category | flops | bytes accessed | tf_op | source)
XLA Modules:
  0.0 72.4 jit_solution(14202738074848587076)
XLA Ops:
  0.0 1.1 %copy-done.1 = f32[2,2,128,384]{3,2,1,0:T(8,128)S(1)} copy-done((f32[2,2,128,384]{3,2,1,0:T(8,128)S(1)}, f32[2,2,128,384]{3,2,1,0:T(8,128)}, u32[]{:S(2)}) %copy-start.1) | copy-done | bytes 786456
  1.2 0.7 collective-permute-start.1
  1.9 4.4 %collective-permute-start = (bf16[1,2,128,384]{3,2,1,0:T(8,128)(2,1)S(1)}, bf16[1,2,128,384]{3,2,1,0:T(8,128)(2,1)S(1)}, u32[]{:S(2)}, u32[]{:S(2)}) collective-permute-start(bf16[1,2,128,384]{3,2,1,0:T(8,128)(2,1)S(1)} %get-tuple-element.41), channel_id=1, source_target_pairs={{0,16},{16,0},{32,48},{48,32},{64,80},{80,64},{96,112},{112,96},{1... | collective-permute-start | bytes 589832 | tf_op jit(solution)/shard_map/ppermute | solution.py:49
  6.9 1.3 %copy-done = f32[48,6144]{1,0:T(8,128)S(1)} copy-done((f32[48,6144]{1,0:T(8,128)S(1)}, f32[48,6144]{1,0:T(8,128)}, u32[]{:S(2)}) %copy-start) | copy-done | bytes 1179672
  8.2 0.9 %copy-done.2 = bf16[2,2,48,384]{3,2,1,0:T(8,128)(2,1)S(1)} copy-done((bf16[2,2,48,384]{3,2,1,0:T(8,128)(2,1)S(1)}, bf16[2,2,48,384]{3,2,1,0:T(8,128)(2,1)}, u32[]{:S(2)}) %copy-start.2) | copy-done | bytes 147480
  9.1 1.6 %shard_map.56 = (bf16[16,48,128]{2,1,0:T(8,128)(2,1)}, bf16[2,48,768]{2,1,0:T(8,128)(2,1)S(1)}, bf16[2,48,768]{2,1,0:T(8,128)(2,1)}, bf16[2,48,768]{2,1,0:T(8,128)(2,1)S(1)}, bf16[2,48,768]{2,1,0:T(8,128)(2,1)S(1)}) custom-call(s32[1,1]{1,0:T(1,128)S(6)} %copy.6.count, bf16[2,2,128,384]{3,2,1,0:T(8,128)(2,1)S(1)} %get-tuple-element.43.rounded, ...), custom_call_target="tpu_custom_call" | custom-call | tf_op jit(solution)/shard_map/pallas_call | solution.py:323
  10.9 0.2 shard_map.57
  11.1 3.2 %collective-permute-start.3 = (bf16[4,1,128,384]{3,2,1,0:T(8,128)(2,1)S(1)}, bf16[4,1,128,384]{3,2,1,0:T(8,128)(2,1)S(1)}, u32[]{:S(2)}, u32[]{:S(2)}) collective-permute-start(bf16[4,1,128,384]{3,2,1,0:T(8,128)(2,1)S(1)} %get-tuple-element.49), channel_id=1, source_target_pairs={{1,2},{2,1},{3,4},{4,3},{5,6},{6,5},{7,8},{8,7},{9,10},{10,9},{11,... | collective-permute-start | bytes 1179656 | tf_op jit(solution)/shard_map/ppermute | solution.py:56
  14.3 1.2 %collective-permute-start.4 = (bf16[2,48,768]{2,1,0:T(8,128)(2,1)}, bf16[2,48,768]{2,1,0:T(8,128)(2,1)S(1)}, u32[]{:S(2)}, u32[]{:S(2)}) collective-permute-start(bf16[2,48,768]{2,1,0:T(8,128)(2,1)} %get-tuple-element.50), channel_id=1, source_target_pairs={{0,16},{16,32},{32,48},{48,0},{1,17},{17,33},{33,49},{49,1},{2,18}... | collective-permute-start | bytes 442376 | tf_op jit(solution)/shard_map/ppermute | solution.py:38
  15.5 5.4 %collective-permute-start.5 = (bf16[2,48,768]{2,1,0:T(8,128)(2,1)S(1)}, bf16[2,48,768]{2,1,0:T(8,128)(2,1)S(1)}, u32[]{:S(2)}, u32[]{:S(2)}) collective-permute-start(bf16[2,48,768]{2,1,0:T(8,128)(2,1)S(1)} %get-tuple-element.51), channel_id=1, source_target_pairs={{0,32},{16,48},{32,0},{48,16},{1,33},{17,49},{33,1},{49,17},{2,34}... | collective-permute-start | bytes 442376 | tf_op jit(solution)/shard_map/ppermute | solution.py:38
  20.9 0.2 collective-permute-start.6
  21.1 5.3 %all-to-all-start = ((bf16[16,48,128]{2,1,0:T(8,128)(2,1)}), bf16[16,48,128]{2,1,0:T(8,128)(2,1)S(1)}, u32[]{:S(2)}, u32[]{:S(2)}) async-start(bf16[16,48,128]{2,1,0:T(8,128)(2,1)} %get-tuple-element.60), calls=%async_computation | async-start | bytes 393216 | tf_op jit(solution)/shard_map/all_to_all | solution.py:474
  26.4 2.1 %collective-permute-done.5.refs_2_ = bf16[2,48,768]{2,1,0:T(8,128)(2,1)S(1)} collective-permute-done((bf16[2,48,768]{2,1,0:T(8,128)(2,1)S(1)}, bf16[2,48,768]{2,1,0:T(8,128)(2,1)S(1)}, u32[]{:S(2)}, u32[]{:S(2)}) %collective-permute-start.5) | collective-permute-done | bytes 147488 | tf_op jit(solution)/shard_map/ppermute | solution.py:38
  28.5 5.5 %shard_map.58 = (bf16[4,1,128,384]{3,2,1,0:T(8,128)(2,1)}, bf16[4,1,128,384]{3,2,1,0:T(8,128)(2,1)}, bf16[2,2,128,384]{3,2,1,0:T(8,128)(2,1)S(1)}, bf16[2,2,128,384]{3,2,1,0:T(8,128)(2,1)S(1)}) custom-call(bf16[2,2,128,384]{3,2,1,0:T(8,128)(2,1)S(1)} %get-tuple-element.46.refs_0_, bf16[2,2,128,384]{3,2,1,0:T(8,128)(2,1)S(1)} %get-tuple-element.47.refs_1_, ...), custom_call_target="tpu_custom_call" | custom-call | flops 1056964608 | bytes 8257536 | tf_op jit(solution)/shard_map/pallas_call | solution.py:143
  34.2 2.1 %collective-permute-start.9 = (bf16[4,1,128,384]{3,2,1,0:T(8,128)(2,1)}, bf16[4,1,128,384]{3,2,1,0:T(8,128)(2,1)S(1)}, u32[]{:S(2)}, u32[]{:S(2)}) collective-permute-start(bf16[4,1,128,384]{3,2,1,0:T(8,128)(2,1)} %get-tuple-element.61), channel_id=1, source_target_pairs={{1,2},{2,1},{3,4},{4,3},{5,6},{6,5},{7,8},{8,7},{9,10},{10,9},{11,... | collective-permute-start | bytes 1179656 | tf_op jit(solution)/shard_map/ppermute | solution.py:56
  36.3 1.4 %collective-permute-done.7.refs_5_ = bf16[16,48,128]{2,1,0:T(8,128)(2,1)S(1)} collective-permute-done((bf16[16,48,128]{2,1,0:T(8,128)(2,1)S(1)}, bf16[16,48,128]{2,1,0:T(8,128)(2,1)S(1)}, u32[]{:S(2)}, u32[]{:S(2)}) %collective-permute-start.7) | collective-permute-done | bytes 196640 | tf_op jit(solution)/shard_map/ppermute | solution.py:42
  37.7 0.3 shard_map.59.refs_4_
  38.0 1.4 %collective-permute-start.12 = (f32[4,48,128]{2,1,0:T(8,128)S(1)}, f32[4,48,128]{2,1,0:T(8,128)S(1)}, u32[]{:S(2)}, u32[]{:S(2)}) collective-permute-start(f32[4,48,128]{2,1,0:T(8,128)S(1)} %shard_map.59.refs_4_), channel_id=1, source_target_pairs={{0,48},{16,0},{32,16},{48,32},{1,49},{17,1},{33,17},{49,33},{2,50}... | collective-permute-start | bytes 294920 | tf_op jit(solution)/shard_map/ppermute | solution.py:38
  39.5 1.6 %collective-permute-start.11 = (f32[4,48,128]{2,1,0:T(8,128)S(1)}, f32[4,48,128]{2,1,0:T(8,128)S(1)}, u32[]{:S(2)}, u32[]{:S(2)}) collective-permute-start(f32[4,48,128]{2,1,0:T(8,128)S(1)} %shard_map.59.refs_4_), channel_id=1, source_target_pairs={{0,32},{16,48},{32,0},{48,16},{1,33},{17,49},{33,1},{49,17},{2,34}... | collective-permute-start | bytes 294920 | tf_op jit(solution)/shard_map/ppermute | solution.py:38
  41.1 1.3 %collective-permute-start.10 = (f32[4,48,128]{2,1,0:T(8,128)S(1)}, f32[4,48,128]{2,1,0:T(8,128)S(1)}, u32[]{:S(2)}, u32[]{:S(2)}) collective-permute-start(f32[4,48,128]{2,1,0:T(8,128)S(1)} %shard_map.59.refs_4_), channel_id=1, source_target_pairs={{0,16},{16,32},{32,48},{48,0},{1,17},{17,33},{33,49},{49,1},{2,18}... | collective-permute-start | bytes 294920 | tf_op jit(solution)/shard_map/ppermute | solution.py:38
  42.4 1.3 %collective-permute-done.9.refs_6_.from_outer = bf16[4,1,128,384]{3,2,1,0:T(8,128)(2,1)S(1)} collective-permute-done((bf16[4,1,128,384]{3,2,1,0:T(8,128)(2,1)}, bf16[4,1,128,384]{3,2,1,0:T(8,128)(2,1)S(1)}, u32[]{:S(2)}, u32[]{:S(2)}) %collective-permute-start.9) | collective-permute-done | bytes 393248 | tf_op jit(solution)/shard_map/ppermute | solution.py:56
  43.8 3.0 %shard_map.60 = (bf16[1,2,128,384]{3,2,1,0:T(8,128)(2,1)S(1)}, bf16[1,2,128,384]{3,2,1,0:T(8,128)(2,1)S(1)}) custom-call(bf16[2,2,128,384]{3,2,1,0:T(8,128)(2,1)S(1)} %get-tuple-element.74.refs_0_, bf16[2,2,128,384]{3,2,1,0:T(8,128)(2,1)S(1)} %get-tuple-element.64.refs_1_, bf16[4,1,128,384]{3,2,1,0:T(8,128)(2,1)S(1)} %collective-permute-done.2.refs_2_, ...), custom_call_target="tpu_custom_call" | custom-call | flops 603979776 | bytes 4718592 | tf_op jit(solution)/shard_map/pallas_call | solution.py:143
  46.7 1.1 %collective-permute-done.10.refs_5_ = f32[4,48,128]{2,1,0:T(8,128)S(1)} collective-permute-done((f32[4,48,128]{2,1,0:T(8,128)S(1)}, f32[4,48,128]{2,1,0:T(8,128)S(1)}, u32[]{:S(2)}, u32[]{:S(2)}) %collective-permute-start.10) | collective-permute-done | bytes 98336 | tf_op jit(solution)/shard_map/ppermute | solution.py:38
  47.8 0.6 shard_map.61
  48.4 0.4 collective-permute-start.13
  48.8 0.7 collective-permute-start.15
  49.5 5.4 %collective-permute-done.13.from_near = bf16[1,2,128,384]{3,2,1,0:T(8,128)(2,1)S(1)} collective-permute-done((bf16[1,2,128,384]{3,2,1,0:T(8,128)(2,1)S(1)}, bf16[1,2,128,384]{3,2,1,0:T(8,128)(2,1)S(1)}, u32[]{:S(2)}, u32[]{:S(2)}) %collective-permute-start.13) | collective-permute-done | bytes 196640 | tf_op jit(solution)/shard_map/ppermute | solution.py:49
  54.9 0.7 %add_convert_fusion = bf16[16,48,128]{2,1,0:T(8,128)(2,1)} fusion(f32[16,48,128]{2,1,0:T(8,128)S(1)} %get-tuple-element.72, bf16[16,48,128]{2,1,0:T(8,128)(2,1)S(1)} %collective-permute-done.14), kind=kLoop, calls=%fused_computation | loop fusion | flops 294912 | bytes 786432 | tf_op jit(solution)/shard_map/convert_element_type | solution.py:489
  55.6 5.8 %all-to-all-start.1 = ((bf16[16,48,128]{2,1,0:T(8,128)(2,1)}), bf16[16,48,128]{2,1,0:T(8,128)(2,1)S(1)}, u32[]{:S(2)}, u32[]{:S(2)}) async-start(bf16[16,48,128]{2,1,0:T(8,128)(2,1)} %add_convert_fusion), calls=%async_computation.1 | async-start | bytes 393216 | tf_op jit(solution)/shard_map/all_to_all | solution.py:490
  61.4 3.3 %shard_map.62.inner = f32[2,2,128,384]{3,2,1,0:T(8,128)S(1)} custom-call(bf16[2,2,128,384]{3,2,1,0:T(8,128)(2,1)S(1)} %get-tuple-element.74.refs_0_, bf16[2,2,128,384]{3,2,1,0:T(8,128)(2,1)S(1)} %get-tuple-element.64.refs_1_, bf16[4,1,128,384]{3,2,1,0:T(8,128)(2,1)S(1)} %collective-permute-done.2.refs_2_, ...), custom_call_target="tpu_custom_call" | custom-call | flops 754974720 | bytes 5898240 | tf_op jit(solution)/shard_map/pallas_call | solution.py:143
  64.9 4.8 %all-to-all-done.1.terms_in = bf16[16,48,128]{2,1,0:T(8,128)(2,1)S(1)} async-done(((bf16[16,48,128]{2,1,0:T(8,128)(2,1)}), bf16[16,48,128]{2,1,0:T(8,128)(2,1)S(1)}, u32[]{:S(2)}, u32[]{:S(2)}) %all-to-all-start.1) | async-done | bytes 196640 | tf_op jit(solution)/shard_map/all_to_all | solution.py:490
  69.7 2.7 %shard_map.64 = f32[2,2,128,384]{3,2,1,0:T(8,128)} custom-call(s32[1,1]{1,0:T(1,128)S(6)} %copy.6.count, f32[2,2,128,384]{3,2,1,0:T(8,128)S(1)} %shard_map.63.first_level, bf16[16,48,128]{2,1,0:T(8,128)(2,1)S(1)} %all-to-all-done.1.terms_in, bf16[2,2,48,384]{3,2,1,0:T(8,128)(2,1)S(1)} %copy-done.3), custom_call_target="tpu_custom_call" | custom-call | tf_op jit(solution)/shard_map/pallas_call | solution.py:441
  (23 shorter events, 0.5 us)
Async XLA Ops:
  0.0 1.1 %copy-start.1 = (f32[2,2,128,384]{3,2,1,0:T(8,128)S(1)}, f32[2,2,128,384]{3,2,1,0:T(8,128)}, u32[]{:S(2)}) copy-start(f32[2,2,128,384]{3,2,1,0:T(8,128)} %residual.1) | copy-start | bytes 2359300
  1.2 9.6 %collective-permute-start.1 = (bf16[1,2,128,384]{3,2,1,0:T(8,128)(2,1)S(1)}, bf16[1,2,128,384]{3,2,1,0:T(8,128)(2,1)S(1)}, u32[]{:S(2)}, u32[]{:S(2)}) collective-permute-start(bf16[1,2,128,384]{3,2,1,0:T(8,128)(2,1)S(1)} %get-tuple-element.42), channel_id=1, source_target_pairs={{16,32},{32,16},{48,64},{64,48},{80,96},{96,80},{17,33},{33,17},{4... | collective-permute-start | bytes 589832 | tf_op jit(solution)/shard_map/ppermute | solution.py:49
  1.9 9.0 %collective-permute-start = (bf16[1,2,128,384]{3,2,1,0:T(8,128)(2,1)S(1)}, bf16[1,2,128,384]{3,2,1,0:T(8,128)(2,1)S(1)}, u32[]{:S(2)}, u32[]{:S(2)}) collective-permute-start(bf16[1,2,128,384]{3,2,1,0:T(8,128)(2,1)S(1)} %get-tuple-element.41), channel_id=1, source_target_pairs={{0,16},{16,0},{32,48},{48,32},{64,80},{80,64},{96,112},{112,96},{1... | collective-permute-start | bytes 589832 | tf_op jit(solution)/shard_map/ppermute | solution.py:49
  6.9 1.3 %copy-start = (f32[48,6144]{1,0:T(8,128)S(1)}, f32[48,6144]{1,0:T(8,128)}, u32[]{:S(2)}) copy-start(f32[48,6144]{1,0:T(8,128)} %factor.1) | copy-start | bytes 3538948
  8.2 0.9 %copy-start.2 = (bf16[2,2,48,384]{3,2,1,0:T(8,128)(2,1)S(1)}, bf16[2,2,48,384]{3,2,1,0:T(8,128)(2,1)}, u32[]{:S(2)}) copy-start(bf16[2,2,48,384]{3,2,1,0:T(8,128)(2,1)} %vectors.3) | copy-start | bytes 442372
  11.1 17.4 %collective-permute-start.3 = (bf16[4,1,128,384]{3,2,1,0:T(8,128)(2,1)S(1)}, bf16[4,1,128,384]{3,2,1,0:T(8,128)(2,1)S(1)}, u32[]{:S(2)}, u32[]{:S(2)}) collective-permute-start(bf16[4,1,128,384]{3,2,1,0:T(8,128)(2,1)S(1)} %get-tuple-element.49), channel_id=1, source_target_pairs={{1,2},{2,1},{3,4},{4,3},{5,6},{6,5},{7,8},{8,7},{9,10},{10,9},{11,... | collective-permute-start | bytes 1179656 | tf_op jit(solution)/shard_map/ppermute | solution.py:56
  14.3 14.2 %collective-permute-start.2 = (bf16[4,1,128,384]{3,2,1,0:T(8,128)(2,1)S(1)}, bf16[4,1,128,384]{3,2,1,0:T(8,128)(2,1)S(1)}, u32[]{:S(2)}, u32[]{:S(2)}) collective-permute-start(bf16[4,1,128,384]{3,2,1,0:T(8,128)(2,1)S(1)} %get-tuple-element.48), channel_id=1, source_target_pairs={{0,1},{1,0},{2,3},{3,2},{4,5},{5,4},{6,7},{7,6},{8,9},{9,8},{10,11... | collective-permute-start | bytes 1179656 | tf_op jit(solution)/shard_map/ppermute | solution.py:42
  14.3 12.1 %collective-permute-start.4 = (bf16[2,48,768]{2,1,0:T(8,128)(2,1)}, bf16[2,48,768]{2,1,0:T(8,128)(2,1)S(1)}, u32[]{:S(2)}, u32[]{:S(2)}) collective-permute-start(bf16[2,48,768]{2,1,0:T(8,128)(2,1)} %get-tuple-element.50), channel_id=1, source_target_pairs={{0,16},{16,32},{32,48},{48,0},{1,17},{17,33},{33,49},{49,1},{2,18}... | collective-permute-start | bytes 442376 | tf_op jit(solution)/shard_map/ppermute | solution.py:38
  15.5 13.0 %collective-permute-start.5 = (bf16[2,48,768]{2,1,0:T(8,128)(2,1)S(1)}, bf16[2,48,768]{2,1,0:T(8,128)(2,1)S(1)}, u32[]{:S(2)}, u32[]{:S(2)}) collective-permute-start(bf16[2,48,768]{2,1,0:T(8,128)(2,1)S(1)} %get-tuple-element.51), channel_id=1, source_target_pairs={{0,32},{16,48},{32,0},{48,16},{1,33},{17,49},{33,1},{49,17},{2,34}... | collective-permute-start | bytes 442376 | tf_op jit(solution)/shard_map/ppermute | solution.py:38
  20.9 7.6 %collective-permute-start.6 = (bf16[2,48,768]{2,1,0:T(8,128)(2,1)S(1)}, bf16[2,48,768]{2,1,0:T(8,128)(2,1)S(1)}, u32[]{:S(2)}, u32[]{:S(2)}) collective-permute-start(bf16[2,48,768]{2,1,0:T(8,128)(2,1)S(1)} %get-tuple-element.52), channel_id=1, source_target_pairs={{0,48},{16,0},{32,16},{48,32},{1,49},{17,1},{33,17},{49,33},{2,50}... | collective-permute-start | bytes 442376 | tf_op jit(solution)/shard_map/ppermute | solution.py:38
  21.1 15.2 %all-to-all-start = ((bf16[16,48,128]{2,1,0:T(8,128)(2,1)}), bf16[16,48,128]{2,1,0:T(8,128)(2,1)S(1)}, u32[]{:S(2)}, u32[]{:S(2)}) async-start(bf16[16,48,128]{2,1,0:T(8,128)(2,1)} %get-tuple-element.60), calls=%async_computation | async-start | bytes 393216 | tf_op jit(solution)/shard_map/all_to_all | solution.py:474
  34.1 8.4 %collective-permute-start.8 = (bf16[4,1,128,384]{3,2,1,0:T(8,128)(2,1)}, bf16[4,1,128,384]{3,2,1,0:T(8,128)(2,1)S(1)}, u32[]{:S(2)}, u32[]{:S(2)}) collective-permute-start(bf16[4,1,128,384]{3,2,1,0:T(8,128)(2,1)} %get-tuple-element.65), channel_id=1, source_target_pairs={{0,1},{1,0},{2,3},{3,2},{4,5},{5,4},{6,7},{7,6},{8,9},{9,8},{10,11... | collective-permute-start | bytes 1179656 | tf_op jit(solution)/shard_map/ppermute | solution.py:42
  34.2 9.6 %collective-permute-start.9 = (bf16[4,1,128,384]{3,2,1,0:T(8,128)(2,1)}, bf16[4,1,128,384]{3,2,1,0:T(8,128)(2,1)S(1)}, u32[]{:S(2)}, u32[]{:S(2)}) collective-permute-start(bf16[4,1,128,384]{3,2,1,0:T(8,128)(2,1)} %get-tuple-element.61), channel_id=1, source_target_pairs={{1,2},{2,1},{3,4},{4,3},{5,6},{6,5},{7,8},{8,7},{9,10},{10,9},{11,... | collective-permute-start | bytes 1179656 | tf_op jit(solution)/shard_map/ppermute | solution.py:56
  36.3 1.4 %collective-permute-start.7 = (bf16[16,48,128]{2,1,0:T(8,128)(2,1)S(1)}, bf16[16,48,128]{2,1,0:T(8,128)(2,1)S(1)}, u32[]{:S(2)}, u32[]{:S(2)}) collective-permute-start(bf16[16,48,128]{2,1,0:T(8,128)(2,1)S(1)} %all-to-all-done.refs_4_), channel_id=1, source_target_pairs={{0,1},{1,0},{2,3},{3,2},{4,5},{5,4},{6,7},{7,6},{8,9},{9,8},{10,11... | collective-permute-start | bytes 589832 | tf_op jit(solution)/shard_map/ppermute | solution.py:42
  38.0 8.7 %collective-permute-start.12 = (f32[4,48,128]{2,1,0:T(8,128)S(1)}, f32[4,48,128]{2,1,0:T(8,128)S(1)}, u32[]{:S(2)}, u32[]{:S(2)}) collective-permute-start(f32[4,48,128]{2,1,0:T(8,128)S(1)} %shard_map.59.refs_4_), channel_id=1, source_target_pairs={{0,48},{16,0},{32,16},{48,32},{1,49},{17,1},{33,17},{49,33},{2,50}... | collective-permute-start | bytes 294920 | tf_op jit(solution)/shard_map/ppermute | solution.py:38
  39.5 7.3 %collective-permute-start.11 = (f32[4,48,128]{2,1,0:T(8,128)S(1)}, f32[4,48,128]{2,1,0:T(8,128)S(1)}, u32[]{:S(2)}, u32[]{:S(2)}) collective-permute-start(f32[4,48,128]{2,1,0:T(8,128)S(1)} %shard_map.59.refs_4_), channel_id=1, source_target_pairs={{0,32},{16,48},{32,0},{48,16},{1,33},{17,49},{33,1},{49,17},{2,34}... | collective-permute-start | bytes 294920 | tf_op jit(solution)/shard_map/ppermute | solution.py:38
  41.1 6.7 %collective-permute-start.10 = (f32[4,48,128]{2,1,0:T(8,128)S(1)}, f32[4,48,128]{2,1,0:T(8,128)S(1)}, u32[]{:S(2)}, u32[]{:S(2)}) collective-permute-start(f32[4,48,128]{2,1,0:T(8,128)S(1)} %shard_map.59.refs_4_), channel_id=1, source_target_pairs={{0,16},{16,32},{32,48},{48,0},{1,17},{17,33},{33,49},{49,1},{2,18}... | collective-permute-start | bytes 294920 | tf_op jit(solution)/shard_map/ppermute | solution.py:38
  43.8 26.0 %copy-start.3 = (bf16[2,2,48,384]{3,2,1,0:T(8,128)(2,1)S(1)}, bf16[2,2,48,384]{3,2,1,0:T(8,128)(2,1)}, u32[]{:S(2)}) copy-start(bf16[2,2,48,384]{3,2,1,0:T(8,128)(2,1)} %vectors.3) | copy-start | bytes 442372
  48.4 6.4 %collective-permute-start.13 = (bf16[1,2,128,384]{3,2,1,0:T(8,128)(2,1)S(1)}, bf16[1,2,128,384]{3,2,1,0:T(8,128)(2,1)S(1)}, u32[]{:S(2)}, u32[]{:S(2)}) collective-permute-start(bf16[1,2,128,384]{3,2,1,0:T(8,128)(2,1)S(1)} %get-tuple-element.71), channel_id=1, source_target_pairs={{0,16},{16,0},{32,48},{48,32},{64,80},{80,64},{96,112},{112,96},{1... | collective-permute-start | bytes 589832 | tf_op jit(solution)/shard_map/ppermute | solution.py:49
  48.8 6.1 %collective-permute-start.14 = (bf16[16,48,128]{2,1,0:T(8,128)(2,1)S(1)}, bf16[16,48,128]{2,1,0:T(8,128)(2,1)S(1)}, u32[]{:S(2)}, u32[]{:S(2)}) collective-permute-start(bf16[16,48,128]{2,1,0:T(8,128)(2,1)S(1)} %get-tuple-element.73), channel_id=1, source_target_pairs={{0,1},{1,0},{2,3},{3,2},{4,5},{5,4},{6,7},{7,6},{8,9},{9,8},{10,11... | collective-permute-start | bytes 589832 | tf_op jit(solution)/shard_map/ppermute | solution.py:42
  48.8 15.9 %collective-permute-start.15 = (bf16[1,2,128,384]{3,2,1,0:T(8,128)(2,1)S(1)}, bf16[1,2,128,384]{3,2,1,0:T(8,128)(2,1)S(1)}, u32[]{:S(2)}, u32[]{:S(2)}) collective-permute-start(bf16[1,2,128,384]{3,2,1,0:T(8,128)(2,1)S(1)} %get-tuple-element.76), channel_id=1, source_target_pairs={{16,32},{32,16},{48,64},{64,48},{80,96},{96,80},{17,33},{33,17},{4... | collective-permute-start | bytes 589832 | tf_op jit(solution)/shard_map/ppermute | solution.py:49
  55.6 14.1 %all-to-all-start.1 = ((bf16[16,48,128]{2,1,0:T(8,128)(2,1)}), bf16[16,48,128]{2,1,0:T(8,128)(2,1)S(1)}, u32[]{:S(2)}, u32[]{:S(2)}) async-start(bf16[16,48,128]{2,1,0:T(8,128)(2,1)} %add_convert_fusion), calls=%async_computation.1 | async-start | bytes 393216 | tf_op jit(solution)/shard_map/all_to_all | solution.py:490

commit v4 on v3

--- a/solution.py
+++ b/solution.py
@@ -103,14 +103,15 @@
                 slot, run = slot + run, 0
         plan.append((start, copies, found))
 
-    if fetch:
-        for load in loads:
-            load.wait()
     first = at[0] == 0
     for a in range(WIDE):
         near, far = pair[a, 0], present(at[3], outer[a, 0])
         sides[0, a] = jnp.where(first, far, near)
         sides[1, a] = jnp.where(first, near, far)
+
+    if fetch:
+        for load in loads:
+            load.wait()
 
     def window(a, b):
         if b == 0:
@@ -411,14 +412,7 @@
     cx, cy, rhs, line = first_level.shape
     slots = deflation.shape[2]
 
-    def body(count, first_level, terms_in, vectors, out, held, basis, made, sems):
-        loads = []
-        for a in range(cx):
-            for b in range(cy):
-                for n, (source, place) in enumerate(((vectors, basis), (first_level, held))):
-                    copy = pltpu.make_async_copy(source.at[a, b], place.at[a, b], sems.at[n, a, b])
-                    copy.start()
-                    loads.append(copy)
+    def body(count, first_level, terms_in, vectors, out, made, sems):
         total = terms_in[0].astype(F32)
         for i in range(1, terms_in.shape[0]):
             total = total + terms_in[i].astype(F32)
@@ -426,30 +420,22 @@
         saves = []
         for a in range(cx):
             for b in range(cy):
-                for n in range(2):
-                    loads[2 * (a * cy + b) + n].wait()
                 value = lax.dot_general(
-                    solved, basis[a, b], (((0,), (0,)), ((), ())), preferred_element_type=F32
+                    solved, vectors[a, b], (((0,), (0,)), ((), ())), preferred_element_type=F32
                 )
-                made[a, b] = value + held[a, b]
-                copy = pltpu.make_async_copy(made.at[a, b], out.at[a, b], sems.at[2, a, b])
-                copy.start()
-                saves.append(copy)
-        for copy in saves:
-            copy.wait()
+                made[a, b] = value + first_level[a, b]
+                saves.append(pltpu.make_async_copy(made.at[a, b], out.at[a, b], sems.at[a, b]))
+                saves[-1].start()
+        for save in saves:
+            save.wait()
 
     return pl.pallas_call(
         body,
         out_shape=struct(first_level.shape, F32),
-        in_specs=[SMEM, HBM, VMEM, HBM],
+        in_specs=[SMEM, VMEM, VMEM, VMEM],
         out_specs=HBM,
-        scratch_shapes=[
-            pltpu.VMEM(first_level.shape, F32),
-            pltpu.VMEM(deflation.shape, deflation.dtype),
-            pltpu.VMEM(first_level.shape, F32),
-            pltpu.SemaphoreType.DMA((3, cx, cy)),
-        ],
-        compiler_params=limit(40),
+        scratch_shapes=[pltpu.VMEM(first_level.shape, F32), pltpu.SemaphoreType.DMA((cx, cy))],
+        compiler_params=limit(6),
     )(counts, first_level, terms_in, deflation)
 
 
@@ -485,7 +471,6 @@
         own_terms, other_terms = raise_back(rows, partial, received)
         to_near, to_far, other_terms = tie((to_near, to_far, other_terms))
         from_near, from_far = swap_pairs(to_near, GRP, n_grp, 0), swap_pairs(to_far, GRP, n_grp, 1)
-        own_terms, from_near = tie((own_terms, from_near))
         terms_out = (own_terms + swap(other_terms, "c").astype(F32)).astype(BF16)
         terms_in = lax.all_to_all(terms_out, SPREAD, 0, 0)
         own, _ = tie((own, terms_out))

time: 72.8 us -> 70.1 us (0.963)
  waiting for transfers between devices: 16.2 us -> 10.5 us
  starting transfers between devices: 33.8 us -> 37.6 us
  Pallas kernels: 17.6 us -> 16.7 us
    ppermute x4, waiting for transfers between devices: 5.52 us -> 0.13 us  [swap_pairs(): return lax.ppermute(value, axes, pairs)]
    all_to_all x1, starting transfers between devices: 5.75 us -> 9.5 us  [body(): terms_in = lax.all_to_all(terms_out, SPREAD, 0, 0)]
    pallas_call x1, Pallas kernels: 2.7 us -> 1.15 us  [leave(): pl.pallas_call(body, out_shape=struct(first_level.shape, F32), in_specs=[...]
  transfers between devices with their start and end apart: 18 -> 18, of which waited for: 7 -> 7; matrix products, arithmetic and copies ran while one was open for 1% -> 1% of each run, Pallas kernels for 19% -> 21%
where the time goes in v4:
time: 70.1 us; the launch traced here: 69.7 us
  starting transfers between devices  37.6 us (54%)
  Pallas kernels  16.7 us (24%)
  waiting for transfers between devices  10.5 us (15%)
  local copies, waits for them, and re-layouts  3.31 us (5%)
  between operations  0.83 us (1%)
  other arithmetic  0.73 us (1%)
    pallas_call x3, Pallas kernels, line_solve(): pl.pallas_call(body, out_shape=shapes, in_specs=[ANY if fetch else VMEM]...  12.5 us
    ppermute x6, starting transfers between devices, rotate(): lax.ppermute(value, axes, [(i, (i + step) % size) for i in range(size)])  11.2 us
    all_to_all x1, starting transfers between devices, body(): terms_in = lax.all_to_all(terms_out, SPREAD, 0, 0)  9.5 us
    ppermute x4, starting transfers between devices, swap_pairs(): return lax.ppermute(value, axes, pairs)  6.08 us
    ppermute x2, starting transfers between devices, swap_outward(): return lax.ppermute(value, SUB, pairs)  5.34 us
    all_to_all x1, starting transfers between devices, body(): gathered = lax.all_to_all(spread, SPREAD, 0, 0)  5.33 us
    all_to_all x1, waiting for transfers between devices, body(): terms_in = lax.all_to_all(terms_out, SPREAD, 0, 0)  4.79 us
    unnamed x8, local copies, waits for them, and re-layouts  3.31 us
  transfers between devices with their start and end apart: 18, of which 7 were waited for; matrix products, arithmetic and copies ran while one was open for 1% of the time, Pallas kernels for 21%

profile of v4, /device:TPU:0, one launch (start us, length us, event | category | flops | bytes accessed | tf_op | source)
XLA Modules:
  0.0 69.7 jit_solution(13597986757975660393)
XLA Ops:
  0.0 1.1 %copy-done.1 = f32[2,2,128,384]{3,2,1,0:T(8,128)S(1)} copy-done((f32[2,2,128,384]{3,2,1,0:T(8,128)S(1)}, f32[2,2,128,384]{3,2,1,0:T(8,128)}, u32[]{:S(2)}) %copy-start.1) | copy-done | bytes 786456
  1.2 0.7 collective-permute-start.1
  1.9 4.4 %collective-permute-start = (bf16[1,2,128,384]{3,2,1,0:T(8,128)(2,1)S(1)}, bf16[1,2,128,384]{3,2,1,0:T(8,128)(2,1)S(1)}, u32[]{:S(2)}, u32[]{:S(2)}) collective-permute-start(bf16[1,2,128,384]{3,2,1,0:T(8,128)(2,1)S(1)} %get-tuple-element.39), channel_id=1, source_target_pairs={{0,16},{16,0},{32,48},{48,32},{64,80},{80,64},{96,112},{112,96},{1... | collective-permute-start | bytes 589832 | tf_op jit(solution)/shard_map/ppermute | solution.py:49
  6.9 1.3 %copy-done = f32[48,6144]{1,0:T(8,128)S(1)} copy-done((f32[48,6144]{1,0:T(8,128)S(1)}, f32[48,6144]{1,0:T(8,128)}, u32[]{:S(2)}) %copy-start) | copy-done | bytes 1179672
  8.2 0.9 %copy-done.2 = bf16[2,2,48,384]{3,2,1,0:T(8,128)(2,1)S(1)} copy-done((bf16[2,2,48,384]{3,2,1,0:T(8,128)(2,1)S(1)}, bf16[2,2,48,384]{3,2,1,0:T(8,128)(2,1)}, u32[]{:S(2)}) %copy-start.2) | copy-done | bytes 147480
  9.1 1.6 %shard_map.56 = (bf16[16,48,128]{2,1,0:T(8,128)(2,1)}, bf16[2,48,768]{2,1,0:T(8,128)(2,1)S(1)}, bf16[2,48,768]{2,1,0:T(8,128)(2,1)}, bf16[2,48,768]{2,1,0:T(8,128)(2,1)S(1)}, bf16[2,48,768]{2,1,0:T(8,128)(2,1)S(1)}) custom-call(s32[1,1]{1,0:T(1,128)S(6)} %copy.6.count, bf16[2,2,128,384]{3,2,1,0:T(8,128)(2,1)S(1)} %get-tuple-element.41.rounded, ...), custom_call_target="tpu_custom_call" | custom-call | tf_op jit(solution)/shard_map/pallas_call | solution.py:324
  10.9 0.2 shard_map.57
  11.1 3.2 %collective-permute-start.3 = (bf16[4,1,128,384]{3,2,1,0:T(8,128)(2,1)S(1)}, bf16[4,1,128,384]{3,2,1,0:T(8,128)(2,1)S(1)}, u32[]{:S(2)}, u32[]{:S(2)}) collective-permute-start(bf16[4,1,128,384]{3,2,1,0:T(8,128)(2,1)S(1)} %get-tuple-element.47), channel_id=1, source_target_pairs={{1,2},{2,1},{3,4},{4,3},{5,6},{6,5},{7,8},{8,7},{9,10},{10,9},{11,... | collective-permute-start | bytes 1179656 | tf_op jit(solution)/shard_map/ppermute | solution.py:56
  14.3 1.2 %collective-permute-start.4 = (bf16[2,48,768]{2,1,0:T(8,128)(2,1)}, bf16[2,48,768]{2,1,0:T(8,128)(2,1)S(1)}, u32[]{:S(2)}, u32[]{:S(2)}) collective-permute-start(bf16[2,48,768]{2,1,0:T(8,128)(2,1)} %get-tuple-element.48), channel_id=1, source_target_pairs={{0,16},{16,32},{32,48},{48,0},{1,17},{17,33},{33,49},{49,1},{2,18}... | collective-permute-start | bytes 442376 | tf_op jit(solution)/shard_map/ppermute | solution.py:38
  15.5 5.4 %collective-permute-start.5 = (bf16[2,48,768]{2,1,0:T(8,128)(2,1)S(1)}, bf16[2,48,768]{2,1,0:T(8,128)(2,1)S(1)}, u32[]{:S(2)}, u32[]{:S(2)}) collective-permute-start(bf16[2,48,768]{2,1,0:T(8,128)(2,1)S(1)} %get-tuple-element.49), channel_id=1, source_target_pairs={{0,32},{16,48},{32,0},{48,16},{1,33},{17,49},{33,1},{49,17},{2,34}... | collective-permute-start | bytes 442376 | tf_op jit(solution)/shard_map/ppermute | solution.py:38
  20.9 0.2 collective-permute-start.6
  21.1 5.3 %all-to-all-start = ((bf16[16,48,128]{2,1,0:T(8,128)(2,1)}), bf16[16,48,128]{2,1,0:T(8,128)(2,1)S(1)}, u32[]{:S(2)}, u32[]{:S(2)}) async-start(bf16[16,48,128]{2,1,0:T(8,128)(2,1)} %get-tuple-element.58), calls=%async_computation | async-start | bytes 393216 | tf_op jit(solution)/shard_map/all_to_all | solution.py:460
  26.4 2.1 %collective-permute-done.5.refs_2_ = bf16[2,48,768]{2,1,0:T(8,128)(2,1)S(1)} collective-permute-done((bf16[2,48,768]{2,1,0:T(8,128)(2,1)S(1)}, bf16[2,48,768]{2,1,0:T(8,128)(2,1)S(1)}, u32[]{:S(2)}, u32[]{:S(2)}) %collective-permute-start.5) | collective-permute-done | bytes 147488 | tf_op jit(solution)/shard_map/ppermute | solution.py:38
  28.5 5.5 %shard_map.58 = (bf16[4,1,128,384]{3,2,1,0:T(8,128)(2,1)}, bf16[4,1,128,384]{3,2,1,0:T(8,128)(2,1)}, bf16[2,2,128,384]{3,2,1,0:T(8,128)(2,1)S(1)}, bf16[2,2,128,384]{3,2,1,0:T(8,128)(2,1)S(1)}) custom-call(bf16[2,2,128,384]{3,2,1,0:T(8,128)(2,1)S(1)} %get-tuple-element.44.refs_0_, bf16[2,2,128,384]{3,2,1,0:T(8,128)(2,1)S(1)} %get-tuple-element.45.refs_1_, ...), custom_call_target="tpu_custom_call" | custom-call | flops 1056964608 | bytes 8257536 | tf_op jit(solution)/shard_map/pallas_call | solution.py:144
  34.2 2.1 %collective-permute-start.9 = (bf16[4,1,128,384]{3,2,1,0:T(8,128)(2,1)}, bf16[4,1,128,384]{3,2,1,0:T(8,128)(2,1)S(1)}, u32[]{:S(2)}, u32[]{:S(2)}) collective-permute-start(bf16[4,1,128,384]{3,2,1,0:T(8,128)(2,1)} %get-tuple-element.59), channel_id=1, source_target_pairs={{1,2},{2,1},{3,4},{4,3},{5,6},{6,5},{7,8},{8,7},{9,10},{10,9},{11,... | collective-permute-start | bytes 1179656 | tf_op jit(solution)/shard_map/ppermute | solution.py:56
  36.3 1.4 %collective-permute-done.7.refs_5_ = bf16[16,48,128]{2,1,0:T(8,128)(2,1)S(1)} collective-permute-done((bf16[16,48,128]{2,1,0:T(8,128)(2,1)S(1)}, bf16[16,48,128]{2,1,0:T(8,128)(2,1)S(1)}, u32[]{:S(2)}, u32[]{:S(2)}) %collective-permute-start.7) | collective-permute-done | bytes 196640 | tf_op jit(solution)/shard_map/ppermute | solution.py:42
  37.7 0.3 shard_map.59.refs_4_
  38.0 1.4 %collective-permute-start.12 = (f32[4,48,128]{2,1,0:T(8,128)S(1)}, f32[4,48,128]{2,1,0:T(8,128)S(1)}, u32[]{:S(2)}, u32[]{:S(2)}) collective-permute-start(f32[4,48,128]{2,1,0:T(8,128)S(1)} %shard_map.59.refs_4_), channel_id=1, source_target_pairs={{0,48},{16,0},{32,16},{48,32},{1,49},{17,1},{33,17},{49,33},{2,50}... | collective-permute-start | bytes 294920 | tf_op jit(solution)/shard_map/ppermute | solution.py:38
  39.5 1.6 %collective-permute-start.11 = (f32[4,48,128]{2,1,0:T(8,128)S(1)}, f32[4,48,128]{2,1,0:T(8,128)S(1)}, u32[]{:S(2)}, u32[]{:S(2)}) collective-permute-start(f32[4,48,128]{2,1,0:T(8,128)S(1)} %shard_map.59.refs_4_), channel_id=1, source_target_pairs={{0,32},{16,48},{32,0},{48,16},{1,33},{17,49},{33,1},{49,17},{2,34}... | collective-permute-start | bytes 294920 | tf_op jit(solution)/shard_map/ppermute | solution.py:38
  41.1 1.3 %collective-permute-start.10 = (f32[4,48,128]{2,1,0:T(8,128)S(1)}, f32[4,48,128]{2,1,0:T(8,128)S(1)}, u32[]{:S(2)}, u32[]{:S(2)}) collective-permute-start(f32[4,48,128]{2,1,0:T(8,128)S(1)} %shard_map.59.refs_4_), channel_id=1, source_target_pairs={{0,16},{16,32},{32,48},{48,0},{1,17},{17,33},{33,49},{49,1},{2,18}... | collective-permute-start | bytes 294920 | tf_op jit(solution)/shard_map/ppermute | solution.py:38
  42.4 1.3 %collective-permute-done.9.refs_6_.from_outer = bf16[4,1,128,384]{3,2,1,0:T(8,128)(2,1)S(1)} collective-permute-done((bf16[4,1,128,384]{3,2,1,0:T(8,128)(2,1)}, bf16[4,1,128,384]{3,2,1,0:T(8,128)(2,1)S(1)}, u32[]{:S(2)}, u32[]{:S(2)}) %collective-permute-start.9) | collective-permute-done | bytes 393248 | tf_op jit(solution)/shard_map/ppermute | solution.py:56
  43.8 3.6 %shard_map.60 = (bf16[1,2,128,384]{3,2,1,0:T(8,128)(2,1)}, bf16[1,2,128,384]{3,2,1,0:T(8,128)(2,1)S(1)}) custom-call(bf16[2,2,128,384]{3,2,1,0:T(8,128)(2,1)S(1)} %get-tuple-element.70.refs_0_, bf16[2,2,128,384]{3,2,1,0:T(8,128)(2,1)S(1)} %get-tuple-element.62.refs_1_, bf16[4,1,128,384]{3,2,1,0:T(8,128)(2,1)S(1)} %collective-permute-done.2.refs_2_, ...), custom_call_target="tpu_custom_call" | custom-call | flops 603979776 | bytes 4718592 | tf_op jit(solution)/shard_map/pallas_call | solution.py:144
  47.4 0.4 collective-permute-done.10.refs_5_
  47.8 0.6 shard_map.61
  48.5 0.4 collective-permute-start.14
  48.9 0.7 collective-permute-start.15
  49.6 0.4 collective-permute-done.13
  50.0 0.7 %add_convert_fusion = bf16[16,48,128]{2,1,0:T(8,128)(2,1)} fusion(f32[16,48,128]{2,1,0:T(8,128)S(1)} %get-tuple-element.66, bf16[16,48,128]{2,1,0:T(8,128)(2,1)S(1)} %collective-permute-done.13), kind=kLoop, calls=%fused_computation | loop fusion | flops 294912 | bytes 786432 | tf_op jit(solution)/shard_map/convert_element_type | solution.py:474
  50.7 9.5 %all-to-all-start.1 = ((bf16[16,48,128]{2,1,0:T(8,128)(2,1)}), bf16[16,48,128]{2,1,0:T(8,128)(2,1)S(1)}, u32[]{:S(2)}, u32[]{:S(2)}) async-start(bf16[16,48,128]{2,1,0:T(8,128)(2,1)} %add_convert_fusion), calls=%async_computation.1 | async-start | bytes 393216 | tf_op jit(solution)/shard_map/all_to_all | solution.py:475
  60.2 3.3 %shard_map.62.inner = f32[2,2,128,384]{3,2,1,0:T(8,128)S(1)} custom-call(bf16[2,2,128,384]{3,2,1,0:T(8,128)(2,1)S(1)} %get-tuple-element.70.refs_0_, bf16[2,2,128,384]{3,2,1,0:T(8,128)(2,1)S(1)} %get-tuple-element.62.refs_1_, bf16[4,1,128,384]{3,2,1,0:T(8,128)(2,1)S(1)} %collective-permute-done.2.refs_2_, ...), custom_call_target="tpu_custom_call" | custom-call | flops 754974720 | bytes 5898240 | tf_op jit(solution)/shard_map/pallas_call | solution.py:144
  63.8 4.8 %all-to-all-done.1.terms_in = bf16[16,48,128]{2,1,0:T(8,128)(2,1)S(1)} async-done(((bf16[16,48,128]{2,1,0:T(8,128)(2,1)}), bf16[16,48,128]{2,1,0:T(8,128)(2,1)S(1)}, u32[]{:S(2)}, u32[]{:S(2)}) %all-to-all-start.1) | async-done | bytes 196640 | tf_op jit(solution)/shard_map/all_to_all | solution.py:475
  68.6 1.1 %shard_map.64 = f32[2,2,128,384]{3,2,1,0:T(8,128)} custom-call(s32[1,1]{1,0:T(1,128)S(6)} %copy.6.count, f32[2,2,128,384]{3,2,1,0:T(8,128)S(1)} %shard_map.63.first_level, bf16[16,48,128]{2,1,0:T(8,128)(2,1)S(1)} %all-to-all-done.1.terms_in, bf16[2,2,48,384]{3,2,1,0:T(8,128)(2,1)S(1)} %copy-done.3), custom_call_target="tpu_custom_call" | custom-call | tf_op jit(solution)/shard_map/pallas_call | solution.py:432
  (23 shorter events, 0.6 us)
Async XLA Ops:
  0.0 1.1 %copy-start.1 = (f32[2,2,128,384]{3,2,1,0:T(8,128)S(1)}, f32[2,2,128,384]{3,2,1,0:T(8,128)}, u32[]{:S(2)}) copy-start(f32[2,2,128,384]{3,2,1,0:T(8,128)} %residual.1) | copy-start | bytes 2359300
  1.2 9.6 %collective-permute-start.1 = (bf16[1,2,128,384]{3,2,1,0:T(8,128)(2,1)S(1)}, bf16[1,2,128,384]{3,2,1,0:T(8,128)(2,1)S(1)}, u32[]{:S(2)}, u32[]{:S(2)}) collective-permute-start(bf16[1,2,128,384]{3,2,1,0:T(8,128)(2,1)S(1)} %get-tuple-element.40), channel_id=1, source_target_pairs={{16,32},{32,16},{48,64},{64,48},{80,96},{96,80},{17,33},{33,17},{4... | collective-permute-start | bytes 589832 | tf_op jit(solution)/shard_map/ppermute | solution.py:49
  1.9 9.0 %collective-permute-start = (bf16[1,2,128,384]{3,2,1,0:T(8,128)(2,1)S(1)}, bf16[1,2,128,384]{3,2,1,0:T(8,128)(2,1)S(1)}, u32[]{:S(2)}, u32[]{:S(2)}) collective-permute-start(bf16[1,2,128,384]{3,2,1,0:T(8,128)(2,1)S(1)} %get-tuple-element.39), channel_id=1, source_target_pairs={{0,16},{16,0},{32,48},{48,32},{64,80},{80,64},{96,112},{112,96},{1... | collective-permute-start | bytes 589832 | tf_op jit(solution)/shard_map/ppermute | solution.py:49
  6.9 1.3 %copy-start = (f32[48,6144]{1,0:T(8,128)S(1)}, f32[48,6144]{1,0:T(8,128)}, u32[]{:S(2)}) copy-start(f32[48,6144]{1,0:T(8,128)} %factor.1) | copy-start | bytes 3538948
  8.2 0.9 %copy-start.2 = (bf16[2,2,48,384]{3,2,1,0:T(8,128)(2,1)S(1)}, bf16[2,2,48,384]{3,2,1,0:T(8,128)(2,1)}, u32[]{:S(2)}) copy-start(bf16[2,2,48,384]{3,2,1,0:T(8,128)(2,1)} %vectors.3) | copy-start | bytes 442372
  11.1 17.4 %collective-permute-start.3 = (bf16[4,1,128,384]{3,2,1,0:T(8,128)(2,1)S(1)}, bf16[4,1,128,384]{3,2,1,0:T(8,128)(2,1)S(1)}, u32[]{:S(2)}, u32[]{:S(2)}) collective-permute-start(bf16[4,1,128,384]{3,2,1,0:T(8,128)(2,1)S(1)} %get-tuple-element.47), channel_id=1, source_target_pairs={{1,2},{2,1},{3,4},{4,3},{5,6},{6,5},{7,8},{8,7},{9,10},{10,9},{11,... | collective-permute-start | bytes 1179656 | tf_op jit(solution)/shard_map/ppermute | solution.py:56
  14.3 14.2 %collective-permute-start.2 = (bf16[4,1,128,384]{3,2,1,0:T(8,128)(2,1)S(1)}, bf16[4,1,128,384]{3,2,1,0:T(8,128)(2,1)S(1)}, u32[]{:S(2)}, u32[]{:S(2)}) collective-permute-start(bf16[4,1,128,384]{3,2,1,0:T(8,128)(2,1)S(1)} %get-tuple-element.46), channel_id=1, source_target_pairs={{0,1},{1,0},{2,3},{3,2},{4,5},{5,4},{6,7},{7,6},{8,9},{9,8},{10,11... | collective-permute-start | bytes 1179656 | tf_op jit(solution)/shard_map/ppermute | solution.py:42
  14.3 12.1 %collective-permute-start.4 = (bf16[2,48,768]{2,1,0:T(8,128)(2,1)}, bf16[2,48,768]{2,1,0:T(8,128)(2,1)S(1)}, u32[]{:S(2)}, u32[]{:S(2)}) collective-permute-start(bf16[2,48,768]{2,1,0:T(8,128)(2,1)} %get-tuple-element.48), channel_id=1, source_target_pairs={{0,16},{16,32},{32,48},{48,0},{1,17},{17,33},{33,49},{49,1},{2,18}... | collective-permute-start | bytes 442376 | tf_op jit(solution)/shard_map/ppermute | solution.py:38
  15.5 13.0 %collective-permute-start.5 = (bf16[2,48,768]{2,1,0:T(8,128)(2,1)S(1)}, bf16[2,48,768]{2,1,0:T(8,128)(2,1)S(1)}, u32[]{:S(2)}, u32[]{:S(2)}) collective-permute-start(bf16[2,48,768]{2,1,0:T(8,128)(2,1)S(1)} %get-tuple-element.49), channel_id=1, source_target_pairs={{0,32},{16,48},{32,0},{48,16},{1,33},{17,49},{33,1},{49,17},{2,34}... | collective-permute-start | bytes 442376 | tf_op jit(solution)/shard_map/ppermute | solution.py:38
  20.9 7.6 %collective-permute-start.6 = (bf16[2,48,768]{2,1,0:T(8,128)(2,1)S(1)}, bf16[2,48,768]{2,1,0:T(8,128)(2,1)S(1)}, u32[]{:S(2)}, u32[]{:S(2)}) collective-permute-start(bf16[2,48,768]{2,1,0:T(8,128)(2,1)S(1)} %get-tuple-element.50), channel_id=1, source_target_pairs={{0,48},{16,0},{32,16},{48,32},{1,49},{17,1},{33,17},{49,33},{2,50}... | collective-permute-start | bytes 442376 | tf_op jit(solution)/shard_map/ppermute | solution.py:38
  21.1 15.2 %all-to-all-start = ((bf16[16,48,128]{2,1,0:T(8,128)(2,1)}), bf16[16,48,128]{2,1,0:T(8,128)(2,1)S(1)}, u32[]{:S(2)}, u32[]{:S(2)}) async-start(bf16[16,48,128]{2,1,0:T(8,128)(2,1)} %get-tuple-element.58), calls=%async_computation | async-start | bytes 393216 | tf_op jit(solution)/shard_map/all_to_all | solution.py:460
  34.1 8.4 %collective-permute-start.8 = (bf16[4,1,128,384]{3,2,1,0:T(8,128)(2,1)}, bf16[4,1,128,384]{3,2,1,0:T(8,128)(2,1)S(1)}, u32[]{:S(2)}, u32[]{:S(2)}) collective-permute-start(bf16[4,1,128,384]{3,2,1,0:T(8,128)(2,1)} %get-tuple-element.63), channel_id=1, source_target_pairs={{0,1},{1,0},{2,3},{3,2},{4,5},{5,4},{6,7},{7,6},{8,9},{9,8},{10,11... | collective-permute-start | bytes 1179656 | tf_op jit(solution)/shard_map/ppermute | solution.py:42
  34.2 9.6 %collective-permute-start.9 = (bf16[4,1,128,384]{3,2,1,0:T(8,128)(2,1)}, bf16[4,1,128,384]{3,2,1,0:T(8,128)(2,1)S(1)}, u32[]{:S(2)}, u32[]{:S(2)}) collective-permute-start(bf16[4,1,128,384]{3,2,1,0:T(8,128)(2,1)} %get-tuple-element.59), channel_id=1, source_target_pairs={{1,2},{2,1},{3,4},{4,3},{5,6},{6,5},{7,8},{8,7},{9,10},{10,9},{11,... | collective-permute-start | bytes 1179656 | tf_op jit(solution)/shard_map/ppermute | solution.py:56
  36.3 1.4 %collective-permute-start.7 = (bf16[16,48,128]{2,1,0:T(8,128)(2,1)S(1)}, bf16[16,48,128]{2,1,0:T(8,128)(2,1)S(1)}, u32[]{:S(2)}, u32[]{:S(2)}) collective-permute-start(bf16[16,48,128]{2,1,0:T(8,128)(2,1)S(1)} %all-to-all-done.refs_4_), channel_id=1, source_target_pairs={{0,1},{1,0},{2,3},{3,2},{4,5},{5,4},{6,7},{7,6},{8,9},{9,8},{10,11... | collective-permute-start | bytes 589832 | tf_op jit(solution)/shard_map/ppermute | solution.py:42
  38.0 9.4 %collective-permute-start.12 = (f32[4,48,128]{2,1,0:T(8,128)S(1)}, f32[4,48,128]{2,1,0:T(8,128)S(1)}, u32[]{:S(2)}, u32[]{:S(2)}) collective-permute-start(f32[4,48,128]{2,1,0:T(8,128)S(1)} %shard_map.59.refs_4_), channel_id=1, source_target_pairs={{0,48},{16,0},{32,16},{48,32},{1,49},{17,1},{33,17},{49,33},{2,50}... | collective-permute-start | bytes 294920 | tf_op jit(solution)/shard_map/ppermute | solution.py:38
  39.5 8.0 %collective-permute-start.11 = (f32[4,48,128]{2,1,0:T(8,128)S(1)}, f32[4,48,128]{2,1,0:T(8,128)S(1)}, u32[]{:S(2)}, u32[]{:S(2)}) collective-permute-start(f32[4,48,128]{2,1,0:T(8,128)S(1)} %shard_map.59.refs_4_), channel_id=1, source_target_pairs={{0,32},{16,48},{32,0},{48,16},{1,33},{17,49},{33,1},{49,17},{2,34}... | collective-permute-start | bytes 294920 | tf_op jit(solution)/shard_map/ppermute | solution.py:38
  41.1 6.7 %collective-permute-start.10 = (f32[4,48,128]{2,1,0:T(8,128)S(1)}, f32[4,48,128]{2,1,0:T(8,128)S(1)}, u32[]{:S(2)}, u32[]{:S(2)}) collective-permute-start(f32[4,48,128]{2,1,0:T(8,128)S(1)} %shard_map.59.refs_4_), channel_id=1, source_target_pairs={{0,16},{16,32},{32,48},{48,0},{1,17},{17,33},{33,49},{49,1},{2,18}... | collective-permute-start | bytes 294920 | tf_op jit(solution)/shard_map/ppermute | solution.py:38
  43.8 24.8 %copy-start.3 = (bf16[2,2,48,384]{3,2,1,0:T(8,128)(2,1)S(1)}, bf16[2,2,48,384]{3,2,1,0:T(8,128)(2,1)}, u32[]{:S(2)}) copy-start(bf16[2,2,48,384]{3,2,1,0:T(8,128)(2,1)} %vectors.3) | copy-start | bytes 442372
  48.4 1.5 %collective-permute-start.13 = (bf16[16,48,128]{2,1,0:T(8,128)(2,1)S(1)}, bf16[16,48,128]{2,1,0:T(8,128)(2,1)S(1)}, u32[]{:S(2)}, u32[]{:S(2)}) collective-permute-start(bf16[16,48,128]{2,1,0:T(8,128)(2,1)S(1)} %get-tuple-element.69), channel_id=1, source_target_pairs={{0,1},{1,0},{2,3},{3,2},{4,5},{5,4},{6,7},{7,6},{8,9},{9,8},{10,11... | collective-permute-start | bytes 589832 | tf_op jit(solution)/shard_map/ppermute | solution.py:42
  48.5 15.0 %collective-permute-start.14 = (bf16[1,2,128,384]{3,2,1,0:T(8,128)(2,1)}, bf16[1,2,128,384]{3,2,1,0:T(8,128)(2,1)S(1)}, u32[]{:S(2)}, u32[]{:S(2)}) collective-permute-start(bf16[1,2,128,384]{3,2,1,0:T(8,128)(2,1)} %get-tuple-element.71), channel_id=1, source_target_pairs={{0,16},{16,0},{32,48},{48,32},{64,80},{80,64},{96,112},{112,96},{1... | collective-permute-start | bytes 589832 | tf_op jit(solution)/shard_map/ppermute | solution.py:49
  48.9 14.6 %collective-permute-start.15 = (bf16[1,2,128,384]{3,2,1,0:T(8,128)(2,1)S(1)}, bf16[1,2,128,384]{3,2,1,0:T(8,128)(2,1)S(1)}, u32[]{:S(2)}, u32[]{:S(2)}) collective-permute-start(bf16[1,2,128,384]{3,2,1,0:T(8,128)(2,1)S(1)} %get-tuple-element.72), channel_id=1, source_target_pairs={{16,32},{32,16},{48,64},{64,48},{80,96},{96,80},{17,33},{33,17},{4... | collective-permute-start | bytes 589832 | tf_op jit(solution)/shard_map/ppermute | solution.py:49
  50.7 17.8 %all-to-all-start.1 = ((bf16[16,48,128]{2,1,0:T(8,128)(2,1)}), bf16[16,48,128]{2,1,0:T(8,128)(2,1)S(1)}, u32[]{:S(2)}, u32[]{:S(2)}) async-start(bf16[16,48,128]{2,1,0:T(8,128)(2,1)} %add_convert_fusion), calls=%async_computation.1 | async-start | bytes 393216 | tf_op jit(solution)/shard_map/all_to_all | solution.py:475

commit v5 on v4

--- a/solution.py
+++ b/solution.py
@@ -83,8 +83,8 @@
     at = position()
     more, (sides, held, sems) = rest[:-3], rest[-3:]
     if fetch:
-        window_sems, more = more[-1], more[:-1]
-        targets, more = more[-2:], more[:-2]
+        (window_sems, stage, stage_sems), targets, outs = more[-3:], more[-5:-3], more[:-5]
+        more = (outs, stage, stage_sems)
         loads = []
         for i, (source, target) in enumerate(zip((own, ends), targets)):
             loads.append(pltpu.make_async_copy(source, target, window_sems.at[i]))
@@ -108,7 +108,6 @@
         near, far = pair[a, 0], present(at[3], outer[a, 0])
         sides[0, a] = jnp.where(first, far, near)
         sides[1, a] = jnp.where(first, near, far)
-
     if fetch:
         for load in loads:
             load.wait()
@@ -129,6 +128,10 @@
         sources = jnp.concatenate([window(sa, sb) for _, sa, sb in found], axis=1)
         weights = held[start : start + len(found)].reshape(len(found) * line, line)
         put(a, b, jnp.dot(sources, weights, preferred_element_type=F32), at, more)
+    if fetch:
+        for i in range(2):
+            for a in range(WIDE):
+                pltpu.make_async_copy(stage.at[i, a], outs[i].at[a, 0], stage_sems.at[i, a]).wait()
 
 
 def line_solve(cells, put, shapes, windows, line_inverse, extra=(), fetch=False):
@@ -139,14 +142,21 @@
     def body(*refs):
         line_kernel(cells, put, fetch, *refs)
 
+    out_specs, scratch = [VMEM] * len(shapes), []
     if fetch:
         shapes = shapes + [struct(w.shape, w.dtype) for w in windows[:2]]
+        out_specs = [HBM] * 2 + [VMEM] * 2
+        scratch = [
+            pltpu.SemaphoreType.DMA((2,)),
+            pltpu.VMEM((2, WIDE, rhs, line), BF16),
+            pltpu.SemaphoreType.DMA((2, WIDE)),
+        ]
     return pl.pallas_call(
         body,
         out_shape=shapes,
         in_specs=[ANY if fetch else VMEM] * 2 + [VMEM] * 2 + [HBM] + [VMEM] * len(extra),
-        out_specs=[VMEM] * len(shapes),
-        scratch_shapes=[pltpu.SemaphoreType.DMA((2,))] * fetch
+        out_specs=out_specs,
+        scratch_shapes=scratch
         + [
             pltpu.VMEM((2, WIDE, rhs, line), BF16),
             pltpu.VMEM((count, line, line), line_inverse.dtype),
@@ -158,17 +168,16 @@
 
 
 def put_rim(a, b, value, at, refs):
+    outs, stage, sems = refs
     value = value.astype(BF16)
     first = at[0] == 0
     to_pair = first if b else jnp.logical_not(first)
-
-    @pl.when(to_pair)
-    def _():
-        refs[0][a, 0] = value
-
-    @pl.when(jnp.logical_not(to_pair))
-    def _():
-        refs[1][a, 0] = value
+    for i, chosen in ((0, to_pair), (1, jnp.logical_not(to_pair))):
+
+        @pl.when(chosen)
+        def _(i=i):
+            stage[i, a] = value
+            pltpu.make_async_copy(stage.at[i, a], outs[i].at[a, 0], sems.at[i, a]).start()
 
 
 def returned(at, from_pair, from_outer, a, b):
@@ -452,13 +461,14 @@
         near, far = swap_pairs(to_near, GRP, n_grp, 0), swap_pairs(to_far, GRP, n_grp, 1)
         receivers = sizes["zh"] * sizes["zl"] * sizes["y"]
         spread, *parts = prepare(rounded, deflation, counts, coarse_factor, receivers, ring, sizes["zh"])
-        rows = [parts[0]] + [rotate(parts[n], RING, ring, n) for n in range(1, ring)]
+        moved = {n: rotate(parts[n], RING, ring, n) for n in (2, 1, 3)}
+        rows = [parts[0]] + [moved[n] for n in range(1, ring)]
         far, _ = tie((far, parts[0]))
         to_pair, to_outer, own, ends = columns(near, far, rounded)
         outer, pair = swap_outward(to_outer, n_sub), swap(to_pair, "c")
         spread, _ = tie((spread, to_outer))
         gathered = lax.all_to_all(spread, SPREAD, 0, 0)
-        outer, *rows = tie((outer, *rows))
+        outer, rows[0], rows[2], rows[1], rows[3] = tie((outer, rows[0], rows[2], rows[1], rows[3]))
 
         to_pair, to_outer, own, ends = rim_lines((own, ends, pair, outer), line_inverse)
         from_outer, from_pair = swap_outward(to_outer, n_sub), swap(to_pair, "c")
@@ -475,6 +485,7 @@
         terms_in = lax.all_to_all(terms_out, SPREAD, 0, 0)
         own, _ = tie((own, terms_out))
         inner = inner_lines((own, ends, pair, outer), line_inverse)
+        inner, from_far = tie((inner, from_far))
         first_level = collect(inner, from_pair, from_outer, from_near, from_far)
         return leave(counts, first_level, terms_in, deflation)
 

time: 70.1 us -> 68.8 us (0.981)
  starting transfers between devices: 37.6 us -> 36.5 us
    all_to_all x1, starting transfers between devices: 9.5 us -> 6.33 us  [body(): terms_in = lax.all_to_all(terms_out, SPREAD, 0, 0)]
    ppermute x4, starting transfers between devices: 6.08 us -> 8.11 us  [swap_pairs(): return lax.ppermute(value, axes, pairs)]
  transfers between devices with their start and end apart: 18 -> 18, of which waited for: 7 -> 6; matrix products, arithmetic and copies ran while one was open for 1% -> 1% of each run, Pallas kernels for 21% -> 21%
where the time goes in v5:
time: 68.8 us; the launch traced here: 68 us
  starting transfers between devices  36.5 us (53%)
  Pallas kernels  16.5 us (24%)
  waiting for transfers between devices  10.1 us (15%)
  local copies, waits for them, and re-layouts  3.31 us (5%)
  between operations  0.84 us (1%)
  other arithmetic  0.73 us (1%)
    pallas_call x3, Pallas kernels, line_solve(): pl.pallas_call(body, out_shape=shapes, in_specs=[ANY if fetch else VMEM]...  12.3 us
    ppermute x6, starting transfers between devices, rotate(): lax.ppermute(value, axes, [(i, (i + step) % size) for i in range(size)])  11.2 us
    ppermute x4, starting transfers between devices, swap_pairs(): return lax.ppermute(value, axes, pairs)  8.11 us
    all_to_all x1, starting transfers between devices, body(): terms_in = lax.all_to_all(terms_out, SPREAD, 0, 0)  6.33 us
    ppermute x2, starting transfers between devices, swap_outward(): return lax.ppermute(value, SUB, pairs)  5.99 us
    all_to_all x1, waiting for transfers between devices, body(): terms_in = lax.all_to_all(terms_out, SPREAD, 0, 0)  4.79 us
    all_to_all x1, starting transfers between devices, body(): gathered = lax.all_to_all(spread, SPREAD, 0, 0)  4.7 us
    unnamed x8, local copies, waits for them, and re-layouts  3.31 us
  transfers between devices with their start and end apart: 18, of which 6 were waited for; matrix products, arithmetic and copies ran while one was open for 1% of the time, Pallas kernels for 21%

profile of v5, /device:TPU:0, one launch (start us, length us, event | category | flops | bytes accessed | tf_op | source)
XLA Modules:
  0.0 68.0 jit_solution(12380261648003166672)
XLA Ops:
  0.0 1.1 %copy-done.1 = f32[2,2,128,384]{3,2,1,0:T(8,128)S(1)} copy-done((f32[2,2,128,384]{3,2,1,0:T(8,128)S(1)}, f32[2,2,128,384]{3,2,1,0:T(8,128)}, u32[]{:S(2)}) %copy-start.1) | copy-done | bytes 786456
  1.2 0.7 collective-permute-start.1
  1.9 4.4 %collective-permute-start = (bf16[1,2,128,384]{3,2,1,0:T(8,128)(2,1)S(1)}, bf16[1,2,128,384]{3,2,1,0:T(8,128)(2,1)S(1)}, u32[]{:S(2)}, u32[]{:S(2)}) collective-permute-start(bf16[1,2,128,384]{3,2,1,0:T(8,128)(2,1)S(1)} %get-tuple-element.41), channel_id=1, source_target_pairs={{0,16},{16,0},{32,48},{48,32},{64,80},{80,64},{96,112},{112,96},{1... | collective-permute-start | bytes 589832 | tf_op jit(solution)/shard_map/ppermute | solution.py:49
  6.9 1.3 %copy-done = f32[48,6144]{1,0:T(8,128)S(1)} copy-done((f32[48,6144]{1,0:T(8,128)S(1)}, f32[48,6144]{1,0:T(8,128)}, u32[]{:S(2)}) %copy-start) | copy-done | bytes 1179672
  8.2 0.9 %copy-done.2 = bf16[2,2,48,384]{3,2,1,0:T(8,128)(2,1)S(1)} copy-done((bf16[2,2,48,384]{3,2,1,0:T(8,128)(2,1)S(1)}, bf16[2,2,48,384]{3,2,1,0:T(8,128)(2,1)}, u32[]{:S(2)}) %copy-start.2) | copy-done | bytes 147480
  9.1 1.7 %shard_map.56 = (bf16[16,48,128]{2,1,0:T(8,128)(2,1)}, bf16[2,48,768]{2,1,0:T(8,128)(2,1)S(1)}, bf16[2,48,768]{2,1,0:T(8,128)(2,1)S(1)}, bf16[2,48,768]{2,1,0:T(8,128)(2,1)}, bf16[2,48,768]{2,1,0:T(8,128)(2,1)S(1)}) custom-call(s32[1,1]{1,0:T(1,128)S(6)} %copy.6.count, bf16[2,2,128,384]{3,2,1,0:T(8,128)(2,1)S(1)} %get-tuple-element.43.rounded, ...), custom_call_target="tpu_custom_call" | custom-call | tf_op jit(solution)/shard_map/pallas_call | solution.py:333
  10.9 0.2 shard_map.57
  11.1 3.2 %collective-permute-start.3 = (bf16[4,1,128,384]{3,2,1,0:T(8,128)(2,1)S(1)}, bf16[4,1,128,384]{3,2,1,0:T(8,128)(2,1)S(1)}, u32[]{:S(2)}, u32[]{:S(2)}) collective-permute-start(bf16[4,1,128,384]{3,2,1,0:T(8,128)(2,1)S(1)} %get-tuple-element.49), channel_id=1, source_target_pairs={{1,2},{2,1},{3,4},{4,3},{5,6},{6,5},{7,8},{8,7},{9,10},{10,9},{11,... | collective-permute-start | bytes 1179656 | tf_op jit(solution)/shard_map/ppermute | solution.py:56
  14.3 4.1 %collective-permute-start.4 = (bf16[2,48,768]{2,1,0:T(8,128)(2,1)}, bf16[2,48,768]{2,1,0:T(8,128)(2,1)S(1)}, u32[]{:S(2)}, u32[]{:S(2)}) collective-permute-start(bf16[2,48,768]{2,1,0:T(8,128)(2,1)} %get-tuple-element.50), channel_id=1, source_target_pairs={{0,32},{16,48},{32,0},{48,16},{1,33},{17,49},{33,1},{49,17},{2,34}... | collective-permute-start | bytes 442376 | tf_op jit(solution)/shard_map/ppermute | solution.py:38
  18.5 1.8 %collective-permute-start.5 = (bf16[2,48,768]{2,1,0:T(8,128)(2,1)S(1)}, bf16[2,48,768]{2,1,0:T(8,128)(2,1)S(1)}, u32[]{:S(2)}, u32[]{:S(2)}) collective-permute-start(bf16[2,48,768]{2,1,0:T(8,128)(2,1)S(1)} %get-tuple-element.51), channel_id=1, source_target_pairs={{0,16},{16,32},{32,48},{48,0},{1,17},{17,33},{33,49},{49,1},{2,18}... | collective-permute-start | bytes 442376 | tf_op jit(solution)/shard_map/ppermute | solution.py:38
  20.3 1.4 %collective-permute-start.6 = (bf16[2,48,768]{2,1,0:T(8,128)(2,1)S(1)}, bf16[2,48,768]{2,1,0:T(8,128)(2,1)S(1)}, u32[]{:S(2)}, u32[]{:S(2)}) collective-permute-start(bf16[2,48,768]{2,1,0:T(8,128)(2,1)S(1)} %get-tuple-element.52), channel_id=1, source_target_pairs={{0,48},{16,0},{32,16},{48,32},{1,49},{17,1},{33,17},{49,33},{2,50}... | collective-permute-start | bytes 442376 | tf_op jit(solution)/shard_map/ppermute | solution.py:38
  21.7 4.7 %all-to-all-start = ((bf16[16,48,128]{2,1,0:T(8,128)(2,1)}), bf16[16,48,128]{2,1,0:T(8,128)(2,1)S(1)}, u32[]{:S(2)}, u32[]{:S(2)}) async-start(bf16[16,48,128]{2,1,0:T(8,128)(2,1)} %get-tuple-element.60), calls=%async_computation | async-start | bytes 393216 | tf_op jit(solution)/shard_map/all_to_all | solution.py:470
  26.4 1.4 %collective-permute-done.6.refs_3_ = bf16[2,48,768]{2,1,0:T(8,128)(2,1)S(1)} collective-permute-done((bf16[2,48,768]{2,1,0:T(8,128)(2,1)S(1)}, bf16[2,48,768]{2,1,0:T(8,128)(2,1)S(1)}, u32[]{:S(2)}, u32[]{:S(2)}) %collective-permute-start.6) | collective-permute-done | bytes 147488 | tf_op jit(solution)/shard_map/ppermute | solution.py:38
  27.9 5.3 %shard_map.58 = (bf16[4,1,128,384]{3,2,1,0:T(8,128)(2,1)}, bf16[4,1,128,384]{3,2,1,0:T(8,128)(2,1)}, bf16[2,2,128,384]{3,2,1,0:T(8,128)(2,1)S(1)}, bf16[2,2,128,384]{3,2,1,0:T(8,128)(2,1)S(1)}) custom-call(bf16[2,2,128,384]{3,2,1,0:T(8,128)(2,1)S(1)} %get-tuple-element.46.refs_0_, bf16[2,2,128,384]{3,2,1,0:T(8,128)(2,1)S(1)} %get-tuple-element.47.refs_1_, ...), custom_call_target="tpu_custom_call" | custom-call | flops 1056964608 | bytes 8257536 | tf_op jit(solution)/shard_map/pallas_call | solution.py:154
  33.3 2.7 %collective-permute-start.9 = (bf16[4,1,128,384]{3,2,1,0:T(8,128)(2,1)}, bf16[4,1,128,384]{3,2,1,0:T(8,128)(2,1)S(1)}, u32[]{:S(2)}, u32[]{:S(2)}) collective-permute-start(bf16[4,1,128,384]{3,2,1,0:T(8,128)(2,1)} %get-tuple-element.61), channel_id=1, source_target_pairs={{1,2},{2,1},{3,4},{4,3},{5,6},{6,5},{7,8},{8,7},{9,10},{10,9},{11,... | collective-permute-start | bytes 1179656 | tf_op jit(solution)/shard_map/ppermute | solution.py:56
  36.1 1.4 %collective-permute-done.7.refs_5_ = bf16[16,48,128]{2,1,0:T(8,128)(2,1)S(1)} collective-permute-done((bf16[16,48,128]{2,1,0:T(8,128)(2,1)S(1)}, bf16[16,48,128]{2,1,0:T(8,128)(2,1)S(1)}, u32[]{:S(2)}, u32[]{:S(2)}) %collective-permute-start.7) | collective-permute-done | bytes 196640 | tf_op jit(solution)/shard_map/ppermute | solution.py:42
  37.5 0.3 shard_map.59.refs_4_
  37.8 1.6 %collective-permute-start.12 = (f32[4,48,128]{2,1,0:T(8,128)S(1)}, f32[4,48,128]{2,1,0:T(8,128)S(1)}, u32[]{:S(2)}, u32[]{:S(2)}) collective-permute-start(f32[4,48,128]{2,1,0:T(8,128)S(1)} %shard_map.59.refs_4_), channel_id=1, source_target_pairs={{0,48},{16,0},{32,16},{48,32},{1,49},{17,1},{33,17},{49,33},{2,50}... | collective-permute-start | bytes 294920 | tf_op jit(solution)/shard_map/ppermute | solution.py:38
  39.5 0.8 %collective-permute-start.11 = (f32[4,48,128]{2,1,0:T(8,128)S(1)}, f32[4,48,128]{2,1,0:T(8,128)S(1)}, u32[]{:S(2)}, u32[]{:S(2)}) collective-permute-start(f32[4,48,128]{2,1,0:T(8,128)S(1)} %shard_map.59.refs_4_), channel_id=1, source_target_pairs={{0,32},{16,48},{32,0},{48,16},{1,33},{17,49},{33,1},{49,17},{2,34}... | collective-permute-start | bytes 294920 | tf_op jit(solution)/shard_map/ppermute | solution.py:38
  40.3 1.3 %collective-permute-start.10 = (f32[4,48,128]{2,1,0:T(8,128)S(1)}, f32[4,48,128]{2,1,0:T(8,128)S(1)}, u32[]{:S(2)}, u32[]{:S(2)}) collective-permute-start(f32[4,48,128]{2,1,0:T(8,128)S(1)} %shard_map.59.refs_4_), channel_id=1, source_target_pairs={{0,16},{16,32},{32,48},{48,0},{1,17},{17,33},{33,49},{49,1},{2,18}... | collective-permute-start | bytes 294920 | tf_op jit(solution)/shard_map/ppermute | solution.py:38
  41.6 1.3 %collective-permute-done.9.refs_6_.from_outer = bf16[4,1,128,384]{3,2,1,0:T(8,128)(2,1)S(1)} collective-permute-done((bf16[4,1,128,384]{3,2,1,0:T(8,128)(2,1)}, bf16[4,1,128,384]{3,2,1,0:T(8,128)(2,1)S(1)}, u32[]{:S(2)}, u32[]{:S(2)}) %collective-permute-start.9) | collective-permute-done | bytes 393248 | tf_op jit(solution)/shard_map/ppermute | solution.py:56
  42.9 3.6 %shard_map.60 = (bf16[1,2,128,384]{3,2,1,0:T(8,128)(2,1)S(1)}, bf16[1,2,128,384]{3,2,1,0:T(8,128)(2,1)}) custom-call(bf16[2,2,128,384]{3,2,1,0:T(8,128)(2,1)S(1)} %get-tuple-element.72.refs_0_, bf16[2,2,128,384]{3,2,1,0:T(8,128)(2,1)S(1)} %get-tuple-element.64.refs_1_, bf16[4,1,128,384]{3,2,1,0:T(8,128)(2,1)S(1)} %collective-permute-done.2.refs_2_, ...), custom_call_target="tpu_custom_call" | custom-call | flops 603979776 | bytes 4718592 | tf_op jit(solution)/shard_map/pallas_call | solution.py:154
  46.6 1.0 %collective-permute-done.10.refs_5_ = f32[4,48,128]{2,1,0:T(8,128)S(1)} collective-permute-done((f32[4,48,128]{2,1,0:T(8,128)S(1)}, f32[4,48,128]{2,1,0:T(8,128)S(1)}, u32[]{:S(2)}, u32[]{:S(2)}) %collective-permute-start.10) | collective-permute-done | bytes 98336 | tf_op jit(solution)/shard_map/ppermute | solution.py:38
  47.6 0.6 shard_map.61
  48.4 0.7 collective-permute-start.14
  49.0 2.4 %collective-permute-start.15 = (bf16[1,2,128,384]{3,2,1,0:T(8,128)(2,1)S(1)}, bf16[1,2,128,384]{3,2,1,0:T(8,128)(2,1)S(1)}, u32[]{:S(2)}, u32[]{:S(2)}) collective-permute-start(bf16[1,2,128,384]{3,2,1,0:T(8,128)(2,1)S(1)} %get-tuple-element.75), channel_id=1, source_target_pairs={{0,16},{16,0},{32,48},{48,32},{64,80},{80,64},{96,112},{112,96},{1... | collective-permute-start | bytes 589832 | tf_op jit(solution)/shard_map/ppermute | solution.py:49
  51.4 0.7 %add_convert_fusion = bf16[16,48,128]{2,1,0:T(8,128)(2,1)} fusion(f32[16,48,128]{2,1,0:T(8,128)S(1)} %get-tuple-element.68, bf16[16,48,128]{2,1,0:T(8,128)(2,1)S(1)} %collective-permute-done.13), kind=kLoop, calls=%fused_computation | loop fusion | flops 294912 | bytes 786432 | tf_op jit(solution)/shard_map/convert_element_type | solution.py:484
  52.2 6.3 %all-to-all-start.1 = ((bf16[16,48,128]{2,1,0:T(8,128)(2,1)}), bf16[16,48,128]{2,1,0:T(8,128)(2,1)S(1)}, u32[]{:S(2)}, u32[]{:S(2)}) async-start(bf16[16,48,128]{2,1,0:T(8,128)(2,1)} %add_convert_fusion), calls=%async_computation.1 | async-start | bytes 393216 | tf_op jit(solution)/shard_map/all_to_all | solution.py:485
  58.5 3.3 %shard_map.62.inner = f32[2,2,128,384]{3,2,1,0:T(8,128)S(1)} custom-call(bf16[2,2,128,384]{3,2,1,0:T(8,128)(2,1)S(1)} %get-tuple-element.72.refs_0_, bf16[2,2,128,384]{3,2,1,0:T(8,128)(2,1)S(1)} %get-tuple-element.64.refs_1_, bf16[4,1,128,384]{3,2,1,0:T(8,128)(2,1)S(1)} %collective-permute-done.2.refs_2_, ...), custom_call_target="tpu_custom_call" | custom-call | flops 754974720 | bytes 5898240 | tf_op jit(solution)/shard_map/pallas_call | solution.py:154
  61.9 0.2 shard_map.63.first_level
  62.1 4.8 %all-to-all-done.1.terms_in = bf16[16,48,128]{2,1,0:T(8,128)(2,1)S(1)} async-done(((bf16[16,48,128]{2,1,0:T(8,128)(2,1)}), bf16[16,48,128]{2,1,0:T(8,128)(2,1)S(1)}, u32[]{:S(2)}, u32[]{:S(2)}) %all-to-all-start.1) | async-done | bytes 196640 | tf_op jit(solution)/shard_map/all_to_all | solution.py:485
  66.9 1.1 %shard_map.64 = f32[2,2,128,384]{3,2,1,0:T(8,128)} custom-call(s32[1,1]{1,0:T(1,128)S(6)} %copy.6.count, f32[2,2,128,384]{3,2,1,0:T(8,128)S(1)} %shard_map.63.first_level, bf16[16,48,128]{2,1,0:T(8,128)(2,1)S(1)} %all-to-all-done.1.terms_in, bf16[2,2,48,384]{3,2,1,0:T(8,128)(2,1)S(1)} %copy-done.3), custom_call_target="tpu_custom_call" | custom-call | tf_op jit(solution)/shard_map/pallas_call | solution.py:441
  (23 shorter events, 0.4 us)
Async XLA Ops:
  0.0 1.1 %copy-start.1 = (f32[2,2,128,384]{3,2,1,0:T(8,128)S(1)}, f32[2,2,128,384]{3,2,1,0:T(8,128)}, u32[]{:S(2)}) copy-start(f32[2,2,128,384]{3,2,1,0:T(8,128)} %residual.1) | copy-start | bytes 2359300
  1.2 9.6 %collective-permute-start.1 = (bf16[1,2,128,384]{3,2,1,0:T(8,128)(2,1)S(1)}, bf16[1,2,128,384]{3,2,1,0:T(8,128)(2,1)S(1)}, u32[]{:S(2)}, u32[]{:S(2)}) collective-permute-start(bf16[1,2,128,384]{3,2,1,0:T(8,128)(2,1)S(1)} %get-tuple-element.42), channel_id=1, source_target_pairs={{16,32},{32,16},{48,64},{64,48},{80,96},{96,80},{17,33},{33,17},{4... | collective-permute-start | bytes 589832 | tf_op jit(solution)/shard_map/ppermute | solution.py:49
  1.9 9.0 %collective-permute-start = (bf16[1,2,128,384]{3,2,1,0:T(8,128)(2,1)S(1)}, bf16[1,2,128,384]{3,2,1,0:T(8,128)(2,1)S(1)}, u32[]{:S(2)}, u32[]{:S(2)}) collective-permute-start(bf16[1,2,128,384]{3,2,1,0:T(8,128)(2,1)S(1)} %get-tuple-element.41), channel_id=1, source_target_pairs={{0,16},{16,0},{32,48},{48,32},{64,80},{80,64},{96,112},{112,96},{1... | collective-permute-start | bytes 589832 | tf_op jit(solution)/shard_map/ppermute | solution.py:49
  6.9 1.3 %copy-start = (f32[48,6144]{1,0:T(8,128)S(1)}, f32[48,6144]{1,0:T(8,128)}, u32[]{:S(2)}) copy-start(f32[48,6144]{1,0:T(8,128)} %factor.1) | copy-start | bytes 3538948
  8.2 0.9 %copy-start.2 = (bf16[2,2,48,384]{3,2,1,0:T(8,128)(2,1)S(1)}, bf16[2,2,48,384]{3,2,1,0:T(8,128)(2,1)}, u32[]{:S(2)}) copy-start(bf16[2,2,48,384]{3,2,1,0:T(8,128)(2,1)} %vectors.3) | copy-start | bytes 442372
  11.1 16.8 %collective-permute-start.3 = (bf16[4,1,128,384]{3,2,1,0:T(8,128)(2,1)S(1)}, bf16[4,1,128,384]{3,2,1,0:T(8,128)(2,1)S(1)}, u32[]{:S(2)}, u32[]{:S(2)}) collective-permute-start(bf16[4,1,128,384]{3,2,1,0:T(8,128)(2,1)S(1)} %get-tuple-element.49), channel_id=1, source_target_pairs={{1,2},{2,1},{3,4},{4,3},{5,6},{6,5},{7,8},{8,7},{9,10},{10,9},{11,... | collective-permute-start | bytes 1179656 | tf_op jit(solution)/shard_map/ppermute | solution.py:56
  14.3 13.6 %collective-permute-start.2 = (bf16[4,1,128,384]{3,2,1,0:T(8,128)(2,1)S(1)}, bf16[4,1,128,384]{3,2,1,0:T(8,128)(2,1)S(1)}, u32[]{:S(2)}, u32[]{:S(2)}) collective-permute-start(bf16[4,1,128,384]{3,2,1,0:T(8,128)(2,1)S(1)} %get-tuple-element.48), channel_id=1, source_target_pairs={{0,1},{1,0},{2,3},{3,2},{4,5},{5,4},{6,7},{7,6},{8,9},{9,8},{10,11... | collective-permute-start | bytes 1179656 | tf_op jit(solution)/shard_map/ppermute | solution.py:42
  14.3 12.1 %collective-permute-start.4 = (bf16[2,48,768]{2,1,0:T(8,128)(2,1)}, bf16[2,48,768]{2,1,0:T(8,128)(2,1)S(1)}, u32[]{:S(2)}, u32[]{:S(2)}) collective-permute-start(bf16[2,48,768]{2,1,0:T(8,128)(2,1)} %get-tuple-element.50), channel_id=1, source_target_pairs={{0,32},{16,48},{32,0},{48,16},{1,33},{17,49},{33,1},{49,17},{2,34}... | collective-permute-start | bytes 442376 | tf_op jit(solution)/shard_map/ppermute | solution.py:38
  18.5 8.0 %collective-permute-start.5 = (bf16[2,48,768]{2,1,0:T(8,128)(2,1)S(1)}, bf16[2,48,768]{2,1,0:T(8,128)(2,1)S(1)}, u32[]{:S(2)}, u32[]{:S(2)}) collective-permute-start(bf16[2,48,768]{2,1,0:T(8,128)(2,1)S(1)} %get-tuple-element.51), channel_id=1, source_target_pairs={{0,16},{16,32},{32,48},{48,0},{1,17},{17,33},{33,49},{49,1},{2,18}... | collective-permute-start | bytes 442376 | tf_op jit(solution)/shard_map/ppermute | solution.py:38
  20.3 7.6 %collective-permute-start.6 = (bf16[2,48,768]{2,1,0:T(8,128)(2,1)S(1)}, bf16[2,48,768]{2,1,0:T(8,128)(2,1)S(1)}, u32[]{:S(2)}, u32[]{:S(2)}) collective-permute-start(bf16[2,48,768]{2,1,0:T(8,128)(2,1)S(1)} %get-tuple-element.52), channel_id=1, source_target_pairs={{0,48},{16,0},{32,16},{48,32},{1,49},{17,1},{33,17},{49,33},{2,50}... | collective-permute-start | bytes 442376 | tf_op jit(solution)/shard_map/ppermute | solution.py:38
  21.7 14.4 %all-to-all-start = ((bf16[16,48,128]{2,1,0:T(8,128)(2,1)}), bf16[16,48,128]{2,1,0:T(8,128)(2,1)S(1)}, u32[]{:S(2)}, u32[]{:S(2)}) async-start(bf16[16,48,128]{2,1,0:T(8,128)(2,1)} %get-tuple-element.60), calls=%async_computation | async-start | bytes 393216 | tf_op jit(solution)/shard_map/all_to_all | solution.py:470
  33.2 8.4 %collective-permute-start.8 = (bf16[4,1,128,384]{3,2,1,0:T(8,128)(2,1)}, bf16[4,1,128,384]{3,2,1,0:T(8,128)(2,1)S(1)}, u32[]{:S(2)}, u32[]{:S(2)}) collective-permute-start(bf16[4,1,128,384]{3,2,1,0:T(8,128)(2,1)} %get-tuple-element.65), channel_id=1, source_target_pairs={{0,1},{1,0},{2,3},{3,2},{4,5},{5,4},{6,7},{7,6},{8,9},{9,8},{10,11... | collective-permute-start | bytes 1179656 | tf_op jit(solution)/shard_map/ppermute | solution.py:42
  33.3 9.6 %collective-permute-start.9 = (bf16[4,1,128,384]{3,2,1,0:T(8,128)(2,1)}, bf16[4,1,128,384]{3,2,1,0:T(8,128)(2,1)S(1)}, u32[]{:S(2)}, u32[]{:S(2)}) collective-permute-start(bf16[4,1,128,384]{3,2,1,0:T(8,128)(2,1)} %get-tuple-element.61), channel_id=1, source_target_pairs={{1,2},{2,1},{3,4},{4,3},{5,6},{6,5},{7,8},{8,7},{9,10},{10,9},{11,... | collective-permute-start | bytes 1179656 | tf_op jit(solution)/shard_map/ppermute | solution.py:56
  36.1 1.4 %collective-permute-start.7 = (bf16[16,48,128]{2,1,0:T(8,128)(2,1)S(1)}, bf16[16,48,128]{2,1,0:T(8,128)(2,1)S(1)}, u32[]{:S(2)}, u32[]{:S(2)}) collective-permute-start(bf16[16,48,128]{2,1,0:T(8,128)(2,1)S(1)} %all-to-all-done.refs_4_), channel_id=1, source_target_pairs={{0,1},{1,0},{2,3},{3,2},{4,5},{5,4},{6,7},{7,6},{8,9},{9,8},{10,11... | collective-permute-start | bytes 589832 | tf_op jit(solution)/shard_map/ppermute | solution.py:42
  37.8 8.8 %collective-permute-start.12 = (f32[4,48,128]{2,1,0:T(8,128)S(1)}, f32[4,48,128]{2,1,0:T(8,128)S(1)}, u32[]{:S(2)}, u32[]{:S(2)}) collective-permute-start(f32[4,48,128]{2,1,0:T(8,128)S(1)} %shard_map.59.refs_4_), channel_id=1, source_target_pairs={{0,48},{16,0},{32,16},{48,32},{1,49},{17,1},{33,17},{49,33},{2,50}... | collective-permute-start | bytes 294920 | tf_op jit(solution)/shard_map/ppermute | solution.py:38
  39.5 7.1 %collective-permute-start.11 = (f32[4,48,128]{2,1,0:T(8,128)S(1)}, f32[4,48,128]{2,1,0:T(8,128)S(1)}, u32[]{:S(2)}, u32[]{:S(2)}) collective-permute-start(f32[4,48,128]{2,1,0:T(8,128)S(1)} %shard_map.59.refs_4_), channel_id=1, source_target_pairs={{0,32},{16,48},{32,0},{48,16},{1,33},{17,49},{33,1},{49,17},{2,34}... | collective-permute-start | bytes 294920 | tf_op jit(solution)/shard_map/ppermute | solution.py:38
  40.3 7.3 %collective-permute-start.10 = (f32[4,48,128]{2,1,0:T(8,128)S(1)}, f32[4,48,128]{2,1,0:T(8,128)S(1)}, u32[]{:S(2)}, u32[]{:S(2)}) collective-permute-start(f32[4,48,128]{2,1,0:T(8,128)S(1)} %shard_map.59.refs_4_), channel_id=1, source_target_pairs={{0,16},{16,32},{32,48},{48,0},{1,17},{17,33},{33,49},{49,1},{2,18}... | collective-permute-start | bytes 294920 | tf_op jit(solution)/shard_map/ppermute | solution.py:38
  42.9 23.9 %copy-start.3 = (bf16[2,2,48,384]{3,2,1,0:T(8,128)(2,1)S(1)}, bf16[2,2,48,384]{3,2,1,0:T(8,128)(2,1)}, u32[]{:S(2)}) copy-start(bf16[2,2,48,384]{3,2,1,0:T(8,128)(2,1)} %vectors.3) | copy-start | bytes 442372
  48.3 3.2 %collective-permute-start.13 = (bf16[16,48,128]{2,1,0:T(8,128)(2,1)S(1)}, bf16[16,48,128]{2,1,0:T(8,128)(2,1)S(1)}, u32[]{:S(2)}, u32[]{:S(2)}) collective-permute-start(bf16[16,48,128]{2,1,0:T(8,128)(2,1)S(1)} %get-tuple-element.71), channel_id=1, source_target_pairs={{0,1},{1,0},{2,3},{3,2},{4,5},{5,4},{6,7},{7,6},{8,9},{9,8},{10,11... | collective-permute-start | bytes 589832 | tf_op jit(solution)/shard_map/ppermute | solution.py:42
  48.4 13.5 %collective-permute-start.14 = (bf16[1,2,128,384]{3,2,1,0:T(8,128)(2,1)}, bf16[1,2,128,384]{3,2,1,0:T(8,128)(2,1)S(1)}, u32[]{:S(2)}, u32[]{:S(2)}) collective-permute-start(bf16[1,2,128,384]{3,2,1,0:T(8,128)(2,1)} %get-tuple-element.73), channel_id=1, source_target_pairs={{16,32},{32,16},{48,64},{64,48},{80,96},{96,80},{17,33},{33,17},{4... | collective-permute-start | bytes 589832 | tf_op jit(solution)/shard_map/ppermute | solution.py:49
  49.0 12.8 %collective-permute-start.15 = (bf16[1,2,128,384]{3,2,1,0:T(8,128)(2,1)S(1)}, bf16[1,2,128,384]{3,2,1,0:T(8,128)(2,1)S(1)}, u32[]{:S(2)}, u32[]{:S(2)}) collective-permute-start(bf16[1,2,128,384]{3,2,1,0:T(8,128)(2,1)S(1)} %get-tuple-element.75), channel_id=1, source_target_pairs={{0,16},{16,0},{32,48},{48,32},{64,80},{80,64},{96,112},{112,96},{1... | collective-permute-start | bytes 589832 | tf_op jit(solution)/shard_map/ppermute | solution.py:49
  52.2 14.7 %all-to-all-start.1 = ((bf16[16,48,128]{2,1,0:T(8,128)(2,1)}), bf16[16,48,128]{2,1,0:T(8,128)(2,1)S(1)}, u32[]{:S(2)}, u32[]{:S(2)}) async-start(bf16[16,48,128]{2,1,0:T(8,128)(2,1)} %add_convert_fusion), calls=%async_computation.1 | async-start | bytes 393216 | tf_op jit(solution)/shard_map/all_to_all | solution.py:485

commit v6 on v5

--- a/solution.py
+++ b/solution.py
@@ -312,7 +312,7 @@
             there = lax.rem(here + n, ring)
             for j in range(blocks):
                 start = pl.multiple_of((j * ring + there) * width, width)
-                cut[n, j] = factor[:, pl.ds(start, width)].astype(BF16)
+                cut[n, j] = factor[:, pl.ds(start, width)]
             saves.append(pltpu.make_async_copy(cut.at[n], parts[n], sems.at[n]))
             saves[-1].start()
         total = None
@@ -322,7 +322,7 @@
                     vectors[a, b], rounded[a, b], (((1,), (1,)), ((), ())), preferred_element_type=F32
                 )
                 total = part if total is None else total + part
-        total = jnp.where(keep_mask(count, slots, rhs), total, 0.0).astype(BF16)
+        total = jnp.where(keep_mask(count, slots, rhs), total, 0.0)
         for i in range(copies):
             made[i] = total
         saves.append(pltpu.make_async_copy(made, spread, sems.at[ring]))
@@ -332,15 +332,15 @@
 
     return pl.pallas_call(
         body,
-        out_shape=[struct((copies, slots, rhs), BF16)] + [struct((blocks, slots, width), BF16)] * ring,
+        out_shape=[struct((copies, slots, rhs), F32)] + [struct((blocks, slots, width), F32)] * ring,
         in_specs=[SMEM, VMEM, VMEM, VMEM],
         out_specs=[HBM] * (1 + ring),
         scratch_shapes=[
-            pltpu.VMEM((copies, slots, rhs), BF16),
-            pltpu.VMEM((ring, blocks, slots, width), BF16),
+            pltpu.VMEM((copies, slots, rhs), F32),
+            pltpu.VMEM((ring, blocks, slots, width), F32),
             pltpu.SemaphoreType.DMA((1 + ring,)),
         ],
-        compiler_params=limit(6),
+        compiler_params=limit(8),
     )(counts, rounded, deflation, factor)
 
 
@@ -364,8 +364,11 @@
             for y in range(per):
                 a, b = mine[j * per + y], other[j * per + y]
                 pieces += [jnp.where(first, a, b), jnp.where(first, b, a)]
-            factor = jnp.concatenate([r[j] for r in rows], 0)
-            part = jnp.dot(factor, jnp.concatenate(pieces, 0), preferred_element_type=F32)
+            high, low = halves(jnp.concatenate([r[j] for r in rows], 0))
+            vector_high, vector_low = halves(jnp.concatenate(pieces, 0))
+            part = jnp.dot(high, vector_high, preferred_element_type=F32)
+            part = part + jnp.dot(high, vector_low, preferred_element_type=F32)
+            part = part + jnp.dot(low, vector_high, preferred_element_type=F32)
             total = part if total is None else total + part
         for n in range(sets):
             out[n] = total[n * slots : (n + 1) * slots]
@@ -398,19 +401,20 @@
         lowered_high, lowered_low = halves(jnp.concatenate(sums, 0))
         over = (((0,), (0,)), ((), ()))
         for j in range(blocks):
-            factor = jnp.concatenate([r[j] for r in rows], 0)
-            part = lax.dot_general(factor, lowered_high, over, preferred_element_type=F32)
-            part = part + lax.dot_general(factor, lowered_low, over, preferred_element_type=F32)
+            high, low = halves(jnp.concatenate([r[j] for r in rows], 0))
+            part = lax.dot_general(high, lowered_high, over, preferred_element_type=F32)
+            part = part + lax.dot_general(high, lowered_low, over, preferred_element_type=F32)
+            part = part + lax.dot_general(low, lowered_high, over, preferred_element_type=F32)
             for y in range(per):
                 a = part[2 * y * slots : (2 * y + 1) * slots]
                 b = part[(2 * y + 1) * slots : (2 * y + 2) * slots]
                 mine[j * per + y] = jnp.where(first, a, b)
-                other[j * per + y] = jnp.where(first, b, a).astype(BF16)
+                other[j * per + y] = jnp.where(first, b, a)
 
     shape = (blocks * per, slots, rhs)
     return pl.pallas_call(
         body,
-        out_shape=[struct(shape, F32), struct(shape, BF16)],
+        out_shape=[struct(shape, F32)] * 2,
         in_specs=[VMEM] * (2 * sets),
         out_specs=[VMEM, VMEM],
         compiler_params=limit(8),
@@ -474,14 +478,15 @@
         from_outer, from_pair = swap_outward(to_outer, n_sub), swap(to_pair, "c")
         gathered, _ = tie((gathered, to_outer))
         partial = lower(rows, gathered, swap(gathered, "c"))
-        received = [rotate(partial, RING, ring, n) for n in range(1, ring)]
+        moved = {n: rotate(partial, RING, ring, n) for n in (2, 1, 3)}
+        received = [moved[n] for n in range(1, ring)]
         own, _ = tie((own, partial))
         to_near, to_far = row_lines((own, ends, pair, outer), line_inverse, from_pair, from_outer)
-        partial, _ = tie((partial, to_near))
+        partial, received[1], received[0], received[2], _ = tie((partial, received[1], received[0], received[2], to_near))
         own_terms, other_terms = raise_back(rows, partial, received)
         to_near, to_far, other_terms = tie((to_near, to_far, other_terms))
         from_near, from_far = swap_pairs(to_near, GRP, n_grp, 0), swap_pairs(to_far, GRP, n_grp, 1)
-        terms_out = (own_terms + swap(other_terms, "c").astype(F32)).astype(BF16)
+        terms_out = own_terms + swap(other_terms, "c")
         terms_in = lax.all_to_all(terms_out, SPREAD, 0, 0)
         own, _ = tie((own, terms_out))
         inner = inner_lines((own, ends, pair, outer), line_inverse)

time: 68.8 us -> 79.4 us (1.15)
  the two profiles are of different devices: /device:TPU:0 before, /device:TPU:6 now
where the time goes in v6:
time: 79.4 us; the launch traced here: 78.9 us
  starting transfers between devices  32.2 us (41%)
  waiting for transfers between devices  21.4 us (27%)
  Pallas kernels  16.4 us (21%)
  local copies, waits for them, and re-layouts  7.2 us (9%)
  between operations  0.91 us (1%)
    ppermute x4, starting transfers between devices, swap_pairs(): return lax.ppermute(value, axes, pairs)  12.9 us
    pallas_call x3, Pallas kernels, line_solve(): pl.pallas_call(body, out_shape=shapes, in_specs=[ANY if fetch else VMEM]...  12.1 us
    ppermute x6, waiting for transfers between devices, rotate(): lax.ppermute(value, axes, [(i, (i + step) % size) for i in range(size)])  9.61 us
    unnamed x26, local copies, waits for them, and re-layouts  7.2 us
    all_to_all x1, starting transfers between devices, body(): gathered = lax.all_to_all(spread, SPREAD, 0, 0)  5.79 us
    ppermute x4, waiting for transfers between devices, swap_pairs(): return lax.ppermute(value, axes, pairs)  5.59 us
    ppermute x6, starting transfers between devices, rotate(): lax.ppermute(value, axes, [(i, (i + step) % size) for i in range(size)])  5.36 us
    ppermute x2, waiting for transfers between devices, swap_outward(): return lax.ppermute(value, SUB, pairs)  4.33 us
  transfers between devices with their start and end apart: 18, of which 8 were waited for; matrix products, arithmetic and copies ran while one was open for 0% of the time, Pallas kernels for 18%

profile of v6, /device:TPU:6, one launch (start us, length us, event | category | flops | bytes accessed | tf_op | source)
XLA Modules:
  0.0 78.9 jit_solution(15712047484646461321)
XLA Ops:
  0.0 1.1 %copy-done.1 = f32[2,2,128,384]{3,2,1,0:T(8,128)S(1)} copy-done((f32[2,2,128,384]{3,2,1,0:T(8,128)S(1)}, f32[2,2,128,384]{3,2,1,0:T(8,128)}, u32[]{:S(2)}) %copy-start.1) | copy-done | bytes 786456
  1.2 5.7 %collective-permute-start.1 = (bf16[1,2,128,384]{3,2,1,0:T(8,128)(2,1)S(1)}, bf16[1,2,128,384]{3,2,1,0:T(8,128)(2,1)S(1)}, u32[]{:S(2)}, u32[]{:S(2)}) collective-permute-start(bf16[1,2,128,384]{3,2,1,0:T(8,128)(2,1)S(1)} %get-tuple-element.45), channel_id=1, source_target_pairs={{16,32},{32,16},{48,64},{64,48},{80,96},{96,80},{17,33},{33,17},{4... | collective-permute-start | bytes 589832 | tf_op jit(solution)/shard_map/ppermute | solution.py:49
  7.7 1.3 %copy-done = f32[48,6144]{1,0:T(8,128)S(1)} copy-done((f32[48,6144]{1,0:T(8,128)S(1)}, f32[48,6144]{1,0:T(8,128)}, u32[]{:S(2)}) %copy-start) | copy-done | bytes 1179672
  8.9 0.9 %copy-done.2 = bf16[2,2,48,384]{3,2,1,0:T(8,128)(2,1)S(1)} copy-done((bf16[2,2,48,384]{3,2,1,0:T(8,128)(2,1)S(1)}, bf16[2,2,48,384]{3,2,1,0:T(8,128)(2,1)}, u32[]{:S(2)}) %copy-start.2) | copy-done | bytes 147480
  9.8 1.2 %shard_map.56 = (f32[16,48,128]{2,1,0:T(8,128)}, f32[2,48,768]{2,1,0:T(8,128)S(1)}, f32[2,48,768]{2,1,0:T(8,128)}, f32[2,48,768]{2,1,0:T(8,128)}, f32[2,48,768]{2,1,0:T(8,128)}) custom-call(s32[1,1]{1,0:T(1,128)S(6)} %copy.6.count, bf16[2,2,128,384]{3,2,1,0:T(8,128)(2,1)S(1)} %get-tuple-element.46.rounded, bf16[2,2,48,384]{3,2,1,0:T(8,128)(2,1)S(1)} %copy-done.2, ...), custom_call_target="tpu_custom_call" | custom-call | tf_op jit(solution)/shard_map/pallas_call | solution.py:333
  11.1 2.3 %collective-permute-done.1.far = bf16[1,2,128,384]{3,2,1,0:T(8,128)(2,1)S(1)} collective-permute-done((bf16[1,2,128,384]{3,2,1,0:T(8,128)(2,1)S(1)}, bf16[1,2,128,384]{3,2,1,0:T(8,128)(2,1)S(1)}, u32[]{:S(2)}, u32[]{:S(2)}) %collective-permute-start.1) | collective-permute-done | bytes 196640 | tf_op jit(solution)/shard_map/ppermute | solution.py:49
  13.6 0.7 copy-done.8
  14.3 2.9 %collective-permute-start.3 = (bf16[4,1,128,384]{3,2,1,0:T(8,128)(2,1)S(1)}, bf16[4,1,128,384]{3,2,1,0:T(8,128)(2,1)S(1)}, u32[]{:S(2)}, u32[]{:S(2)}) collective-permute-start(bf16[4,1,128,384]{3,2,1,0:T(8,128)(2,1)S(1)} %get-tuple-element.52), channel_id=1, source_target_pairs={{1,2},{2,1},{3,4},{4,3},{5,6},{6,5},{7,8},{8,7},{9,10},{10,9},{11,... | collective-permute-start | bytes 1179656 | tf_op jit(solution)/shard_map/ppermute | solution.py:56
  17.3 2.1 %collective-permute-start.5 = (f32[2,48,768]{2,1,0:T(8,128)}, f32[2,48,768]{2,1,0:T(8,128)S(1)}, u32[]{:S(2)}, u32[]{:S(2)}) collective-permute-start(f32[2,48,768]{2,1,0:T(8,128)} %get-tuple-element.54), channel_id=1, source_target_pairs={{0,16},{16,32},{32,48},{48,0},{1,17},{17,33},{33,49},{49,1},{2,18}... | collective-permute-start | bytes 884744 | tf_op jit(solution)/shard_map/ppermute | solution.py:38
  19.3 5.8 %all-to-all-start = ((f32[16,48,128]{2,1,0:T(8,128)}), f32[16,48,128]{2,1,0:T(8,128)S(1)}, u32[]{:S(2)}, u32[]{:S(2)}) async-start(f32[16,48,128]{2,1,0:T(8,128)} %get-tuple-element.63), calls=%async_computation | async-start | bytes 786432 | tf_op jit(solution)/shard_map/all_to_all | solution.py:474
  25.1 3.7 %collective-permute-done.4.refs_2_ = f32[2,48,768]{2,1,0:T(8,128)S(1)} collective-permute-done((f32[2,48,768]{2,1,0:T(8,128)}, f32[2,48,768]{2,1,0:T(8,128)S(1)}, u32[]{:S(2)}, u32[]{:S(2)}) %collective-permute-start.4) | collective-permute-done | bytes 294944 | tf_op jit(solution)/shard_map/ppermute | solution.py:38
  28.8 2.1 %collective-permute-done.5.refs_1_ = f32[2,48,768]{2,1,0:T(8,128)S(1)} collective-permute-done((f32[2,48,768]{2,1,0:T(8,128)}, f32[2,48,768]{2,1,0:T(8,128)S(1)}, u32[]{:S(2)}, u32[]{:S(2)}) %collective-permute-start.5) | collective-permute-done | bytes 294944 | tf_op jit(solution)/shard_map/ppermute | solution.py:38
  30.9 3.8 %collective-permute-done.6.refs_3_ = f32[2,48,768]{2,1,0:T(8,128)S(1)} collective-permute-done((f32[2,48,768]{2,1,0:T(8,128)}, f32[2,48,768]{2,1,0:T(8,128)S(1)}, u32[]{:S(2)}, u32[]{:S(2)}) %collective-permute-start.6) | collective-permute-done | bytes 294944 | tf_op jit(solution)/shard_map/ppermute | solution.py:38
  34.7 1.0 %copy-done.9 = bf16[2,2,128,384]{3,2,1,0:T(8,128)(2,1)S(1)} copy-done((bf16[2,2,128,384]{3,2,1,0:T(8,128)(2,1)S(1)}, bf16[2,2,128,384]{3,2,1,0:T(8,128)(2,1)}, u32[]{:S(2)}) %copy-start.9) | copy-done | bytes 393240
  35.7 5.7 %shard_map.58 = (bf16[4,1,128,384]{3,2,1,0:T(8,128)(2,1)S(1)}, bf16[4,1,128,384]{3,2,1,0:T(8,128)(2,1)S(1)}, bf16[2,2,128,384]{3,2,1,0:T(8,128)(2,1)S(1)}, bf16[2,2,128,384]{3,2,1,0:T(8,128)(2,1)S(1)}) custom-call(bf16[2,2,128,384]{3,2,1,0:T(8,128)(2,1)S(1)} %get-tuple-element.49.refs_0_, bf16[2,2,128,384]{3,2,1,0:T(8,128)(2,1)S(1)} %copy-done.9, ...), custom_call_target="tpu_custom_call" | custom-call | flops 1056964608 | bytes 8257536 | tf_op jit(solution)/shard_map/pallas_call | solution.py:154
  41.4 0.7 copy-done.10
  42.2 0.7 copy-done.11
  43.0 0.4 collective-permute-start.11
  43.4 1.1 %collective-permute-start.12 = (bf16[4,1,128,384]{3,2,1,0:T(8,128)(2,1)}, bf16[4,1,128,384]{3,2,1,0:T(8,128)(2,1)S(1)}, u32[]{:S(2)}, u32[]{:S(2)}) collective-permute-start(bf16[4,1,128,384]{3,2,1,0:T(8,128)(2,1)} %copy-done.10), channel_id=1, source_target_pairs={{1,2},{2,1},{3,4},{4,3},{5,6},{6,5},{7,8},{8,7},{9,10},{10,9},{11,... | collective-permute-start | bytes 1179656 | tf_op jit(solution)/shard_map/ppermute | solution.py:56
  44.6 0.7 shard_map.59.refs_4_
  45.4 3.2 %collective-permute-start.9 = (f32[4,48,128]{2,1,0:T(8,128)S(1)}, f32[4,48,128]{2,1,0:T(8,128)S(1)}, u32[]{:S(2)}, u32[]{:S(2)}) collective-permute-start(f32[4,48,128]{2,1,0:T(8,128)S(1)} %shard_map.59.refs_4_), channel_id=1, source_target_pairs={{0,16},{16,32},{32,48},{48,0},{1,17},{17,33},{33,49},{49,1},{2,18}... | collective-permute-start | bytes 294920 | tf_op jit(solution)/shard_map/ppermute | solution.py:38
  48.6 4.3 %collective-permute-done.12.refs_6_.from_outer = bf16[4,1,128,384]{3,2,1,0:T(8,128)(2,1)S(1)} collective-permute-done((bf16[4,1,128,384]{3,2,1,0:T(8,128)(2,1)}, bf16[4,1,128,384]{3,2,1,0:T(8,128)(2,1)S(1)}, u32[]{:S(2)}, u32[]{:S(2)}) %collective-permute-start.12) | collective-permute-done | bytes 393248 | tf_op jit(solution)/shard_map/ppermute | solution.py:56
  52.9 3.1 %shard_map.60 = (bf16[1,2,128,384]{3,2,1,0:T(8,128)(2,1)S(1)}, bf16[1,2,128,384]{3,2,1,0:T(8,128)(2,1)S(1)}) custom-call(bf16[2,2,128,384]{3,2,1,0:T(8,128)(2,1)S(1)} %get-tuple-element.78.refs_0_, bf16[2,2,128,384]{3,2,1,0:T(8,128)(2,1)S(1)} %get-tuple-element.67.refs_1_, bf16[4,1,128,384]{3,2,1,0:T(8,128)(2,1)S(1)} %collective-permute-done.2.refs_2_, ...), custom_call_target="tpu_custom_call" | custom-call | flops 603979776 | bytes 4718592 | tf_op jit(solution)/shard_map/pallas_call | solution.py:154
  56.1 0.6 copy-done.12
  56.7 0.8 %shard_map.61 = (f32[16,48,128]{2,1,0:T(8,128)S(1)}, f32[16,48,128]{2,1,0:T(8,128)S(1)}) custom-call(f32[2,48,768]{2,1,0:T(8,128)S(1)} %get-tuple-element.58.refs_0_, f32[2,48,768]{2,1,0:T(8,128)S(1)} %collective-permute-done.5.refs_1_, f32[2,48,768]{2,1,0:T(8,128)S(1)} %collective-permute-done.4.refs_2_, f32[2,48,768]{2,1,0:T(8,128)S(1)} %collective-permute-done.6.refs_3_, ...), custom_call_target="tpu_custom_call" | custom-call | tf_op jit(solution)/shard_map/pallas_call | solution.py:415
  57.7 1.7 %collective-permute-done.13 = f32[16,48,128]{2,1,0:T(8,128)S(1)} collective-permute-done((f32[16,48,128]{2,1,0:T(8,128)S(1)}, f32[16,48,128]{2,1,0:T(8,128)S(1)}, u32[]{:S(2)}, u32[]{:S(2)}) %collective-permute-start.13) | collective-permute-done | bytes 393248 | tf_op jit(solution)/shard_map/ppermute | solution.py:42
  59.4 0.8 %add.3 = f32[16,48,128]{2,1,0:T(8,128)} add(f32[16,48,128]{2,1,0:T(8,128)S(1)} %get-tuple-element.74, f32[16,48,128]{2,1,0:T(8,128)S(1)} %collective-permute-done.13) | non-fusion elementwise | flops 98304 | bytes 1179648 | tf_op jit(solution)/shard_map/add | solution.py:489
  60.2 3.6 %all-to-all-start.1 = ((f32[16,48,128]{2,1,0:T(8,128)}), f32[16,48,128]{2,1,0:T(8,128)S(1)}, u32[]{:S(2)}, u32[]{:S(2)}) async-start(f32[16,48,128]{2,1,0:T(8,128)} %add.3), calls=%async_computation.1 | async-start | bytes 786432 | tf_op jit(solution)/shard_map/all_to_all | solution.py:490
  63.8 7.0 %collective-permute-start.14 = (bf16[1,2,128,384]{3,2,1,0:T(8,128)(2,1)}, bf16[1,2,128,384]{3,2,1,0:T(8,128)(2,1)S(1)}, u32[]{:S(2)}, u32[]{:S(2)}) collective-permute-start(bf16[1,2,128,384]{3,2,1,0:T(8,128)(2,1)} %copy-done.12), channel_id=1, source_target_pairs={{16,32},{32,16},{48,64},{64,48},{80,96},{96,80},{17,33},{33,17},{4... | collective-permute-start | bytes 589832 | tf_op jit(solution)/shard_map/ppermute | solution.py:49
  70.9 3.3 %shard_map.62.inner = f32[2,2,128,384]{3,2,1,0:T(8,128)S(1)} custom-call(bf16[2,2,128,384]{3,2,1,0:T(8,128)(2,1)S(1)} %get-tuple-element.78.refs_0_, bf16[2,2,128,384]{3,2,1,0:T(8,128)(2,1)S(1)} %get-tuple-element.67.refs_1_, bf16[4,1,128,384]{3,2,1,0:T(8,128)(2,1)S(1)} %collective-permute-done.2.refs_2_, ...), custom_call_target="tpu_custom_call" | custom-call | flops 754974720 | bytes 5898240 | tf_op jit(solution)/shard_map/pallas_call | solution.py:154
  74.2 3.3 %collective-permute-done.14.from_far = bf16[1,2,128,384]{3,2,1,0:T(8,128)(2,1)S(1)} collective-permute-done((bf16[1,2,128,384]{3,2,1,0:T(8,128)(2,1)}, bf16[1,2,128,384]{3,2,1,0:T(8,128)(2,1)S(1)}, u32[]{:S(2)}, u32[]{:S(2)}) %collective-permute-start.14) | collective-permute-done | bytes 196640 | tf_op jit(solution)/shard_map/ppermute | solution.py:49
  77.8 1.1 %shard_map.64 = f32[2,2,128,384]{3,2,1,0:T(8,128)} custom-call(s32[1,1]{1,0:T(1,128)S(6)} %copy.6.count, f32[2,2,128,384]{3,2,1,0:T(8,128)S(1)} %shard_map.63.first_level, f32[16,48,128]{2,1,0:T(8,128)S(1)} %all-to-all-done.1.terms_in, bf16[2,2,48,384]{3,2,1,0:T(8,128)(2,1)S(1)} %copy-done.3), custom_call_target="tpu_custom_call" | custom-call | tf_op jit(solution)/shard_map/pallas_call | solution.py:445
  (41 shorter events, 1.0 us)
Async XLA Ops:
  0.0 1.1 %copy-start.1 = (f32[2,2,128,384]{3,2,1,0:T(8,128)S(1)}, f32[2,2,128,384]{3,2,1,0:T(8,128)}, u32[]{:S(2)}) copy-start(f32[2,2,128,384]{3,2,1,0:T(8,128)} %residual.1) | copy-start | bytes 2359300
  1.2 12.1 %collective-permute-start.1 = (bf16[1,2,128,384]{3,2,1,0:T(8,128)(2,1)S(1)}, bf16[1,2,128,384]{3,2,1,0:T(8,128)(2,1)S(1)}, u32[]{:S(2)}, u32[]{:S(2)}) collective-permute-start(bf16[1,2,128,384]{3,2,1,0:T(8,128)(2,1)S(1)} %get-tuple-element.45), channel_id=1, source_target_pairs={{16,32},{32,16},{48,64},{64,48},{80,96},{96,80},{17,33},{33,17},{4... | collective-permute-start | bytes 589832 | tf_op jit(solution)/shard_map/ppermute | solution.py:49
  6.9 6.4 %collective-permute-start = (bf16[1,2,128,384]{3,2,1,0:T(8,128)(2,1)S(1)}, bf16[1,2,128,384]{3,2,1,0:T(8,128)(2,1)S(1)}, u32[]{:S(2)}, u32[]{:S(2)}) collective-permute-start(bf16[1,2,128,384]{3,2,1,0:T(8,128)(2,1)S(1)} %get-tuple-element.44), channel_id=1, source_target_pairs={{0,16},{16,0},{32,48},{48,32},{64,80},{80,64},{96,112},{112,96},{1... | collective-permute-start | bytes 589832 | tf_op jit(solution)/shard_map/ppermute | solution.py:49
  7.7 1.3 %copy-start = (f32[48,6144]{1,0:T(8,128)S(1)}, f32[48,6144]{1,0:T(8,128)}, u32[]{:S(2)}) copy-start(f32[48,6144]{1,0:T(8,128)} %factor.1) | copy-start | bytes 3538948
  8.9 0.9 %copy-start.2 = (bf16[2,2,48,384]{3,2,1,0:T(8,128)(2,1)S(1)}, bf16[2,2,48,384]{3,2,1,0:T(8,128)(2,1)}, u32[]{:S(2)}) copy-start(bf16[2,2,48,384]{3,2,1,0:T(8,128)(2,1)} %vectors.3) | copy-start | bytes 442372
  13.6 0.7 copy-start.8
  14.3 20.4 %collective-permute-start.3 = (bf16[4,1,128,384]{3,2,1,0:T(8,128)(2,1)S(1)}, bf16[4,1,128,384]{3,2,1,0:T(8,128)(2,1)S(1)}, u32[]{:S(2)}, u32[]{:S(2)}) collective-permute-start(bf16[4,1,128,384]{3,2,1,0:T(8,128)(2,1)S(1)} %get-tuple-element.52), channel_id=1, source_target_pairs={{1,2},{2,1},{3,4},{4,3},{5,6},{6,5},{7,8},{8,7},{9,10},{10,9},{11,... | collective-permute-start | bytes 1179656 | tf_op jit(solution)/shard_map/ppermute | solution.py:56
  17.3 17.5 %collective-permute-start.2 = (bf16[4,1,128,384]{3,2,1,0:T(8,128)(2,1)S(1)}, bf16[4,1,128,384]{3,2,1,0:T(8,128)(2,1)S(1)}, u32[]{:S(2)}, u32[]{:S(2)}) collective-permute-start(bf16[4,1,128,384]{3,2,1,0:T(8,128)(2,1)S(1)} %get-tuple-element.51), channel_id=1, source_target_pairs={{0,1},{1,0},{2,3},{3,2},{4,5},{5,4},{6,7},{7,6},{8,9},{9,8},{10,11... | collective-permute-start | bytes 1179656 | tf_op jit(solution)/shard_map/ppermute | solution.py:42
  17.3 11.6 %collective-permute-start.4 = (f32[2,48,768]{2,1,0:T(8,128)}, f32[2,48,768]{2,1,0:T(8,128)S(1)}, u32[]{:S(2)}, u32[]{:S(2)}) collective-permute-start(f32[2,48,768]{2,1,0:T(8,128)} %get-tuple-element.53), channel_id=1, source_target_pairs={{0,32},{16,48},{32,0},{48,16},{1,33},{17,49},{33,1},{49,17},{2,34}... | collective-permute-start | bytes 884744 | tf_op jit(solution)/shard_map/ppermute | solution.py:38
  17.3 13.6 %collective-permute-start.5 = (f32[2,48,768]{2,1,0:T(8,128)}, f32[2,48,768]{2,1,0:T(8,128)S(1)}, u32[]{:S(2)}, u32[]{:S(2)}) collective-permute-start(f32[2,48,768]{2,1,0:T(8,128)} %get-tuple-element.54), channel_id=1, source_target_pairs={{0,16},{16,32},{32,48},{48,0},{1,17},{17,33},{33,49},{49,1},{2,18}... | collective-permute-start | bytes 884744 | tf_op jit(solution)/shard_map/ppermute | solution.py:38
  19.3 15.4 %collective-permute-start.6 = (f32[2,48,768]{2,1,0:T(8,128)}, f32[2,48,768]{2,1,0:T(8,128)S(1)}, u32[]{:S(2)}, u32[]{:S(2)}) collective-permute-start(f32[2,48,768]{2,1,0:T(8,128)} %get-tuple-element.55), channel_id=1, source_target_pairs={{0,48},{16,0},{32,16},{48,32},{1,49},{17,1},{33,17},{49,33},{2,50}... | collective-permute-start | bytes 884744 | tf_op jit(solution)/shard_map/ppermute | solution.py:38
  19.3 23.6 %all-to-all-start = ((f32[16,48,128]{2,1,0:T(8,128)}), f32[16,48,128]{2,1,0:T(8,128)S(1)}, u32[]{:S(2)}, u32[]{:S(2)}) async-start(f32[16,48,128]{2,1,0:T(8,128)} %get-tuple-element.63), calls=%async_computation | async-start | bytes 786432 | tf_op jit(solution)/shard_map/all_to_all | solution.py:474
  34.7 1.0 %copy-start.9 = (bf16[2,2,128,384]{3,2,1,0:T(8,128)(2,1)S(1)}, bf16[2,2,128,384]{3,2,1,0:T(8,128)(2,1)}, u32[]{:S(2)}) copy-start(bf16[2,2,128,384]{3,2,1,0:T(8,128)(2,1)} %copy-done.8) | copy-start | bytes 1179652
  41.4 0.8 copy-start.10
  42.2 0.7 copy-start.11
  42.9 1.7 %collective-permute-start.7 = (f32[16,48,128]{2,1,0:T(8,128)S(1)}, f32[16,48,128]{2,1,0:T(8,128)S(1)}, u32[]{:S(2)}, u32[]{:S(2)}) collective-permute-start(f32[16,48,128]{2,1,0:T(8,128)S(1)} %all-to-all-done.refs_4_), channel_id=1, source_target_pairs={{0,1},{1,0},{2,3},{3,2},{4,5},{5,4},{6,7},{7,6},{8,9},{9,8},{10,11... | collective-permute-start | bytes 1179656 | tf_op jit(solution)/shard_map/ppermute | solution.py:42
  43.0 5.6 %collective-permute-start.11 = (bf16[4,1,128,384]{3,2,1,0:T(8,128)(2,1)}, bf16[4,1,128,384]{3,2,1,0:T(8,128)(2,1)S(1)}, u32[]{:S(2)}, u32[]{:S(2)}) collective-permute-start(bf16[4,1,128,384]{3,2,1,0:T(8,128)(2,1)} %copy-done.11), channel_id=1, source_target_pairs={{0,1},{1,0},{2,3},{3,2},{4,5},{5,4},{6,7},{7,6},{8,9},{9,8},{10,11... | collective-permute-start | bytes 1179656 | tf_op jit(solution)/shard_map/ppermute | solution.py:42
  43.4 9.5 %collective-permute-start.12 = (bf16[4,1,128,384]{3,2,1,0:T(8,128)(2,1)}, bf16[4,1,128,384]{3,2,1,0:T(8,128)(2,1)S(1)}, u32[]{:S(2)}, u32[]{:S(2)}) collective-permute-start(bf16[4,1,128,384]{3,2,1,0:T(8,128)(2,1)} %copy-done.10), channel_id=1, source_target_pairs={{1,2},{2,1},{3,4},{4,3},{5,6},{6,5},{7,8},{8,7},{9,10},{10,9},{11,... | collective-permute-start | bytes 1179656 | tf_op jit(solution)/shard_map/ppermute | solution.py:56
  45.3 10.8 %collective-permute-start.10 = (f32[4,48,128]{2,1,0:T(8,128)S(1)}, f32[4,48,128]{2,1,0:T(8,128)S(1)}, u32[]{:S(2)}, u32[]{:S(2)}) collective-permute-start(f32[4,48,128]{2,1,0:T(8,128)S(1)} %shard_map.59.refs_4_), channel_id=1, source_target_pairs={{0,48},{16,0},{32,16},{48,32},{1,49},{17,1},{33,17},{49,33},{2,50}... | collective-permute-start | bytes 294920 | tf_op jit(solution)/shard_map/ppermute | solution.py:38
  45.4 10.7 %collective-permute-start.9 = (f32[4,48,128]{2,1,0:T(8,128)S(1)}, f32[4,48,128]{2,1,0:T(8,128)S(1)}, u32[]{:S(2)}, u32[]{:S(2)}) collective-permute-start(f32[4,48,128]{2,1,0:T(8,128)S(1)} %shard_map.59.refs_4_), channel_id=1, source_target_pairs={{0,16},{16,32},{32,48},{48,0},{1,17},{17,33},{33,49},{49,1},{2,18}... | collective-permute-start | bytes 294920 | tf_op jit(solution)/shard_map/ppermute | solution.py:38
  48.6 7.5 %collective-permute-start.8 = (f32[4,48,128]{2,1,0:T(8,128)S(1)}, f32[4,48,128]{2,1,0:T(8,128)S(1)}, u32[]{:S(2)}, u32[]{:S(2)}) collective-permute-start(f32[4,48,128]{2,1,0:T(8,128)S(1)} %shard_map.59.refs_4_), channel_id=1, source_target_pairs={{0,32},{16,48},{32,0},{48,16},{1,33},{17,49},{33,1},{49,17},{2,34}... | collective-permute-start | bytes 294920 | tf_op jit(solution)/shard_map/ppermute | solution.py:38
  48.6 9.0 %copy-start.4 = (bf16[4,1,128,384]{3,2,1,0:T(8,128)(2,1)}, bf16[4,1,128,384]{3,2,1,0:T(8,128)(2,1)S(1)}, u32[]{:S(2)}) copy-start(bf16[4,1,128,384]{3,2,1,0:T(8,128)(2,1)S(1)} %collective-permute-done.11.refs_5_.from_pair) | copy-start | bytes 1179652
  52.9 4.6 %copy-start.6 = (bf16[4,1,128,384]{3,2,1,0:T(8,128)(2,1)}, bf16[4,1,128,384]{3,2,1,0:T(8,128)(2,1)S(1)}, u32[]{:S(2)}) copy-start(bf16[4,1,128,384]{3,2,1,0:T(8,128)(2,1)S(1)} %collective-permute-done.12.refs_6_.from_outer) | copy-start | bytes 1179652
  52.9 24.8 %copy-start.3 = (bf16[2,2,48,384]{3,2,1,0:T(8,128)(2,1)S(1)}, bf16[2,2,48,384]{3,2,1,0:T(8,128)(2,1)}, u32[]{:S(2)}) copy-start(bf16[2,2,48,384]{3,2,1,0:T(8,128)(2,1)} %vectors.3) | copy-start | bytes 442372
  56.0 0.7 copy-start.12
  57.6 19.9 %copy-start.5 = (bf16[4,1,128,384]{3,2,1,0:T(8,128)(2,1)S(1)}, bf16[4,1,128,384]{3,2,1,0:T(8,128)(2,1)}, u32[]{:S(2)}) copy-start(bf16[4,1,128,384]{3,2,1,0:T(8,128)(2,1)} %copy-done.4) | copy-start | bytes 1179652
  57.6 19.9 %copy-start.7 = (bf16[4,1,128,384]{3,2,1,0:T(8,128)(2,1)S(1)}, bf16[4,1,128,384]{3,2,1,0:T(8,128)(2,1)}, u32[]{:S(2)}) copy-start(bf16[4,1,128,384]{3,2,1,0:T(8,128)(2,1)} %copy-done.6) | copy-start | bytes 1179652
  57.6 1.8 %collective-permute-start.13 = (f32[16,48,128]{2,1,0:T(8,128)S(1)}, f32[16,48,128]{2,1,0:T(8,128)S(1)}, u32[]{:S(2)}, u32[]{:S(2)}) collective-permute-start(f32[16,48,128]{2,1,0:T(8,128)S(1)} %get-tuple-element.77), channel_id=1, source_target_pairs={{0,1},{1,0},{2,3},{3,2},{4,5},{5,4},{6,7},{7,6},{8,9},{9,8},{10,11... | collective-permute-start | bytes 1179656 | tf_op jit(solution)/shard_map/ppermute | solution.py:42
  60.2 17.5 %all-to-all-start.1 = ((f32[16,48,128]{2,1,0:T(8,128)}), f32[16,48,128]{2,1,0:T(8,128)S(1)}, u32[]{:S(2)}, u32[]{:S(2)}) async-start(f32[16,48,128]{2,1,0:T(8,128)} %add.3), calls=%async_computation.1 | async-start | bytes 786432 | tf_op jit(solution)/shard_map/all_to_all | solution.py:490
  63.8 13.8 %collective-permute-start.14 = (bf16[1,2,128,384]{3,2,1,0:T(8,128)(2,1)}, bf16[1,2,128,384]{3,2,1,0:T(8,128)(2,1)S(1)}, u32[]{:S(2)}, u32[]{:S(2)}) collective-permute-start(bf16[1,2,128,384]{3,2,1,0:T(8,128)(2,1)} %copy-done.12), channel_id=1, source_target_pairs={{16,32},{32,16},{48,64},{64,48},{80,96},{96,80},{17,33},{33,17},{4... | collective-permute-start | bytes 589832 | tf_op jit(solution)/shard_map/ppermute | solution.py:49
  70.8 6.7 %collective-permute-start.15 = (bf16[1,2,128,384]{3,2,1,0:T(8,128)(2,1)S(1)}, bf16[1,2,128,384]{3,2,1,0:T(8,128)(2,1)S(1)}, u32[]{:S(2)}, u32[]{:S(2)}) collective-permute-start(bf16[1,2,128,384]{3,2,1,0:T(8,128)(2,1)S(1)} %get-tuple-element.81), channel_id=1, source_target_pairs={{0,16},{16,0},{32,48},{48,32},{64,80},{80,64},{96,112},{112,96},{1... | collective-permute-start | bytes 589832 | tf_op jit(solution)/shard_map/ppermute | solution.py:49

commit v7 on v5

--- a/solution.py
+++ b/solution.py
@@ -474,10 +474,11 @@
         from_outer, from_pair = swap_outward(to_outer, n_sub), swap(to_pair, "c")
         gathered, _ = tie((gathered, to_outer))
         partial = lower(rows, gathered, swap(gathered, "c"))
-        received = [rotate(partial, RING, ring, n) for n in range(1, ring)]
+        moved = {n: rotate(partial, RING, ring, n) for n in (2, 1, 3)}
+        received = [moved[n] for n in range(1, ring)]
         own, _ = tie((own, partial))
         to_near, to_far = row_lines((own, ends, pair, outer), line_inverse, from_pair, from_outer)
-        partial, _ = tie((partial, to_near))
+        partial, received[1], received[0], received[2], _ = tie((partial, received[1], received[0], received[2], to_near))
         own_terms, other_terms = raise_back(rows, partial, received)
         to_near, to_far, other_terms = tie((to_near, to_far, other_terms))
         from_near, from_far = swap_pairs(to_near, GRP, n_grp, 0), swap_pairs(to_far, GRP, n_grp, 1)

time: 68.8 us -> 68.5 us (level)
  waiting for transfers between devices: 10.1 us -> 9.25 us
where the time goes in v7:
time: 68.5 us; the launch traced here: 67.8 us
  starting transfers between devices  37.1 us (54%)
  Pallas kernels  16.5 us (24%)
  waiting for transfers between devices  9.25 us (14%)
  local copies, waits for them, and re-layouts  3.31 us (5%)
  between operations  0.83 us (1%)
  other arithmetic  0.73 us (1%)
    pallas_call x3, Pallas kernels, line_solve(): pl.pallas_call(body, out_shape=shapes, in_specs=[ANY if fetch else VMEM]...  12.3 us
    ppermute x6, starting transfers between devices, rotate(): lax.ppermute(value, axes, [(i, (i + step) % size) for i in range(size)])  11.8 us
    ppermute x4, starting transfers between devices, swap_pairs(): return lax.ppermute(value, axes, pairs)  8.04 us
    all_to_all x1, starting transfers between devices, body(): terms_in = lax.all_to_all(terms_out, SPREAD, 0, 0)  6.45 us
    ppermute x2, starting transfers between devices, swap_outward(): return lax.ppermute(value, SUB, pairs)  5.99 us
    all_to_all x1, waiting for transfers between devices, body(): terms_in = lax.all_to_all(terms_out, SPREAD, 0, 0)  4.79 us
    all_to_all x1, starting transfers between devices, body(): gathered = lax.all_to_all(spread, SPREAD, 0, 0)  4.7 us
    unnamed x8, local copies, waits for them, and re-layouts  3.31 us
  transfers between devices with their start and end apart: 18, of which 6 were waited for; matrix products, arithmetic and copies ran while one was open for 1% of the time, Pallas kernels for 21%

profile of v7, /device:TPU:0, one launch (start us, length us, event | category | flops | bytes accessed | tf_op | source)
XLA Modules:
  0.0 67.8 jit_solution(13576488902749805096)
XLA Ops:
  0.0 1.1 %copy-done.1 = f32[2,2,128,384]{3,2,1,0:T(8,128)S(1)} copy-done((f32[2,2,128,384]{3,2,1,0:T(8,128)S(1)}, f32[2,2,128,384]{3,2,1,0:T(8,128)}, u32[]{:S(2)}) %copy-start.1) | copy-done | bytes 786456
  1.2 0.7 collective-permute-start.1
  1.9 4.4 %collective-permute-start = (bf16[1,2,128,384]{3,2,1,0:T(8,128)(2,1)S(1)}, bf16[1,2,128,384]{3,2,1,0:T(8,128)(2,1)S(1)}, u32[]{:S(2)}, u32[]{:S(2)}) collective-permute-start(bf16[1,2,128,384]{3,2,1,0:T(8,128)(2,1)S(1)} %get-tuple-element.44), channel_id=1, source_target_pairs={{0,16},{16,0},{32,48},{48,32},{64,80},{80,64},{96,112},{112,96},{1... | collective-permute-start | bytes 589832 | tf_op jit(solution)/shard_map/ppermute | solution.py:49
  6.9 1.3 %copy-done = f32[48,6144]{1,0:T(8,128)S(1)} copy-done((f32[48,6144]{1,0:T(8,128)S(1)}, f32[48,6144]{1,0:T(8,128)}, u32[]{:S(2)}) %copy-start) | copy-done | bytes 1179672
  8.2 0.9 %copy-done.2 = bf16[2,2,48,384]{3,2,1,0:T(8,128)(2,1)S(1)} copy-done((bf16[2,2,48,384]{3,2,1,0:T(8,128)(2,1)S(1)}, bf16[2,2,48,384]{3,2,1,0:T(8,128)(2,1)}, u32[]{:S(2)}) %copy-start.2) | copy-done | bytes 147480
  9.1 1.7 %shard_map.56 = (bf16[16,48,128]{2,1,0:T(8,128)(2,1)}, bf16[2,48,768]{2,1,0:T(8,128)(2,1)S(1)}, bf16[2,48,768]{2,1,0:T(8,128)(2,1)S(1)}, bf16[2,48,768]{2,1,0:T(8,128)(2,1)}, bf16[2,48,768]{2,1,0:T(8,128)(2,1)S(1)}) custom-call(s32[1,1]{1,0:T(1,128)S(6)} %copy.6.count, bf16[2,2,128,384]{3,2,1,0:T(8,128)(2,1)S(1)} %get-tuple-element.46.rounded, ...), custom_call_target="tpu_custom_call" | custom-call | tf_op jit(solution)/shard_map/pallas_call | solution.py:333
  10.9 0.2 shard_map.57
  11.1 3.2 %collective-permute-start.3 = (bf16[4,1,128,384]{3,2,1,0:T(8,128)(2,1)S(1)}, bf16[4,1,128,384]{3,2,1,0:T(8,128)(2,1)S(1)}, u32[]{:S(2)}, u32[]{:S(2)}) collective-permute-start(bf16[4,1,128,384]{3,2,1,0:T(8,128)(2,1)S(1)} %get-tuple-element.52), channel_id=1, source_target_pairs={{1,2},{2,1},{3,4},{4,3},{5,6},{6,5},{7,8},{8,7},{9,10},{10,9},{11,... | collective-permute-start | bytes 1179656 | tf_op jit(solution)/shard_map/ppermute | solution.py:56
  14.3 4.1 %collective-permute-start.4 = (bf16[2,48,768]{2,1,0:T(8,128)(2,1)}, bf16[2,48,768]{2,1,0:T(8,128)(2,1)S(1)}, u32[]{:S(2)}, u32[]{:S(2)}) collective-permute-start(bf16[2,48,768]{2,1,0:T(8,128)(2,1)} %get-tuple-element.53), channel_id=1, source_target_pairs={{0,32},{16,48},{32,0},{48,16},{1,33},{17,49},{33,1},{49,17},{2,34}... | collective-permute-start | bytes 442376 | tf_op jit(solution)/shard_map/ppermute | solution.py:38
  18.5 1.8 %collective-permute-start.5 = (bf16[2,48,768]{2,1,0:T(8,128)(2,1)S(1)}, bf16[2,48,768]{2,1,0:T(8,128)(2,1)S(1)}, u32[]{:S(2)}, u32[]{:S(2)}) collective-permute-start(bf16[2,48,768]{2,1,0:T(8,128)(2,1)S(1)} %get-tuple-element.54), channel_id=1, source_target_pairs={{0,16},{16,32},{32,48},{48,0},{1,17},{17,33},{33,49},{49,1},{2,18}... | collective-permute-start | bytes 442376 | tf_op jit(solution)/shard_map/ppermute | solution.py:38
  20.3 1.4 %collective-permute-start.6 = (bf16[2,48,768]{2,1,0:T(8,128)(2,1)S(1)}, bf16[2,48,768]{2,1,0:T(8,128)(2,1)S(1)}, u32[]{:S(2)}, u32[]{:S(2)}) collective-permute-start(bf16[2,48,768]{2,1,0:T(8,128)(2,1)S(1)} %get-tuple-element.55), channel_id=1, source_target_pairs={{0,48},{16,0},{32,16},{48,32},{1,49},{17,1},{33,17},{49,33},{2,50}... | collective-permute-start | bytes 442376 | tf_op jit(solution)/shard_map/ppermute | solution.py:38
  21.7 4.7 %all-to-all-start = ((bf16[16,48,128]{2,1,0:T(8,128)(2,1)}), bf16[16,48,128]{2,1,0:T(8,128)(2,1)S(1)}, u32[]{:S(2)}, u32[]{:S(2)}) async-start(bf16[16,48,128]{2,1,0:T(8,128)(2,1)} %get-tuple-element.63), calls=%async_computation | async-start | bytes 393216 | tf_op jit(solution)/shard_map/all_to_all | solution.py:470
  26.4 1.4 %collective-permute-done.6.refs_3_ = bf16[2,48,768]{2,1,0:T(8,128)(2,1)S(1)} collective-permute-done((bf16[2,48,768]{2,1,0:T(8,128)(2,1)S(1)}, bf16[2,48,768]{2,1,0:T(8,128)(2,1)S(1)}, u32[]{:S(2)}, u32[]{:S(2)}) %collective-permute-start.6) | collective-permute-done | bytes 147488 | tf_op jit(solution)/shard_map/ppermute | solution.py:38
  27.9 5.3 %shard_map.58 = (bf16[4,1,128,384]{3,2,1,0:T(8,128)(2,1)}, bf16[4,1,128,384]{3,2,1,0:T(8,128)(2,1)}, bf16[2,2,128,384]{3,2,1,0:T(8,128)(2,1)S(1)}, bf16[2,2,128,384]{3,2,1,0:T(8,128)(2,1)S(1)}) custom-call(bf16[2,2,128,384]{3,2,1,0:T(8,128)(2,1)S(1)} %get-tuple-element.49.refs_0_, bf16[2,2,128,384]{3,2,1,0:T(8,128)(2,1)S(1)} %get-tuple-element.50.refs_1_, ...), custom_call_target="tpu_custom_call" | custom-call | flops 1056964608 | bytes 8257536 | tf_op jit(solution)/shard_map/pallas_call | solution.py:154
  33.3 2.7 %collective-permute-start.12 = (bf16[4,1,128,384]{3,2,1,0:T(8,128)(2,1)}, bf16[4,1,128,384]{3,2,1,0:T(8,128)(2,1)S(1)}, u32[]{:S(2)}, u32[]{:S(2)}) collective-permute-start(bf16[4,1,128,384]{3,2,1,0:T(8,128)(2,1)} %get-tuple-element.64), channel_id=1, source_target_pairs={{1,2},{2,1},{3,4},{4,3},{5,6},{6,5},{7,8},{8,7},{9,10},{10,9},{11,... | collective-permute-start | bytes 1179656 | tf_op jit(solution)/shard_map/ppermute | solution.py:56
  36.1 1.4 %collective-permute-done.7.refs_5_ = bf16[16,48,128]{2,1,0:T(8,128)(2,1)S(1)} collective-permute-done((bf16[16,48,128]{2,1,0:T(8,128)(2,1)S(1)}, bf16[16,48,128]{2,1,0:T(8,128)(2,1)S(1)}, u32[]{:S(2)}, u32[]{:S(2)}) %collective-permute-start.7) | collective-permute-done | bytes 196640 | tf_op jit(solution)/shard_map/ppermute | solution.py:42
  37.5 0.3 shard_map.59.refs_4_
  37.8 1.6 %collective-permute-start.10 = (f32[4,48,128]{2,1,0:T(8,128)S(1)}, f32[4,48,128]{2,1,0:T(8,128)S(1)}, u32[]{:S(2)}, u32[]{:S(2)}) collective-permute-start(f32[4,48,128]{2,1,0:T(8,128)S(1)} %shard_map.59.refs_4_), channel_id=1, source_target_pairs={{0,48},{16,0},{32,16},{48,32},{1,49},{17,1},{33,17},{49,33},{2,50}... | collective-permute-start | bytes 294920 | tf_op jit(solution)/shard_map/ppermute | solution.py:38
  39.5 0.5 collective-permute-start.9
  39.9 2.3 %collective-permute-start.8 = (f32[4,48,128]{2,1,0:T(8,128)S(1)}, f32[4,48,128]{2,1,0:T(8,128)S(1)}, u32[]{:S(2)}, u32[]{:S(2)}) collective-permute-start(f32[4,48,128]{2,1,0:T(8,128)S(1)} %shard_map.59.refs_4_), channel_id=1, source_target_pairs={{0,32},{16,48},{32,0},{48,16},{1,33},{17,49},{33,1},{49,17},{2,34}... | collective-permute-start | bytes 294920 | tf_op jit(solution)/shard_map/ppermute | solution.py:38
  42.2 0.7 %collective-permute-done.12.refs_6_.from_outer = bf16[4,1,128,384]{3,2,1,0:T(8,128)(2,1)S(1)} collective-permute-done((bf16[4,1,128,384]{3,2,1,0:T(8,128)(2,1)}, bf16[4,1,128,384]{3,2,1,0:T(8,128)(2,1)S(1)}, u32[]{:S(2)}, u32[]{:S(2)}) %collective-permute-start.12) | collective-permute-done | bytes 393248 | tf_op jit(solution)/shard_map/ppermute | solution.py:56
  42.9 3.6 %shard_map.60 = (bf16[1,2,128,384]{3,2,1,0:T(8,128)(2,1)S(1)}, bf16[1,2,128,384]{3,2,1,0:T(8,128)(2,1)}) custom-call(bf16[2,2,128,384]{3,2,1,0:T(8,128)(2,1)S(1)} %get-tuple-element.78.refs_0_, bf16[2,2,128,384]{3,2,1,0:T(8,128)(2,1)S(1)} %get-tuple-element.67.refs_1_, bf16[4,1,128,384]{3,2,1,0:T(8,128)(2,1)S(1)} %collective-permute-done.2.refs_2_, ...), custom_call_target="tpu_custom_call" | custom-call | flops 603979776 | bytes 4718592 | tf_op jit(solution)/shard_map/pallas_call | solution.py:154
  46.6 0.8 %collective-permute-done.9.refs_5_ = f32[4,48,128]{2,1,0:T(8,128)S(1)} collective-permute-done((f32[4,48,128]{2,1,0:T(8,128)S(1)}, f32[4,48,128]{2,1,0:T(8,128)S(1)}, u32[]{:S(2)}, u32[]{:S(2)}) %collective-permute-start.9) | collective-permute-done | bytes 98336 | tf_op jit(solution)/shard_map/ppermute | solution.py:38
  47.4 0.6 shard_map.61
  48.1 0.7 collective-permute-start.14
  48.8 2.3 %collective-permute-start.15 = (bf16[1,2,128,384]{3,2,1,0:T(8,128)(2,1)S(1)}, bf16[1,2,128,384]{3,2,1,0:T(8,128)(2,1)S(1)}, u32[]{:S(2)}, u32[]{:S(2)}) collective-permute-start(bf16[1,2,128,384]{3,2,1,0:T(8,128)(2,1)S(1)} %get-tuple-element.81), channel_id=1, source_target_pairs={{0,16},{16,0},{32,48},{48,32},{64,80},{80,64},{96,112},{112,96},{1... | collective-permute-start | bytes 589832 | tf_op jit(solution)/shard_map/ppermute | solution.py:49
  51.1 0.7 %add_convert_fusion = bf16[16,48,128]{2,1,0:T(8,128)(2,1)} fusion(f32[16,48,128]{2,1,0:T(8,128)S(1)} %get-tuple-element.74, bf16[16,48,128]{2,1,0:T(8,128)(2,1)S(1)} %collective-permute-done.13), kind=kLoop, calls=%fused_computation | loop fusion | flops 294912 | bytes 786432 | tf_op jit(solution)/shard_map/convert_element_type | solution.py:485
  51.8 6.5 %all-to-all-start.1 = ((bf16[16,48,128]{2,1,0:T(8,128)(2,1)}), bf16[16,48,128]{2,1,0:T(8,128)(2,1)S(1)}, u32[]{:S(2)}, u32[]{:S(2)}) async-start(bf16[16,48,128]{2,1,0:T(8,128)(2,1)} %add_convert_fusion), calls=%async_computation.1 | async-start | bytes 393216 | tf_op jit(solution)/shard_map/all_to_all | solution.py:486
  58.3 3.3 %shard_map.62.inner = f32[2,2,128,384]{3,2,1,0:T(8,128)S(1)} custom-call(bf16[2,2,128,384]{3,2,1,0:T(8,128)(2,1)S(1)} %get-tuple-element.78.refs_0_, bf16[2,2,128,384]{3,2,1,0:T(8,128)(2,1)S(1)} %get-tuple-element.67.refs_1_, bf16[4,1,128,384]{3,2,1,0:T(8,128)(2,1)S(1)} %collective-permute-done.2.refs_2_, ...), custom_call_target="tpu_custom_call" | custom-call | flops 754974720 | bytes 5898240 | tf_op jit(solution)/shard_map/pallas_call | solution.py:154
  61.6 0.2 shard_map.63.first_level
  61.8 4.8 %all-to-all-done.1.terms_in = bf16[16,48,128]{2,1,0:T(8,128)(2,1)S(1)} async-done(((bf16[16,48,128]{2,1,0:T(8,128)(2,1)}), bf16[16,48,128]{2,1,0:T(8,128)(2,1)S(1)}, u32[]{:S(2)}, u32[]{:S(2)}) %all-to-all-start.1) | async-done | bytes 196640 | tf_op jit(solution)/shard_map/all_to_all | solution.py:486
  66.6 1.1 %shard_map.64 = f32[2,2,128,384]{3,2,1,0:T(8,128)} custom-call(s32[1,1]{1,0:T(1,128)S(6)} %copy.6.count, f32[2,2,128,384]{3,2,1,0:T(8,128)S(1)} %shard_map.63.first_level, bf16[16,48,128]{2,1,0:T(8,128)(2,1)S(1)} %all-to-all-done.1.terms_in, bf16[2,2,48,384]{3,2,1,0:T(8,128)(2,1)S(1)} %copy-done.3), custom_call_target="tpu_custom_call" | custom-call | tf_op jit(solution)/shard_map/pallas_call | solution.py:441
  (23 shorter events, 0.4 us)
Async XLA Ops:
  0.0 1.1 %copy-start.1 = (f32[2,2,128,384]{3,2,1,0:T(8,128)S(1)}, f32[2,2,128,384]{3,2,1,0:T(8,128)}, u32[]{:S(2)}) copy-start(f32[2,2,128,384]{3,2,1,0:T(8,128)} %residual.1) | copy-start | bytes 2359300
  1.2 9.6 %collective-permute-start.1 = (bf16[1,2,128,384]{3,2,1,0:T(8,128)(2,1)S(1)}, bf16[1,2,128,384]{3,2,1,0:T(8,128)(2,1)S(1)}, u32[]{:S(2)}, u32[]{:S(2)}) collective-permute-start(bf16[1,2,128,384]{3,2,1,0:T(8,128)(2,1)S(1)} %get-tuple-element.45), channel_id=1, source_target_pairs={{16,32},{32,16},{48,64},{64,48},{80,96},{96,80},{17,33},{33,17},{4... | collective-permute-start | bytes 589832 | tf_op jit(solution)/shard_map/ppermute | solution.py:49
  1.9 9.0 %collective-permute-start = (bf16[1,2,128,384]{3,2,1,0:T(8,128)(2,1)S(1)}, bf16[1,2,128,384]{3,2,1,0:T(8,128)(2,1)S(1)}, u32[]{:S(2)}, u32[]{:S(2)}) collective-permute-start(bf16[1,2,128,384]{3,2,1,0:T(8,128)(2,1)S(1)} %get-tuple-element.44), channel_id=1, source_target_pairs={{0,16},{16,0},{32,48},{48,32},{64,80},{80,64},{96,112},{112,96},{1... | collective-permute-start | bytes 589832 | tf_op jit(solution)/shard_map/ppermute | solution.py:49
  6.9 1.3 %copy-start = (f32[48,6144]{1,0:T(8,128)S(1)}, f32[48,6144]{1,0:T(8,128)}, u32[]{:S(2)}) copy-start(f32[48,6144]{1,0:T(8,128)} %factor.1) | copy-start | bytes 3538948
  8.2 0.9 %copy-start.2 = (bf16[2,2,48,384]{3,2,1,0:T(8,128)(2,1)S(1)}, bf16[2,2,48,384]{3,2,1,0:T(8,128)(2,1)}, u32[]{:S(2)}) copy-start(bf16[2,2,48,384]{3,2,1,0:T(8,128)(2,1)} %vectors.3) | copy-start | bytes 442372
  11.1 16.8 %collective-permute-start.3 = (bf16[4,1,128,384]{3,2,1,0:T(8,128)(2,1)S(1)}, bf16[4,1,128,384]{3,2,1,0:T(8,128)(2,1)S(1)}, u32[]{:S(2)}, u32[]{:S(2)}) collective-permute-start(bf16[4,1,128,384]{3,2,1,0:T(8,128)(2,1)S(1)} %get-tuple-element.52), channel_id=1, source_target_pairs={{1,2},{2,1},{3,4},{4,3},{5,6},{6,5},{7,8},{8,7},{9,10},{10,9},{11,... | collective-permute-start | bytes 1179656 | tf_op jit(solution)/shard_map/ppermute | solution.py:56
  14.3 13.6 %collective-permute-start.2 = (bf16[4,1,128,384]{3,2,1,0:T(8,128)(2,1)S(1)}, bf16[4,1,128,384]{3,2,1,0:T(8,128)(2,1)S(1)}, u32[]{:S(2)}, u32[]{:S(2)}) collective-permute-start(bf16[4,1,128,384]{3,2,1,0:T(8,128)(2,1)S(1)} %get-tuple-element.51), channel_id=1, source_target_pairs={{0,1},{1,0},{2,3},{3,2},{4,5},{5,4},{6,7},{7,6},{8,9},{9,8},{10,11... | collective-permute-start | bytes 1179656 | tf_op jit(solution)/shard_map/ppermute | solution.py:42
  14.3 12.1 %collective-permute-start.4 = (bf16[2,48,768]{2,1,0:T(8,128)(2,1)}, bf16[2,48,768]{2,1,0:T(8,128)(2,1)S(1)}, u32[]{:S(2)}, u32[]{:S(2)}) collective-permute-start(bf16[2,48,768]{2,1,0:T(8,128)(2,1)} %get-tuple-element.53), channel_id=1, source_target_pairs={{0,32},{16,48},{32,0},{48,16},{1,33},{17,49},{33,1},{49,17},{2,34}... | collective-permute-start | bytes 442376 | tf_op jit(solution)/shard_map/ppermute | solution.py:38
  18.5 8.0 %collective-permute-start.5 = (bf16[2,48,768]{2,1,0:T(8,128)(2,1)S(1)}, bf16[2,48,768]{2,1,0:T(8,128)(2,1)S(1)}, u32[]{:S(2)}, u32[]{:S(2)}) collective-permute-start(bf16[2,48,768]{2,1,0:T(8,128)(2,1)S(1)} %get-tuple-element.54), channel_id=1, source_target_pairs={{0,16},{16,32},{32,48},{48,0},{1,17},{17,33},{33,49},{49,1},{2,18}... | collective-permute-start | bytes 442376 | tf_op jit(solution)/shard_map/ppermute | solution.py:38
  20.3 7.6 %collective-permute-start.6 = (bf16[2,48,768]{2,1,0:T(8,128)(2,1)S(1)}, bf16[2,48,768]{2,1,0:T(8,128)(2,1)S(1)}, u32[]{:S(2)}, u32[]{:S(2)}) collective-permute-start(bf16[2,48,768]{2,1,0:T(8,128)(2,1)S(1)} %get-tuple-element.55), channel_id=1, source_target_pairs={{0,48},{16,0},{32,16},{48,32},{1,49},{17,1},{33,17},{49,33},{2,50}... | collective-permute-start | bytes 442376 | tf_op jit(solution)/shard_map/ppermute | solution.py:38
  21.7 14.4 %all-to-all-start = ((bf16[16,48,128]{2,1,0:T(8,128)(2,1)}), bf16[16,48,128]{2,1,0:T(8,128)(2,1)S(1)}, u32[]{:S(2)}, u32[]{:S(2)}) async-start(bf16[16,48,128]{2,1,0:T(8,128)(2,1)} %get-tuple-element.63), calls=%async_computation | async-start | bytes 393216 | tf_op jit(solution)/shard_map/all_to_all | solution.py:470
  33.2 9.0 %collective-permute-start.11 = (bf16[4,1,128,384]{3,2,1,0:T(8,128)(2,1)}, bf16[4,1,128,384]{3,2,1,0:T(8,128)(2,1)S(1)}, u32[]{:S(2)}, u32[]{:S(2)}) collective-permute-start(bf16[4,1,128,384]{3,2,1,0:T(8,128)(2,1)} %get-tuple-element.68), channel_id=1, source_target_pairs={{0,1},{1,0},{2,3},{3,2},{4,5},{5,4},{6,7},{7,6},{8,9},{9,8},{10,11... | collective-permute-start | bytes 1179656 | tf_op jit(solution)/shard_map/ppermute | solution.py:42
  33.3 9.6 %collective-permute-start.12 = (bf16[4,1,128,384]{3,2,1,0:T(8,128)(2,1)}, bf16[4,1,128,384]{3,2,1,0:T(8,128)(2,1)S(1)}, u32[]{:S(2)}, u32[]{:S(2)}) collective-permute-start(bf16[4,1,128,384]{3,2,1,0:T(8,128)(2,1)} %get-tuple-element.64), channel_id=1, source_target_pairs={{1,2},{2,1},{3,4},{4,3},{5,6},{6,5},{7,8},{8,7},{9,10},{10,9},{11,... | collective-permute-start | bytes 1179656 | tf_op jit(solution)/shard_map/ppermute | solution.py:56
  36.1 1.4 %collective-permute-start.7 = (bf16[16,48,128]{2,1,0:T(8,128)(2,1)S(1)}, bf16[16,48,128]{2,1,0:T(8,128)(2,1)S(1)}, u32[]{:S(2)}, u32[]{:S(2)}) collective-permute-start(bf16[16,48,128]{2,1,0:T(8,128)(2,1)S(1)} %all-to-all-done.refs_4_), channel_id=1, source_target_pairs={{0,1},{1,0},{2,3},{3,2},{4,5},{5,4},{6,7},{7,6},{8,9},{9,8},{10,11... | collective-permute-start | bytes 589832 | tf_op jit(solution)/shard_map/ppermute | solution.py:42
  37.8 8.8 %collective-permute-start.10 = (f32[4,48,128]{2,1,0:T(8,128)S(1)}, f32[4,48,128]{2,1,0:T(8,128)S(1)}, u32[]{:S(2)}, u32[]{:S(2)}) collective-permute-start(f32[4,48,128]{2,1,0:T(8,128)S(1)} %shard_map.59.refs_4_), channel_id=1, source_target_pairs={{0,48},{16,0},{32,16},{48,32},{1,49},{17,1},{33,17},{49,33},{2,50}... | collective-permute-start | bytes 294920 | tf_op jit(solution)/shard_map/ppermute | solution.py:38
  39.5 7.9 %collective-permute-start.9 = (f32[4,48,128]{2,1,0:T(8,128)S(1)}, f32[4,48,128]{2,1,0:T(8,128)S(1)}, u32[]{:S(2)}, u32[]{:S(2)}) collective-permute-start(f32[4,48,128]{2,1,0:T(8,128)S(1)} %shard_map.59.refs_4_), channel_id=1, source_target_pairs={{0,16},{16,32},{32,48},{48,0},{1,17},{17,33},{33,49},{49,1},{2,18}... | collective-permute-start | bytes 294920 | tf_op jit(solution)/shard_map/ppermute | solution.py:38
  39.9 7.4 %collective-permute-start.8 = (f32[4,48,128]{2,1,0:T(8,128)S(1)}, f32[4,48,128]{2,1,0:T(8,128)S(1)}, u32[]{:S(2)}, u32[]{:S(2)}) collective-permute-start(f32[4,48,128]{2,1,0:T(8,128)S(1)} %shard_map.59.refs_4_), channel_id=1, source_target_pairs={{0,32},{16,48},{32,0},{48,16},{1,33},{17,49},{33,1},{49,17},{2,34}... | collective-permute-start | bytes 294920 | tf_op jit(solution)/shard_map/ppermute | solution.py:38
  42.9 23.7 %copy-start.3 = (bf16[2,2,48,384]{3,2,1,0:T(8,128)(2,1)S(1)}, bf16[2,2,48,384]{3,2,1,0:T(8,128)(2,1)}, u32[]{:S(2)}) copy-start(bf16[2,2,48,384]{3,2,1,0:T(8,128)(2,1)} %vectors.3) | copy-start | bytes 442372
  48.0 3.1 %collective-permute-start.13 = (bf16[16,48,128]{2,1,0:T(8,128)(2,1)S(1)}, bf16[16,48,128]{2,1,0:T(8,128)(2,1)S(1)}, u32[]{:S(2)}, u32[]{:S(2)}) collective-permute-start(bf16[16,48,128]{2,1,0:T(8,128)(2,1)S(1)} %get-tuple-element.77), channel_id=1, source_target_pairs={{0,1},{1,0},{2,3},{3,2},{4,5},{5,4},{6,7},{7,6},{8,9},{9,8},{10,11... | collective-permute-start | bytes 589832 | tf_op jit(solution)/shard_map/ppermute | solution.py:42
  48.1 13.5 %collective-permute-start.14 = (bf16[1,2,128,384]{3,2,1,0:T(8,128)(2,1)}, bf16[1,2,128,384]{3,2,1,0:T(8,128)(2,1)S(1)}, u32[]{:S(2)}, u32[]{:S(2)}) collective-permute-start(bf16[1,2,128,384]{3,2,1,0:T(8,128)(2,1)} %get-tuple-element.79), channel_id=1, source_target_pairs={{16,32},{32,16},{48,64},{64,48},{80,96},{96,80},{17,33},{33,17},{4... | collective-permute-start | bytes 589832 | tf_op jit(solution)/shard_map/ppermute | solution.py:49
  48.8 12.9 %collective-permute-start.15 = (bf16[1,2,128,384]{3,2,1,0:T(8,128)(2,1)S(1)}, bf16[1,2,128,384]{3,2,1,0:T(8,128)(2,1)S(1)}, u32[]{:S(2)}, u32[]{:S(2)}) collective-permute-start(bf16[1,2,128,384]{3,2,1,0:T(8,128)(2,1)S(1)} %get-tuple-element.81), channel_id=1, source_target_pairs={{0,16},{16,0},{32,48},{48,32},{64,80},{80,64},{96,112},{112,96},{1... | collective-permute-start | bytes 589832 | tf_op jit(solution)/shard_map/ppermute | solution.py:49
  51.8 14.8 %all-to-all-start.1 = ((bf16[16,48,128]{2,1,0:T(8,128)(2,1)}), bf16[16,48,128]{2,1,0:T(8,128)(2,1)S(1)}, u32[]{:S(2)}, u32[]{:S(2)}) async-start(bf16[16,48,128]{2,1,0:T(8,128)(2,1)} %add_convert_fusion), calls=%async_computation.1 | async-start | bytes 393216 | tf_op jit(solution)/shard_map/all_to_all | solution.py:486

commit v8 on v7

--- a/solution.py
+++ b/solution.py
@@ -297,14 +297,14 @@
     )(residual_field)
 
 
-def prepare(rounded, deflation, counts, factor, copies, ring, blocks):
+def prepare(rounded, deflation, counts, factor, ring, blocks):
     slots, line = deflation.shape[2:]
     cx, cy, rhs, _ = rounded.shape
     width = factor.shape[1] // (ring * blocks)
 
     def body(count, rounded, vectors, factor, *refs):
-        spread, parts = refs[0], refs[1 : 1 + ring]
-        made, cut, sems = refs[1 + ring :]
+        vector, parts = refs[0], refs[1 : 1 + ring]
+        cut, sems = refs[1 + ring :]
         here = lax.axis_index("x")
         saves = []
         for step in range(ring):
@@ -323,20 +323,16 @@
                 )
                 total = part if total is None else total + part
         total = jnp.where(keep_mask(count, slots, rhs), total, 0.0).astype(BF16)
-        for i in range(copies):
-            made[i] = total
-        saves.append(pltpu.make_async_copy(made, spread, sems.at[ring]))
-        saves[-1].start()
+        vector[...] = total
         for save in saves:
             save.wait()
 
     return pl.pallas_call(
         body,
-        out_shape=[struct((copies, slots, rhs), BF16)] + [struct((blocks, slots, width), BF16)] * ring,
+        out_shape=[struct((slots, rhs), BF16)] + [struct((blocks, slots, width), BF16)] * ring,
         in_specs=[SMEM, VMEM, VMEM, VMEM],
-        out_specs=[HBM] * (1 + ring),
+        out_specs=[VMEM] + [HBM] * ring,
         scratch_shapes=[
-            pltpu.VMEM((copies, slots, rhs), BF16),
             pltpu.VMEM((ring, blocks, slots, width), BF16),
             pltpu.SemaphoreType.DMA((1 + ring,)),
         ],
@@ -344,26 +340,47 @@
     )(counts, rounded, deflation, factor)
 
 
+def spread_pair(mine, other, copies):
+    slots, rhs = mine.shape
+
+    def body(mine, other, out, made, sem):
+        first = lax.axis_index("c") == 0
+        low, high = jnp.where(first, mine[...], other[...]), jnp.where(first, other[...], mine[...])
+        for i in range(copies):
+            made[i, 0], made[i, 1] = low, high
+        copy = pltpu.make_async_copy(made, out, sem)
+        copy.start()
+        copy.wait()
+
+    shape = (copies, 2, slots, rhs)
+    return pl.pallas_call(
+        body,
+        out_shape=struct(shape, BF16),
+        in_specs=[VMEM, VMEM],
+        out_specs=HBM,
+        scratch_shapes=[pltpu.VMEM(shape, BF16), pltpu.SemaphoreType.DMA],
+        compiler_params=limit(4),
+    )(mine, other)
+
+
 def halves(value):
     high = value.astype(BF16)
     return high, (value - high.astype(F32)).astype(BF16)
 
 
-def lower(rows, mine, other):
+def lower(rows, gathered):
     sets = len(rows)
     blocks, slots, _ = rows[0].shape
-    count, _, rhs = mine.shape
+    count, _, _, rhs = gathered.shape
     per = count // blocks
 
     def body(*refs):
-        rows, (mine, other, out) = refs[:sets], refs[sets:]
-        first = lax.axis_index("c") == 0
+        rows, (gathered, out) = refs[:sets], refs[sets:]
         total = None
         for j in range(blocks):
             pieces = []
             for y in range(per):
-                a, b = mine[j * per + y], other[j * per + y]
-                pieces += [jnp.where(first, a, b), jnp.where(first, b, a)]
+                pieces += [gathered[j * per + y, 0], gathered[j * per + y, 1]]
             factor = jnp.concatenate([r[j] for r in rows], 0)
             part = jnp.dot(factor, jnp.concatenate(pieces, 0), preferred_element_type=F32)
             total = part if total is None else total + part
@@ -373,10 +390,10 @@
     return pl.pallas_call(
         body,
         out_shape=struct((sets, slots, rhs), F32),
-        in_specs=[VMEM] * (sets + 2),
+        in_specs=[VMEM] * (sets + 1),
         out_specs=VMEM,
         compiler_params=limit(8),
-    )(*rows, mine, other)
+    )(*rows, gathered)
 
 
 def raise_back(rows, partial, received):
@@ -460,10 +477,11 @@
         rounded, to_near, to_far = round_cells(residual_field)
         near, far = swap_pairs(to_near, GRP, n_grp, 0), swap_pairs(to_far, GRP, n_grp, 1)
         receivers = sizes["zh"] * sizes["zl"] * sizes["y"]
-        spread, *parts = prepare(rounded, deflation, counts, coarse_factor, receivers, ring, sizes["zh"])
+        vector, *parts = prepare(rounded, deflation, counts, coarse_factor, ring, sizes["zh"])
         moved = {n: rotate(parts[n], RING, ring, n) for n in (2, 1, 3)}
         rows = [parts[0]] + [moved[n] for n in range(1, ring)]
-        far, _ = tie((far, parts[0]))
+        spread = spread_pair(vector, swap(vector, "c"), receivers)
+        far, spread, _ = tie((far, spread, parts[0]))
         to_pair, to_outer, own, ends = columns(near, far, rounded)
         outer, pair = swap_outward(to_outer, n_sub), swap(to_pair, "c")
         spread, _ = tie((spread, to_outer))
@@ -473,7 +491,7 @@
         to_pair, to_outer, own, ends = rim_lines((own, ends, pair, outer), line_inverse)
         from_outer, from_pair = swap_outward(to_outer, n_sub), swap(to_pair, "c")
         gathered, _ = tie((gathered, to_outer))
-        partial = lower(rows, gathered, swap(gathered, "c"))
+        partial = lower(rows, gathered)
         moved = {n: rotate(partial, RING, ring, n) for n in (2, 1, 3)}
         received = [moved[n] for n in range(1, ring)]
         own, _ = tie((own, partial))

time: 68.5 us -> 69.1 us (level)
  waiting for transfers between devices: 9.25 us -> 10.4 us
    ppermute x2, waiting for transfers between devices: 0.69 us -> 2.73 us  [swap_outward(): return lax.ppermute(value, SUB, pairs)]
    ppermute x6, starting transfers between devices: 11.8 us -> 10.3 us  [rotate(): lax.ppermute(value, axes, [(i, (i + step) % size) for i in range(size)])]
    ppermute x2, starting transfers between devices: 5.99 us -> 7.23 us  [swap_outward(): return lax.ppermute(value, SUB, pairs)]
    all_to_all x1, starting transfers between devices: 4.7 us -> 3.55 us  [body(): gathered = lax.all_to_all(spread, SPREAD, 0, 0)]
    ppermute x6, waiting for transfers between devices: 2.21 us -> 1.09 us  [rotate(): lax.ppermute(value, axes, [(i, (i + step) % size) for i in range(size)])]
    ppermute x4, starting transfers between devices: 8.04 us -> 8.85 us  [swap_pairs(): return lax.ppermute(value, axes, pairs)]
    pallas_call x1 -> x2, Pallas kernels: 1.67 us -> 1.6 us  [the longest x1 0.82 us: spread_pair(): pl.pallas_call(body, out_shape=struct(shape, BF16), in_specs=[VMEM, VMEM]...]
  transfers between devices with their start and end apart: 18 -> 18, of which waited for: 6 -> 5; matrix products, arithmetic and copies ran while one was open for 1% -> 1% of each run, Pallas kernels for 21% -> 21%
where the time goes in v8:
time: 69.1 us; the launch traced here: 68.2 us
  starting transfers between devices  36.5 us (53%)
  Pallas kernels  16.5 us (24%)
  waiting for transfers between devices  10.4 us (15%)
  local copies, waits for them, and re-layouts  3.31 us (5%)
  between operations  0.86 us (1%)
  other arithmetic  0.73 us (1%)
    pallas_call x3, Pallas kernels, line_solve(): pl.pallas_call(body, out_shape=shapes, in_specs=[ANY if fetch else VMEM]...  12.3 us
    ppermute x6, starting transfers between devices, rotate(): lax.ppermute(value, axes, [(i, (i + step) % size) for i in range(size)])  10.3 us
    ppermute x4, starting transfers between devices, swap_pairs(): return lax.ppermute(value, axes, pairs)  8.85 us
    ppermute x2, starting transfers between devices, swap_outward(): return lax.ppermute(value, SUB, pairs)  7.23 us
    all_to_all x1, starting transfers between devices, body(): terms_in = lax.all_to_all(terms_out, SPREAD, 0, 0)  6.25 us
    all_to_all x1, waiting for transfers between devices, body(): terms_in = lax.all_to_all(terms_out, SPREAD, 0, 0)  4.79 us
    all_to_all x1, starting transfers between devices, body(): gathered = lax.all_to_all(spread, SPREAD, 0, 0)  3.55 us
    unnamed x8, local copies, waits for them, and re-layouts  3.31 us
  transfers between devices with their start and end apart: 18, of which 5 were waited for; matrix products, arithmetic and copies ran while one was open for 1% of the time, Pallas kernels for 21%

profile of v8, /device:TPU:0, one launch (start us, length us, event | category | flops | bytes accessed | tf_op | source)
XLA Modules:
  0.0 68.2 jit_solution(6474217901525870830)
XLA Ops:
  0.0 1.1 %copy-done.1 = f32[2,2,128,384]{3,2,1,0:T(8,128)S(1)} copy-done((f32[2,2,128,384]{3,2,1,0:T(8,128)S(1)}, f32[2,2,128,384]{3,2,1,0:T(8,128)}, u32[]{:S(2)}) %copy-start.1) | copy-done | bytes 786456
  1.2 0.7 collective-permute-start.1
  1.9 4.4 %collective-permute-start = (bf16[1,2,128,384]{3,2,1,0:T(8,128)(2,1)S(1)}, bf16[1,2,128,384]{3,2,1,0:T(8,128)(2,1)S(1)}, u32[]{:S(2)}, u32[]{:S(2)}) collective-permute-start(bf16[1,2,128,384]{3,2,1,0:T(8,128)(2,1)S(1)} %get-tuple-element.45), channel_id=1, source_target_pairs={{0,16},{16,0},{32,48},{48,32},{64,80},{80,64},{96,112},{112,96},{1... | collective-permute-start | bytes 589832 | tf_op jit(solution)/shard_map/ppermute | solution.py:49
  6.9 1.3 %copy-done = f32[48,6144]{1,0:T(8,128)S(1)} copy-done((f32[48,6144]{1,0:T(8,128)S(1)}, f32[48,6144]{1,0:T(8,128)}, u32[]{:S(2)}) %copy-start) | copy-done | bytes 1179672
  8.2 0.9 %copy-done.2 = bf16[2,2,48,384]{3,2,1,0:T(8,128)(2,1)S(1)} copy-done((bf16[2,2,48,384]{3,2,1,0:T(8,128)(2,1)S(1)}, bf16[2,2,48,384]{3,2,1,0:T(8,128)(2,1)}, u32[]{:S(2)}) %copy-start.2) | copy-done | bytes 147480
  9.1 0.8 %shard_map.56 = (bf16[48,128]{1,0:T(8,128)(2,1)S(1)}, bf16[2,48,768]{2,1,0:T(8,128)(2,1)S(1)}, bf16[2,48,768]{2,1,0:T(8,128)(2,1)}, bf16[2,48,768]{2,1,0:T(8,128)(2,1)}, bf16[2,48,768]{2,1,0:T(8,128)(2,1)S(1)}) custom-call(s32[1,1]{1,0:T(1,128)S(6)} %copy.6.count, bf16[2,2,128,384]{3,2,1,0:T(8,128)(2,1)S(1)} %get-tuple-element.47.rounded, ...), custom_call_target="tpu_custom_call" | custom-call | tf_op jit(solution)/shard_map/pallas_call | solution.py:330
  10.0 1.2 %collective-permute-done.2.other = bf16[48,128]{1,0:T(8,128)(2,1)S(1)} collective-permute-done((bf16[48,128]{1,0:T(8,128)(2,1)S(1)}, bf16[48,128]{1,0:T(8,128)(2,1)S(1)}, u32[]{:S(2)}, u32[]{:S(2)}) %collective-permute-start.2) | collective-permute-done | bytes 12320 | tf_op jit(solution)/shard_map/ppermute | solution.py:42
  11.2 0.8 %shard_map.57 = bf16[16,2,48,128]{3,2,1,0:T(8,128)(2,1)} custom-call(bf16[48,128]{1,0:T(8,128)(2,1)S(1)} %get-tuple-element.48.mine, bf16[48,128]{1,0:T(8,128)(2,1)S(1)} %collective-permute-done.2.other), custom_call_target="tpu_custom_call" | custom-call | tf_op jit(solution)/shard_map/pallas_call | solution.py:356
  12.0 0.2 shard_map.58
  12.2 4.2 %collective-permute-start.4 = (bf16[4,1,128,384]{3,2,1,0:T(8,128)(2,1)S(1)}, bf16[4,1,128,384]{3,2,1,0:T(8,128)(2,1)S(1)}, u32[]{:S(2)}, u32[]{:S(2)}) collective-permute-start(bf16[4,1,128,384]{3,2,1,0:T(8,128)(2,1)S(1)} %get-tuple-element.54), channel_id=1, source_target_pairs={{1,2},{2,1},{3,4},{4,3},{5,6},{6,5},{7,8},{8,7},{9,10},{10,9},{11,... | collective-permute-start | bytes 1179656 | tf_op jit(solution)/shard_map/ppermute | solution.py:56
  16.4 4.1 %collective-permute-start.5 = (bf16[2,48,768]{2,1,0:T(8,128)(2,1)}, bf16[2,48,768]{2,1,0:T(8,128)(2,1)S(1)}, u32[]{:S(2)}, u32[]{:S(2)}) collective-permute-start(bf16[2,48,768]{2,1,0:T(8,128)(2,1)} %get-tuple-element.55), channel_id=1, source_target_pairs={{0,32},{16,48},{32,0},{48,16},{1,33},{17,49},{33,1},{49,17},{2,34}... | collective-permute-start | bytes 442376 | tf_op jit(solution)/shard_map/ppermute | solution.py:38
  20.6 3.2 %collective-permute-start.7 = (bf16[2,48,768]{2,1,0:T(8,128)(2,1)S(1)}, bf16[2,48,768]{2,1,0:T(8,128)(2,1)S(1)}, u32[]{:S(2)}, u32[]{:S(2)}) collective-permute-start(bf16[2,48,768]{2,1,0:T(8,128)(2,1)S(1)} %get-tuple-element.57), channel_id=1, source_target_pairs={{0,48},{16,0},{32,16},{48,32},{1,49},{17,1},{33,17},{49,33},{2,50}... | collective-permute-start | bytes 442376 | tf_op jit(solution)/shard_map/ppermute | solution.py:38
  23.8 3.6 %all-to-all-start = ((bf16[16,2,48,128]{3,2,1,0:T(8,128)(2,1)}), bf16[16,2,48,128]{3,2,1,0:T(8,128)(2,1)S(1)}, u32[]{:S(2)}, u32[]{:S(2)}) async-start(bf16[16,2,48,128]{3,2,1,0:T(8,128)(2,1)} %shard_map.57), calls=%async_computation | async-start | bytes 786432 | tf_op jit(solution)/shard_map/all_to_all | solution.py:488
  27.4 1.1 %collective-permute-done.6.refs_1_ = bf16[2,48,768]{2,1,0:T(8,128)(2,1)S(1)} collective-permute-done((bf16[2,48,768]{2,1,0:T(8,128)(2,1)}, bf16[2,48,768]{2,1,0:T(8,128)(2,1)S(1)}, u32[]{:S(2)}, u32[]{:S(2)}) %collective-permute-start.6) | collective-permute-done | bytes 147488 | tf_op jit(solution)/shard_map/ppermute | solution.py:38
  28.5 5.3 %shard_map.59 = (bf16[4,1,128,384]{3,2,1,0:T(8,128)(2,1)}, bf16[4,1,128,384]{3,2,1,0:T(8,128)(2,1)}, bf16[2,2,128,384]{3,2,1,0:T(8,128)(2,1)S(1)}, bf16[2,2,128,384]{3,2,1,0:T(8,128)(2,1)S(1)}) custom-call(bf16[2,2,128,384]{3,2,1,0:T(8,128)(2,1)S(1)} %get-tuple-element.51.refs_0_, bf16[2,2,128,384]{3,2,1,0:T(8,128)(2,1)S(1)} %get-tuple-element.52.refs_1_, ...), custom_call_target="tpu_custom_call" | custom-call | flops 1056964608 | bytes 8257536 | tf_op jit(solution)/shard_map/pallas_call | solution.py:154
  33.9 3.0 %collective-permute-start.12 = (bf16[4,1,128,384]{3,2,1,0:T(8,128)(2,1)}, bf16[4,1,128,384]{3,2,1,0:T(8,128)(2,1)S(1)}, u32[]{:S(2)}, u32[]{:S(2)}) collective-permute-start(bf16[4,1,128,384]{3,2,1,0:T(8,128)(2,1)} %get-tuple-element.66), channel_id=1, source_target_pairs={{1,2},{2,1},{3,4},{4,3},{5,6},{6,5},{7,8},{8,7},{9,10},{10,9},{11,... | collective-permute-start | bytes 1179656 | tf_op jit(solution)/shard_map/ppermute | solution.py:56
  36.9 0.6 all-to-all-done.refs_4_
  37.5 0.3 shard_map.60.refs_4_
  37.8 0.4 collective-permute-start.10
  38.3 1.7 %collective-permute-start.9 = (f32[4,48,128]{2,1,0:T(8,128)S(1)}, f32[4,48,128]{2,1,0:T(8,128)S(1)}, u32[]{:S(2)}, u32[]{:S(2)}) collective-permute-start(f32[4,48,128]{2,1,0:T(8,128)S(1)} %shard_map.60.refs_4_), channel_id=1, source_target_pairs={{0,16},{16,32},{32,48},{48,0},{1,17},{17,33},{33,49},{49,1},{2,18}... | collective-permute-start | bytes 294920 | tf_op jit(solution)/shard_map/ppermute | solution.py:38
  39.9 0.9 %collective-permute-start.8 = (f32[4,48,128]{2,1,0:T(8,128)S(1)}, f32[4,48,128]{2,1,0:T(8,128)S(1)}, u32[]{:S(2)}, u32[]{:S(2)}) collective-permute-start(f32[4,48,128]{2,1,0:T(8,128)S(1)} %shard_map.60.refs_4_), channel_id=1, source_target_pairs={{0,32},{16,48},{32,0},{48,16},{1,33},{17,49},{33,1},{49,17},{2,34}... | collective-permute-start | bytes 294920 | tf_op jit(solution)/shard_map/ppermute | solution.py:38
  40.8 2.7 %collective-permute-done.12.refs_6_.from_outer = bf16[4,1,128,384]{3,2,1,0:T(8,128)(2,1)S(1)} collective-permute-done((bf16[4,1,128,384]{3,2,1,0:T(8,128)(2,1)}, bf16[4,1,128,384]{3,2,1,0:T(8,128)(2,1)S(1)}, u32[]{:S(2)}, u32[]{:S(2)}) %collective-permute-start.12) | collective-permute-done | bytes 393248 | tf_op jit(solution)/shard_map/ppermute | solution.py:56
  43.5 3.6 %shard_map.61 = (bf16[1,2,128,384]{3,2,1,0:T(8,128)(2,1)S(1)}, bf16[1,2,128,384]{3,2,1,0:T(8,128)(2,1)}) custom-call(bf16[2,2,128,384]{3,2,1,0:T(8,128)(2,1)S(1)} %get-tuple-element.80.refs_0_, bf16[2,2,128,384]{3,2,1,0:T(8,128)(2,1)S(1)} %get-tuple-element.69.refs_1_, bf16[4,1,128,384]{3,2,1,0:T(8,128)(2,1)S(1)} %collective-permute-done.3.refs_2_, ...), custom_call_target="tpu_custom_call" | custom-call | flops 603979776 | bytes 4718592 | tf_op jit(solution)/shard_map/pallas_call | solution.py:154
  47.2 0.6 shard_map.62
  47.9 0.7 collective-permute-start.14
  48.6 3.1 %collective-permute-start.15 = (bf16[1,2,128,384]{3,2,1,0:T(8,128)(2,1)S(1)}, bf16[1,2,128,384]{3,2,1,0:T(8,128)(2,1)S(1)}, u32[]{:S(2)}, u32[]{:S(2)}) collective-permute-start(bf16[1,2,128,384]{3,2,1,0:T(8,128)(2,1)S(1)} %get-tuple-element.83), channel_id=1, source_target_pairs={{0,16},{16,0},{32,48},{48,32},{64,80},{80,64},{96,112},{112,96},{1... | collective-permute-start | bytes 589832 | tf_op jit(solution)/shard_map/ppermute | solution.py:49
  51.7 0.7 %add_convert_fusion = bf16[16,48,128]{2,1,0:T(8,128)(2,1)} fusion(f32[16,48,128]{2,1,0:T(8,128)S(1)} %get-tuple-element.76, bf16[16,48,128]{2,1,0:T(8,128)(2,1)S(1)} %collective-permute-done.13), kind=kLoop, calls=%fused_computation | loop fusion | flops 294912 | bytes 786432 | tf_op jit(solution)/shard_map/convert_element_type | solution.py:503
  52.5 6.3 %all-to-all-start.1 = ((bf16[16,48,128]{2,1,0:T(8,128)(2,1)}), bf16[16,48,128]{2,1,0:T(8,128)(2,1)S(1)}, u32[]{:S(2)}, u32[]{:S(2)}) async-start(bf16[16,48,128]{2,1,0:T(8,128)(2,1)} %add_convert_fusion), calls=%async_computation.1 | async-start | bytes 393216 | tf_op jit(solution)/shard_map/all_to_all | solution.py:504
  58.7 3.3 %shard_map.63.inner = f32[2,2,128,384]{3,2,1,0:T(8,128)S(1)} custom-call(bf16[2,2,128,384]{3,2,1,0:T(8,128)(2,1)S(1)} %get-tuple-element.80.refs_0_, bf16[2,2,128,384]{3,2,1,0:T(8,128)(2,1)S(1)} %get-tuple-element.69.refs_1_, bf16[4,1,128,384]{3,2,1,0:T(8,128)(2,1)S(1)} %collective-permute-done.3.refs_2_, ...), custom_call_target="tpu_custom_call" | custom-call | flops 754974720 | bytes 5898240 | tf_op jit(solution)/shard_map/pallas_call | solution.py:154
  62.1 0.2 shard_map.64.first_level
  62.3 4.8 %all-to-all-done.1.terms_in = bf16[16,48,128]{2,1,0:T(8,128)(2,1)S(1)} async-done(((bf16[16,48,128]{2,1,0:T(8,128)(2,1)}), bf16[16,48,128]{2,1,0:T(8,128)(2,1)S(1)}, u32[]{:S(2)}, u32[]{:S(2)}) %all-to-all-start.1) | async-done | bytes 196640 | tf_op jit(solution)/shard_map/all_to_all | solution.py:504
  67.1 1.1 %shard_map.65 = f32[2,2,128,384]{3,2,1,0:T(8,128)} custom-call(s32[1,1]{1,0:T(1,128)S(6)} %copy.6.count, f32[2,2,128,384]{3,2,1,0:T(8,128)S(1)} %shard_map.64.first_level, bf16[16,48,128]{2,1,0:T(8,128)(2,1)S(1)} %all-to-all-done.1.terms_in, bf16[2,2,48,384]{3,2,1,0:T(8,128)(2,1)S(1)} %copy-done.3), custom_call_target="tpu_custom_call" | custom-call | tf_op jit(solution)/shard_map/pallas_call | solution.py:458
  (24 shorter events, 0.4 us)
Async XLA Ops:
  0.0 1.1 %copy-start.1 = (f32[2,2,128,384]{3,2,1,0:T(8,128)S(1)}, f32[2,2,128,384]{3,2,1,0:T(8,128)}, u32[]{:S(2)}) copy-start(f32[2,2,128,384]{3,2,1,0:T(8,128)} %residual.1) | copy-start | bytes 2359300
  1.2 10.8 %collective-permute-start.1 = (bf16[1,2,128,384]{3,2,1,0:T(8,128)(2,1)S(1)}, bf16[1,2,128,384]{3,2,1,0:T(8,128)(2,1)S(1)}, u32[]{:S(2)}, u32[]{:S(2)}) collective-permute-start(bf16[1,2,128,384]{3,2,1,0:T(8,128)(2,1)S(1)} %get-tuple-element.46), channel_id=1, source_target_pairs={{16,32},{32,16},{48,64},{64,48},{80,96},{96,80},{17,33},{33,17},{4... | collective-permute-start | bytes 589832 | tf_op jit(solution)/shard_map/ppermute | solution.py:49
  1.9 10.1 %collective-permute-start = (bf16[1,2,128,384]{3,2,1,0:T(8,128)(2,1)S(1)}, bf16[1,2,128,384]{3,2,1,0:T(8,128)(2,1)S(1)}, u32[]{:S(2)}, u32[]{:S(2)}) collective-permute-start(bf16[1,2,128,384]{3,2,1,0:T(8,128)(2,1)S(1)} %get-tuple-element.45), channel_id=1, source_target_pairs={{0,16},{16,0},{32,48},{48,32},{64,80},{80,64},{96,112},{112,96},{1... | collective-permute-start | bytes 589832 | tf_op jit(solution)/shard_map/ppermute | solution.py:49
  6.9 1.3 %copy-start = (f32[48,6144]{1,0:T(8,128)S(1)}, f32[48,6144]{1,0:T(8,128)}, u32[]{:S(2)}) copy-start(f32[48,6144]{1,0:T(8,128)} %factor.1) | copy-start | bytes 3538948
  8.2 0.9 %copy-start.2 = (bf16[2,2,48,384]{3,2,1,0:T(8,128)(2,1)S(1)}, bf16[2,2,48,384]{3,2,1,0:T(8,128)(2,1)}, u32[]{:S(2)}) copy-start(bf16[2,2,48,384]{3,2,1,0:T(8,128)(2,1)} %vectors.3) | copy-start | bytes 442372
  9.9 1.3 %collective-permute-start.2 = (bf16[48,128]{1,0:T(8,128)(2,1)S(1)}, bf16[48,128]{1,0:T(8,128)(2,1)S(1)}, u32[]{:S(2)}, u32[]{:S(2)}) collective-permute-start(bf16[48,128]{1,0:T(8,128)(2,1)S(1)} %get-tuple-element.48.mine), channel_id=1, source_target_pairs={{0,1},{1,0},{2,3},{3,2},{4,5},{5,4},{6,7},{7,6},{8,9},{9,8},{10,11... | collective-permute-start | bytes 36872 | tf_op jit(solution)/shard_map/ppermute | solution.py:42
  12.2 16.2 %collective-permute-start.4 = (bf16[4,1,128,384]{3,2,1,0:T(8,128)(2,1)S(1)}, bf16[4,1,128,384]{3,2,1,0:T(8,128)(2,1)S(1)}, u32[]{:S(2)}, u32[]{:S(2)}) collective-permute-start(bf16[4,1,128,384]{3,2,1,0:T(8,128)(2,1)S(1)} %get-tuple-element.54), channel_id=1, source_target_pairs={{1,2},{2,1},{3,4},{4,3},{5,6},{6,5},{7,8},{8,7},{9,10},{10,9},{11,... | collective-permute-start | bytes 1179656 | tf_op jit(solution)/shard_map/ppermute | solution.py:56
  16.4 12.0 %collective-permute-start.3 = (bf16[4,1,128,384]{3,2,1,0:T(8,128)(2,1)S(1)}, bf16[4,1,128,384]{3,2,1,0:T(8,128)(2,1)S(1)}, u32[]{:S(2)}, u32[]{:S(2)}) collective-permute-start(bf16[4,1,128,384]{3,2,1,0:T(8,128)(2,1)S(1)} %get-tuple-element.53), channel_id=1, source_target_pairs={{0,1},{1,0},{2,3},{3,2},{4,5},{5,4},{6,7},{7,6},{8,9},{9,8},{10,11... | collective-permute-start | bytes 1179656 | tf_op jit(solution)/shard_map/ppermute | solution.py:42
  16.4 10.9 %collective-permute-start.5 = (bf16[2,48,768]{2,1,0:T(8,128)(2,1)}, bf16[2,48,768]{2,1,0:T(8,128)(2,1)S(1)}, u32[]{:S(2)}, u32[]{:S(2)}) collective-permute-start(bf16[2,48,768]{2,1,0:T(8,128)(2,1)} %get-tuple-element.55), channel_id=1, source_target_pairs={{0,32},{16,48},{32,0},{48,16},{1,33},{17,49},{33,1},{49,17},{2,34}... | collective-permute-start | bytes 442376 | tf_op jit(solution)/shard_map/ppermute | solution.py:38
  20.6 7.9 %collective-permute-start.6 = (bf16[2,48,768]{2,1,0:T(8,128)(2,1)}, bf16[2,48,768]{2,1,0:T(8,128)(2,1)S(1)}, u32[]{:S(2)}, u32[]{:S(2)}) collective-permute-start(bf16[2,48,768]{2,1,0:T(8,128)(2,1)} %get-tuple-element.56), channel_id=1, source_target_pairs={{0,16},{16,32},{32,48},{48,0},{1,17},{17,33},{33,49},{49,1},{2,18}... | collective-permute-start | bytes 442376 | tf_op jit(solution)/shard_map/ppermute | solution.py:38
  20.6 7.9 %collective-permute-start.7 = (bf16[2,48,768]{2,1,0:T(8,128)(2,1)S(1)}, bf16[2,48,768]{2,1,0:T(8,128)(2,1)S(1)}, u32[]{:S(2)}, u32[]{:S(2)}) collective-permute-start(bf16[2,48,768]{2,1,0:T(8,128)(2,1)S(1)} %get-tuple-element.57), channel_id=1, source_target_pairs={{0,48},{16,0},{32,16},{48,32},{1,49},{17,1},{33,17},{49,33},{2,50}... | collective-permute-start | bytes 442376 | tf_op jit(solution)/shard_map/ppermute | solution.py:38
  23.8 13.7 %all-to-all-start = ((bf16[16,2,48,128]{3,2,1,0:T(8,128)(2,1)}), bf16[16,2,48,128]{3,2,1,0:T(8,128)(2,1)S(1)}, u32[]{:S(2)}, u32[]{:S(2)}) async-start(bf16[16,2,48,128]{3,2,1,0:T(8,128)(2,1)} %shard_map.57), calls=%async_computation | async-start | bytes 786432 | tf_op jit(solution)/shard_map/all_to_all | solution.py:488
  33.8 7.0 %collective-permute-start.11 = (bf16[4,1,128,384]{3,2,1,0:T(8,128)(2,1)}, bf16[4,1,128,384]{3,2,1,0:T(8,128)(2,1)S(1)}, u32[]{:S(2)}, u32[]{:S(2)}) collective-permute-start(bf16[4,1,128,384]{3,2,1,0:T(8,128)(2,1)} %get-tuple-element.70), channel_id=1, source_target_pairs={{0,1},{1,0},{2,3},{3,2},{4,5},{5,4},{6,7},{7,6},{8,9},{9,8},{10,11... | collective-permute-start | bytes 1179656 | tf_op jit(solution)/shard_map/ppermute | solution.py:42
  33.9 9.6 %collective-permute-start.12 = (bf16[4,1,128,384]{3,2,1,0:T(8,128)(2,1)}, bf16[4,1,128,384]{3,2,1,0:T(8,128)(2,1)S(1)}, u32[]{:S(2)}, u32[]{:S(2)}) collective-permute-start(bf16[4,1,128,384]{3,2,1,0:T(8,128)(2,1)} %get-tuple-element.66), channel_id=1, source_target_pairs={{1,2},{2,1},{3,4},{4,3},{5,6},{6,5},{7,8},{8,7},{9,10},{10,9},{11,... | collective-permute-start | bytes 1179656 | tf_op jit(solution)/shard_map/ppermute | solution.py:56
  37.8 9.3 %collective-permute-start.10 = (f32[4,48,128]{2,1,0:T(8,128)S(1)}, f32[4,48,128]{2,1,0:T(8,128)S(1)}, u32[]{:S(2)}, u32[]{:S(2)}) collective-permute-start(f32[4,48,128]{2,1,0:T(8,128)S(1)} %shard_map.60.refs_4_), channel_id=1, source_target_pairs={{0,48},{16,0},{32,16},{48,32},{1,49},{17,1},{33,17},{49,33},{2,50}... | collective-permute-start | bytes 294920 | tf_op jit(solution)/shard_map/ppermute | solution.py:38
  38.3 8.9 %collective-permute-start.9 = (f32[4,48,128]{2,1,0:T(8,128)S(1)}, f32[4,48,128]{2,1,0:T(8,128)S(1)}, u32[]{:S(2)}, u32[]{:S(2)}) collective-permute-start(f32[4,48,128]{2,1,0:T(8,128)S(1)} %shard_map.60.refs_4_), channel_id=1, source_target_pairs={{0,16},{16,32},{32,48},{48,0},{1,17},{17,33},{33,49},{49,1},{2,18}... | collective-permute-start | bytes 294920 | tf_op jit(solution)/shard_map/ppermute | solution.py:38
  39.9 7.3 %collective-permute-start.8 = (f32[4,48,128]{2,1,0:T(8,128)S(1)}, f32[4,48,128]{2,1,0:T(8,128)S(1)}, u32[]{:S(2)}, u32[]{:S(2)}) collective-permute-start(f32[4,48,128]{2,1,0:T(8,128)S(1)} %shard_map.60.refs_4_), channel_id=1, source_target_pairs={{0,32},{16,48},{32,0},{48,16},{1,33},{17,49},{33,1},{49,17},{2,34}... | collective-permute-start | bytes 294920 | tf_op jit(solution)/shard_map/ppermute | solution.py:38
  43.5 23.6 %copy-start.3 = (bf16[2,2,48,384]{3,2,1,0:T(8,128)(2,1)S(1)}, bf16[2,2,48,384]{3,2,1,0:T(8,128)(2,1)}, u32[]{:S(2)}) copy-start(bf16[2,2,48,384]{3,2,1,0:T(8,128)(2,1)} %vectors.3) | copy-start | bytes 442372
  47.8 3.9 %collective-permute-start.13 = (bf16[16,48,128]{2,1,0:T(8,128)(2,1)S(1)}, bf16[16,48,128]{2,1,0:T(8,128)(2,1)S(1)}, u32[]{:S(2)}, u32[]{:S(2)}) collective-permute-start(bf16[16,48,128]{2,1,0:T(8,128)(2,1)S(1)} %get-tuple-element.79), channel_id=1, source_target_pairs={{0,1},{1,0},{2,3},{3,2},{4,5},{5,4},{6,7},{7,6},{8,9},{9,8},{10,11... | collective-permute-start | bytes 589832 | tf_op jit(solution)/shard_map/ppermute | solution.py:42
  47.9 14.1 %collective-permute-start.14 = (bf16[1,2,128,384]{3,2,1,0:T(8,128)(2,1)}, bf16[1,2,128,384]{3,2,1,0:T(8,128)(2,1)S(1)}, u32[]{:S(2)}, u32[]{:S(2)}) collective-permute-start(bf16[1,2,128,384]{3,2,1,0:T(8,128)(2,1)} %get-tuple-element.81), channel_id=1, source_target_pairs={{16,32},{32,16},{48,64},{64,48},{80,96},{96,80},{17,33},{33,17},{4... | collective-permute-start | bytes 589832 | tf_op jit(solution)/shard_map/ppermute | solution.py:49
  48.6 13.5 %collective-permute-start.15 = (bf16[1,2,128,384]{3,2,1,0:T(8,128)(2,1)S(1)}, bf16[1,2,128,384]{3,2,1,0:T(8,128)(2,1)S(1)}, u32[]{:S(2)}, u32[]{:S(2)}) collective-permute-start(bf16[1,2,128,384]{3,2,1,0:T(8,128)(2,1)S(1)} %get-tuple-element.83), channel_id=1, source_target_pairs={{0,16},{16,0},{32,48},{48,32},{64,80},{80,64},{96,112},{112,96},{1... | collective-permute-start | bytes 589832 | tf_op jit(solution)/shard_map/ppermute | solution.py:49
  52.5 14.6 %all-to-all-start.1 = ((bf16[16,48,128]{2,1,0:T(8,128)(2,1)}), bf16[16,48,128]{2,1,0:T(8,128)(2,1)S(1)}, u32[]{:S(2)}, u32[]{:S(2)}) async-start(bf16[16,48,128]{2,1,0:T(8,128)(2,1)} %add_convert_fusion), calls=%async_computation.1 | async-start | bytes 393216 | tf_op jit(solution)/shard_map/all_to_all | solution.py:504
